TPU v7x, 128 devices: a whole 4x4x4 slice. The times are simulated.
128 devices in a mesh: leaf: 16 (over x, z), blk: 8 (over y, core).
Axes of the slice: x: 4, y: 4, z: 4, core: 2. Of those that a mesh axis runs over, the one named last changes fastest.
Arguments:
- particular: float32 [64, 73728], P('blk', 'leaf'), may hold values from -6 to 6
- root_inverse: float32 [12288, 12288], P('leaf', 'blk'), may hold values from -0.0390625 to 0.0390625
- mid_inverse: float32 [8192, 4096], P('leaf', 'blk'), may hold values from -0.0625 to 0.0625
- low_inverse: float32 [16384, 4096], P('leaf', 'blk'), may hold values from -0.0625 to 0.0625
- mid_lift: float32 [24576, 4096], P('leaf', 'blk'), may hold values from -0.0625 to 0.0625
- low_lift: float32 [40960, 4096], P('leaf', 'blk'), may hold values from -0.0625 to 0.0625
- mid_solve: float32 [8192, 12288], P('leaf', 'blk'), may hold values from -0.0546875 to 0.0546875
- low_solve: float32 [16384, 10240], P('leaf', 'blk'), may hold values from -0.0625 to 0.0625
Outputs:
- root_values: float32 [64, 12288], P('blk', 'leaf')
- middle_values: float32 [64, 8192], P('blk', 'leaf')
- lower_values: float32 [64, 16384], P('blk', 'leaf')
All inputs are finite; a program needn't handle non-finite values.
Results may differ from a plain program's by a relative error of at most 0.00019.
Values sent between devices are 32-bit elements; how exact they have to be, the bound alone decides.
No kernel may reach another device: no remote copies, remote signals or barrier semaphores. Data moves between devices by JAX's collectives and lax.ppermute only.
A program may use at most 128 MiB of HBM per device.

v0:
```python
import jax
import jax.numpy as jnp
from jax import lax
from jax.sharding import PartitionSpec as P

BD1 = 12288
BD2 = 10240


def from_partner(value, axis, bit):
    mask = 2**bit
    pairs = [(source, source ^ mask) for source in range(lax.axis_size(axis))]
    return lax.ppermute(value, axis, pairs)


def collect(pieces, members):
    position = lax.axis_index("leaf")
    gathered = lax.all_gather(pieces, "leaf", axis=1, tiled=True)
    span_cols = pieces.shape[1] * members
    offset_col = position // members * span_cols
    return lax.dynamic_slice_in_dim(gathered, offset_col, span_cols, 1)


def apply_block(operator, vectors):
    spread = lax.all_to_all(vectors, "blk", split_axis=1, concat_axis=0, tiled=True)
    return lax.psum_scatter(
        lax.dot_general(
            spread,
            operator,
            (((1,), (1,)), ((), ())),
            precision=lax.Precision.HIGHEST,
            preferred_element_type=jnp.float32,
        ),
        "blk",
        scatter_dimension=0,
        tiled=True,
    )


def pair_up(child, bit_index, half_size):
    partner = from_partner(child, "leaf", bit_index)
    is_second = lax.axis_index("leaf") // 2**bit_index % 2 == 1
    first_child = jnp.where(is_second, partner, child)
    second_child = jnp.where(is_second, child, partner)
    jump_vals = second_child[:, half_size:] - first_child[:, half_size:]
    outer_part = jnp.concatenate([first_child[:, :half_size], second_child[:, :half_size]], 1)
    return (jump_vals, outer_part)


def own_slice(whole, members, size_total):
    piece_cols = size_total // members
    return lax.dynamic_slice_in_dim(
        whole, lax.axis_index("leaf") % members * piece_cols, piece_cols, 1
    )


def local(
    particular, root_inverse, mid_inverse, low_inverse, mid_lift, low_lift, mid_solve, low_solve
):
    leaves = lax.axis_size("leaf")
    group_three = leaves // 8
    group_two = leaves // 4
    group_one = leaves // 2
    position = lax.axis_index("leaf")
    side_id = position // group_two % 2
    half_one = BD1 // 2
    child_flux = collect(particular, group_three)
    jump_two, outer_two = pair_up(child_flux, group_three.bit_length() - 1, BD2 // 2)
    low_w = apply_block(low_inverse, jump_two)
    low_full = collect(low_w, group_two)
    flux_two = apply_block(low_lift, low_full) + own_slice(outer_two, group_two, BD2)
    flux_two_full = collect(flux_two, group_two)
    jump_one, outer_one = pair_up(flux_two_full, group_two.bit_length() - 1, BD1 // 2)
    mid_w = apply_block(mid_inverse, jump_one)
    mid_full = collect(mid_w, group_one)
    flux_one = apply_block(mid_lift, mid_full) + own_slice(outer_one, group_one, BD1)
    flux_one_full = collect(flux_one, group_one)
    jump_root, unused_outer = pair_up(flux_one_full, group_one.bit_length() - 1, 0)
    root_values = apply_block(root_inverse, jump_root)
    root_full = collect(root_values, leaves)
    middle_values = apply_block(mid_solve, root_full) + mid_w
    middle_full = collect(middle_values, group_one)
    bound_two = jnp.concatenate(
        [lax.dynamic_slice_in_dim(root_full, side_id * half_one, half_one, 1), middle_full], 1
    )
    lower_values = apply_block(low_solve, bound_two) + low_w
    return (root_values, middle_values, lower_values)


def solution(mesh):
    placed = (
        P("blk", "leaf"),
        P("leaf", "blk"),
        P("leaf", "blk"),
        P("leaf", "blk"),
        P("leaf", "blk"),
        P("leaf", "blk"),
        P("leaf", "blk"),
        P("leaf", "blk"),
    )
    return jax.shard_map(
        local,
        mesh=mesh,
        in_specs=placed,
        out_specs=(P("blk", "leaf"), P("blk", "leaf"), P("blk", "leaf")),
        check_vma=False,
    )
```

profile of v0, /device:TPU:0, one launch (start us, length us, event | category | flops | bytes accessed | tf_op | source)
XLA Modules:
  0.0 583.5 jit_solution(11723100964334532577)
XLA Ops:
  8.0 50.5 %all-gather.3.cloned.1.call-done = f32[8,73728]{1,0:T(8,128)} async-done(((f32[8,4608]{1,0:T(8,128)}), f32[8,73728]{1,0:T(8,128)}) %all-gather.3.cloned.1.call-update) | async-done | bytes 2359312 | tf_op jit(solution)/shard_map/all_gather | solution.py:18
  61.3 7.6 %collective-permute-done = f32[8,9216]{1,0:T(8,128)} collective-permute-done((f32[8,9216]{1,0:T(8,128)S(1)}, f32[8,9216]{1,0:T(8,128)}, u32[]{:S(2)}, u32[]{:S(2)}) %collective-permute-start) | collective-permute-done | bytes 294944 | tf_op jit(solution)/shard_map/ppermute | solution.py:13
  70.8 10.2 %all_to_all.133 = f32[8,8,512]{2,0,1:T(8,128)S(1)} all-to-all(f32[8,8,512]{2,0,1:T(8,128)S(1)} %bitcast.51), channel_id=1, replica_groups=mesh['leaf'=16,'blk'=8] {'blk'}, dimensions={1} | all-to-all | bytes 262144 | tf_op jit(solution)/shard_map/all_to_all | solution.py:25
  85.5 27.9 %reduce-scatter.8.cloned.1.call-done = f32[8,1024]{1,0:T(8,128)} async-done(((f32[64,1024]{1,0:T(8,128)}), f32[8,1024]{1,0:T(8,128)}) %reduce-scatter.8.cloned.1.call-update) | async-done | bytes 32784 | tf_op jit(solution)/shard_map/reduce_scatter | solution.py:26
  113.4 24.1 %all_gather.22 = f32[8,16384]{1,0:T(8,128)S(1)} all-gather(f32[8,1024]{1,0:T(8,128)} %reduce-scatter.8.cloned.1.call-done), channel_id=1, replica_groups=mesh['leaf'=16,'blk'=8] {'leaf'}, dimensions={1}, use_global_device_ids=true | all-gather | bytes 557056 | tf_op jit(solution)/shard_map/all_gather | solution.py:18
  137.6 8.5 %all_to_all.134 = f32[8,8,512]{2,0,1:T(8,128)S(1)} all-to-all(f32[8,8,512]{2,0,1:T(8,128)S(1)} %bitcast.53), channel_id=1, replica_groups=mesh['leaf'=16,'blk'=8] {'blk'}, dimensions={1} | all-to-all | bytes 262144 | tf_op jit(solution)/shard_map/all_to_all | solution.py:25
  146.1 8.4 %fusion.10 = f32[64,2560]{1,0:T(8,128)} fusion(f32[2560,512]{1,0:T(8,128)} %param.13, f32[8,8,512]{2,0,1:T(8,128)S(1)} %all_to_all.134), kind=kOutput, calls=%fused_computation.22 | convolution fusion | flops 1006632960 | bytes 6029312 | tf_op jit(solution)/shard_map/dot_general | solution.py:27
  156.8 26.5 %reduce-scatter.10.cloned.1.call-done = f32[8,2560]{1,0:T(8,128)} async-done(((f32[64,2560]{1,0:T(8,128)}), f32[8,2560]{1,0:T(8,128)}) %reduce-scatter.10.cloned.1.call-update) | async-done | bytes 81936 | tf_op jit(solution)/shard_map/reduce_scatter | solution.py:26
  185.0 42.9 %all-gather.5.cloned.1.call-done = f32[8,40960]{1,0:T(8,128)} async-done(((f32[8,2560]{1,0:T(8,128)}), f32[8,40960]{1,0:T(8,128)}) %all-gather.5.cloned.1.call-update) | async-done | bytes 1310736 | tf_op jit(solution)/shard_map/all_gather | solution.py:18
  239.5 10.2 %all_to_all.135 = f32[8,8,512]{2,0,1:T(8,128)S(1)} all-to-all(f32[8,8,512]{2,0,1:T(8,128)S(1)} %bitcast.52), channel_id=1, replica_groups=mesh['leaf'=16,'blk'=8] {'blk'}, dimensions={1} | all-to-all | bytes 262144 | tf_op jit(solution)/shard_map/all_to_all | solution.py:25
  252.8 27.7 %reduce-scatter.12.cloned.1.call-done = f32[8,512]{1,0:T(8,128)} async-done(((f32[64,512]{1,0:T(8,128)}), f32[8,512]{1,0:T(8,128)}) %reduce-scatter.12.cloned.1.call-update) | async-done | bytes 16400 | tf_op jit(solution)/shard_map/reduce_scatter | solution.py:26
  280.5 23.9 %all_gather.24 = f32[8,8192]{1,0:T(8,128)S(1)} all-gather(f32[8,512]{1,0:T(8,128)} %reduce-scatter.12.cloned.1.call-done), channel_id=1, replica_groups=mesh['leaf'=16,'blk'=8] {'leaf'}, dimensions={1}, use_global_device_ids=true | all-gather | bytes 278528 | tf_op jit(solution)/shard_map/all_gather | solution.py:18
  304.5 8.5 %all_to_all.136 = f32[8,8,512]{2,0,1:T(8,128)S(1)} all-to-all(f32[8,8,512]{2,0,1:T(8,128)S(1)} %bitcast.54), channel_id=1, replica_groups=mesh['leaf'=16,'blk'=8] {'blk'}, dimensions={1} | all-to-all | bytes 262144 | tf_op jit(solution)/shard_map/all_to_all | solution.py:25
  319.3 25.9 %reduce-scatter.14.cloned.1.call-done = f32[8,1536]{1,0:T(8,128)} async-done(((f32[64,1536]{1,0:T(8,128)}), f32[8,1536]{1,0:T(8,128)}) %reduce-scatter.14.cloned.1.call-update) | async-done | bytes 49168 | tf_op jit(solution)/shard_map/reduce_scatter | solution.py:26
  346.1 25.8 %all_gather.25 = f32[8,24576]{1,0:T(8,128)S(1)} all-gather(f32[8,1536]{1,0:T(8,128)S(1)} %fusion.17), channel_id=1, replica_groups=mesh['leaf'=16,'blk'=8] {'leaf'}, dimensions={1}, use_global_device_ids=true | all-gather | bytes 835584 | tf_op jit(solution)/shard_map/all_gather | solution.py:18
  384.1 11.3 %all_to_all.137 = f32[8,8,1536]{2,0,1:T(8,128)S(1)} all-to-all(f32[8,8,1536]{2,0,1:T(8,128)S(1)} %bitcast.49), channel_id=1, replica_groups=mesh['leaf'=16,'blk'=8] {'blk'}, dimensions={1} | all-to-all | bytes 786432 | tf_op jit(solution)/shard_map/all_to_all | solution.py:25
  403.0 29.1 %reduce-scatter.16.cloned.1.call-done = f32[8,768]{1,0:T(8,128)} async-done(((f32[64,768]{1,0:T(8,128)}), f32[8,768]{1,0:T(8,128)}) %reduce-scatter.16.cloned.1.call-update) | async-done | bytes 24592 | tf_op jit(solution)/shard_map/reduce_scatter | solution.py:26
  432.1 26.5 %all_gather.26 = f32[8,12288]{1,0:T(8,128)} all-gather(f32[8,768]{1,0:T(8,128)} %reduce-scatter.16.cloned.1.call-done), channel_id=1, replica_groups=mesh['leaf'=16,'blk'=8] {'leaf'}, dimensions={1}, use_global_device_ids=true | all-gather | bytes 417792 | tf_op jit(solution)/shard_map/all_gather | solution.py:18
  462.1 8.8 %all-to-all-done.5 = f32[8,8,1536]{2,0,1:T(8,128)S(1)} async-done(((f32[8,8,1536]{2,0,1:T(8,128)}), f32[8,8,1536]{2,0,1:T(8,128)S(1)}, u32[]{:S(2)}, u32[]{:S(2)}) %all-to-all-start.5) | async-done | bytes 393248 | tf_op jit(solution)/shard_map/all_to_all | solution.py:25
  477.6 26.4 %reduce-scatter.18.cloned.1.call-done = f32[8,512]{1,0:T(8,128)} async-done(((f32[64,512]{1,0:T(8,128)}), f32[8,512]{1,0:T(8,128)}) %reduce-scatter.18.cloned.1.call-update) | async-done | bytes 16400 | tf_op jit(solution)/shard_map/reduce_scatter | solution.py:26
  504.7 23.9 %all_gather.27 = f32[8,8192]{1,0:T(8,128)S(1)} all-gather(f32[8,512]{1,0:T(8,128)S(1)} %add.87), channel_id=1, replica_groups=mesh['leaf'=16,'blk'=8] {'leaf'}, dimensions={1}, use_global_device_ids=true | all-gather | bytes 278528 | tf_op jit(solution)/shard_map/all_gather | solution.py:18
  528.7 10.6 %all_to_all.138 = f32[8,8,1280]{2,0,1:T(8,128)S(1)} all-to-all(f32[8,8,1280]{2,0,1:T(8,128)S(1)} %bitcast.50), channel_id=1, replica_groups=mesh['leaf'=16,'blk'=8] {'blk'}, dimensions={1} | all-to-all | bytes 655360 | tf_op jit(solution)/shard_map/all_to_all | solution.py:25
  539.3 8.2 %fusion.4 = f32[64,1024]{1,0:T(8,128)} fusion(f32[1024,1280]{1,0:T(8,128)} %param.15, f32[8,8,1280]{2,0,1:T(8,128)S(1)} %all_to_all.138), kind=kOutput, calls=%fused_computation.10 | convolution fusion | flops 1006632960 | bytes 5832704 | tf_op jit(solution)/shard_map/dot_general | solution.py:27
  547.5 28.1 %reduce-scatter.20.cloned.1.call-done = f32[8,1024]{1,0:T(8,128)} async-done(((f32[64,1024]{1,0:T(8,128)}), f32[8,1024]{1,0:T(8,128)}) %reduce-scatter.20.cloned.1.call-update) | async-done | bytes 32784 | tf_op jit(solution)/shard_map/reduce_scatter | solution.py:26
  (64 shorter events, 67.7 us)
Async XLA Ops:
  7.2 305.8 %copy-start = (f32[1536,512]{1,0:T(8,128)S(1)}, f32[1536,512]{1,0:T(8,128)}, u32[]{:S(2)}) copy-start(f32[1536,512]{1,0:T(8,128)} %param.12) | copy-start | bytes 9437188
  7.2 51.3 %all-gather.3.cloned.1.call-start = ((), (), s32[]{:S(2)}) async-start(), calls=%async_computation.14 | async-start | bytes 2506752 | tf_op jit(solution)/shard_map/all_gather | solution.py:18
  7.9 105.5 %reduce-scatter.8.cloned.1.call-start = ((), (), s32[]{:S(2)}) async-start(), calls=%async_computation.15 | async-start | bytes 294912 | tf_op jit(solution)/shard_map/reduce_scatter | solution.py:26
  59.5 9.5 %collective-permute-start = (f32[8,9216]{1,0:T(8,128)S(1)}, f32[8,9216]{1,0:T(8,128)}, u32[]{:S(2)}, u32[]{:S(2)}) collective-permute-start(f32[8,9216]{1,0:T(8,128)S(1)} %constant_dynamic-slice_fusion.6), channel_id=1, source_target_pairs={{0,16},{8,24},{16,0},{24,8},{32,48},{40,56},{48,32},{56,40},{64,80... | collective-permute-start | bytes 884744 | tf_op jit(solution)/shard_map/ppermute | solution.py:13
  70.0 0.7 copy-start.3
  85.4 97.8 %reduce-scatter.10.cloned.1.call-start = ((), (), s32[]{:S(2)}) async-start(), calls=%async_computation.16 | async-start | bytes 737280 | tf_op jit(solution)/shard_map/reduce_scatter | solution.py:26
  154.5 73.4 %all-gather.5.cloned.1.call-start = ((), (), s32[]{:S(2)}) async-start(), calls=%async_computation.17 | async-start | bytes 1392640 | tf_op jit(solution)/shard_map/all_gather | solution.py:18
  184.9 95.6 %reduce-scatter.12.cloned.1.call-start = ((), (), s32[]{:S(2)}) async-start(), calls=%async_computation.18 | async-start | bytes 147456 | tf_op jit(solution)/shard_map/reduce_scatter | solution.py:26
  228.8 8.8 %collective-permute-start.1 = (f32[8,10240]{1,0:T(8,128)S(1)}, f32[8,10240]{1,0:T(8,128)}, u32[]{:S(2)}, u32[]{:S(2)}) collective-permute-start(f32[8,10240]{1,0:T(8,128)S(1)} %constant_dynamic-slice_fusion.4), channel_id=1, source_target_pairs={{0,32},{8,40},{16,48},{24,56},{32,0},{40,8},{48,16},{56,24},{64,96... | collective-permute-start | bytes 983048 | tf_op jit(solution)/shard_map/ppermute | solution.py:13
  238.7 0.7 copy-start.2
  252.7 92.5 %reduce-scatter.14.cloned.1.call-start = ((), (), s32[]{:S(2)}) async-start(), calls=%async_computation.19 | async-start | bytes 442368 | tf_op jit(solution)/shard_map/reduce_scatter | solution.py:26
  316.9 115.2 %reduce-scatter.16.cloned.1.call-start = ((), (), s32[]{:S(2)}) async-start(), calls=%async_computation.20 | async-start | bytes 221184 | tf_op jit(solution)/shard_map/reduce_scatter | solution.py:26
  371.9 0.9 copy-start.1
  373.6 9.5 %collective-permute-start.2 = (f32[8,12288]{1,0:T(8,128)}, f32[8,12288]{1,0:T(8,128)S(1)}, u32[]{:S(2)}, u32[]{:S(2)}) collective-permute-start(f32[8,12288]{1,0:T(8,128)} %constant_dynamic-slice_fusion.2), channel_id=1, source_target_pairs={{0,64},{8,72},{16,80},{24,88},{32,96},{40,104},{48,112},{56,120},{... | collective-permute-start | bytes 1179656 | tf_op jit(solution)/shard_map/ppermute | solution.py:13
  403.0 101.0 %copy-start.5 = (f32[8,512]{1,0:T(8,128)S(1)}, f32[8,512]{1,0:T(8,128)}, u32[]{:S(2)}) copy-start(f32[8,512]{1,0:T(8,128)} %reduce-scatter.12.cloned.1.call-done) | copy-start | bytes 49156
  458.6 12.3 %all-to-all-start.5 = ((f32[8,8,1536]{2,0,1:T(8,128)}), f32[8,8,1536]{2,0,1:T(8,128)S(1)}, u32[]{:S(2)}, u32[]{:S(2)}) async-start(f32[8,8,1536]{2,0,1:T(8,128)} %bitcast.15), calls=%async_computation.10 | async-start | bytes 786432 | tf_op jit(solution)/shard_map/all_to_all | solution.py:25
  462.0 41.9 %reduce-scatter.18.cloned.1.call-start = ((), (), s32[]{:S(2)}) async-start(), calls=%async_computation.21 | async-start | bytes 147456 | tf_op jit(solution)/shard_map/reduce_scatter | solution.py:26
  476.6 99.0 %reduce-scatter.20.cloned.1.call-start = ((), (), s32[]{:S(2)}) async-start(), calls=%async_computation.22 | async-start | bytes 294912 | tf_op jit(solution)/shard_map/reduce_scatter | solution.py:26
  504.7 42.8 %copy-start.6 = (f32[8,512]{1,0:T(8,128)}, f32[8,512]{1,0:T(8,128)S(1)}, u32[]{:S(2)}) copy-start(f32[8,512]{1,0:T(8,128)S(1)} %add.87) | copy-start | bytes 49156
  539.3 36.3 %copy-start.4 = (f32[8,1024]{1,0:T(8,128)S(1)}, f32[8,1024]{1,0:T(8,128)}, u32[]{:S(2)}) copy-start(f32[8,1024]{1,0:T(8,128)} %reduce-scatter.8.cloned.1.call-done) | copy-start | bytes 98308
Sparse Core Ops, SparseCore 0:
  10.2 48.2 all-gather.2
  85.6 27.8 reduce-scatter.7
  154.6 28.6 reduce-scatter.9
  185.6 42.2 all-gather.4
  252.8 27.6 reduce-scatter.11
  317.0 28.1 reduce-scatter.13
  403.1 28.9 reduce-scatter.15
  476.7 27.2 reduce-scatter.17
  547.7 27.9 reduce-scatter.19
where the time goes:
time: 585 us; the launch traced here: 584 us
  waiting for transfers between devices  317 us (54%)
  blocking collectives  184 us (31%)
  matrix products  41 us (7%)
  between operations  14.1 us (2%)
  local copies, waits for them, and re-layouts  10.7 us (2%)
  starting transfers between devices  8.93 us (2%)
  other arithmetic  7.83 us (1%)
    reduce_scatter x7, waiting for transfers between devices, apply_block(): lax.psum_scatter(lax.dot_general(spread, operator, (((1,), (1,)), ((), ()...  192 us
    all_gather x5, blocking collectives, collect(): gathered = lax.all_gather(pieces, 'leaf', axis=1, tiled=True)  124 us
    all_gather x2, waiting for transfers between devices, collect(): gathered = lax.all_gather(pieces, 'leaf', axis=1, tiled=True)  93.4 us
    all_to_all x6, blocking collectives, apply_block(): lax.all_to_all(vectors, 'blk', split_axis=1, concat_axis=0, tiled=True)  59.4 us
    dot_general x7, matrix products, apply_block(): lax.dot_general(spread, operator, (((1,), (1,)), ((), ())), precision=lax...  41 us
    ppermute x3, waiting for transfers between devices, from_partner(): return lax.ppermute(value, axis, pairs)  22.6 us
  transfers between devices with their start and end apart: 13, of which 13 were waited for; matrix products, arithmetic and copies ran while one was open for 1% of the time, Pallas kernels for 0%

commit v1 on v0

v1 whole, which is shorter than its diff:
```python
import jax
import jax.numpy as jnp
from jax import lax
from jax.sharding import PartitionSpec as P

AXES = ("leaf", "blk")
DEVICES = [(s // 32, s // 8 % 4, s // 2 % 4, s % 2) for s in range(128)]


def flat(x, z, y, c):
    return ((x * 4 + z) * 4 + y) * 2 + c


def send(value, hop):
    pairs = []
    for source, place in enumerate(DEVICES):
        target = hop(*place)
        if target is not None:
            pairs.append((source, flat(*target)))
    return lax.ppermute(value, AXES, pairs)


def exchange(value, key, order):
    groups = {}
    for source, place in enumerate(DEVICES):
        groups.setdefault(key(*place), []).append((order(*place), source))
    members = [[source for _, source in sorted(group)] for group in groups.values()]
    return lax.all_to_all(value, AXES, 0, 0, axis_index_groups=members)


def over_blk(value):
    return exchange(value, lambda x, z, y, c: (x, z), lambda x, z, y, c: 2 * y + c)


def over_leaf(value):
    return exchange(value, lambda x, z, y, c: (y, c), lambda x, z, y, c: 4 * x + z)


def over_half(value):
    return exchange(value, lambda x, z, y, c: (x // 2, y, c), lambda x, z, y, c: 4 * x + z)


def copies(value, number):
    return jnp.broadcast_to(value[None], (number, *value.shape))


def swap_core(value):
    return send(value, lambda x, z, y, c: (x, z, y, 1 - c))


def sum_y(value):
    return value + total([send(value, lambda x, z, y, c: (x, z, y ^ k, c)) for k in (1, 2, 3)])


def cols(value, start, size):
    return lax.dynamic_slice_in_dim(value, start, size, value.ndim - 1)


def rows(value, start, size):
    return lax.dynamic_slice_in_dim(value, start, size, 0)


def apply(vectors, operator):
    return lax.dot_general(
        vectors,
        operator,
        (((1,), (1,)), ((), ())),
        precision=lax.Precision.HIGH,
        preferred_element_type=jnp.float32,
    )


def pick(pieces, index):
    out = pieces[0]
    for number in range(1, len(pieces)):
        out = jnp.where(index == number, pieces[number], out)
    return out


def total(parts):
    out = parts[0]
    for part in parts[1:]:
        out = out + part
    return out


def widen(value):
    return value.transpose(0, 2, 1, 3).reshape(64, -1)


def local(
    particular, root_inverse, mid_inverse, low_inverse, mid_lift, low_lift, mid_solve, low_solve
):
    leaf, blk = lax.axis_index("leaf"), lax.axis_index("blk")
    x, z, y, c = leaf // 4, leaf % 4, blk // 2, blk % 2
    xh, xl = x // 2, x % 2

    inner = jnp.where(z == 3, 1.0, -1.0) * particular[:, 512:]
    inner = inner.reshape(8, 8, 512).transpose(1, 0, 2)
    spread = exchange(
        jnp.broadcast_to(inner[None], (4, 8, 8, 512)).reshape(32, 8, 512),
        lambda x, z, y, c: x,
        lambda x, z, y, c: (z, y, c),
    )
    jump_two = (spread[8:16] + spread[24:]).reshape(64, 512)

    low_part = apply(jump_two, low_inverse)
    half = cols(low_part, 512 * c, 512) + swap_core(cols(low_part, 512 * (1 - c), 512))
    low_w = send(sum_y(half), lambda x, z, y, c: (x, y, z, c))

    moved = send(
        particular[:, 2560:], lambda x, z, y, c: (x, z + 1, y, c) if z % 2 == 0 else None
    )
    outer = jnp.where(
        z % 2 == 0, particular[:, :2560], jnp.concatenate([moved, particular[:, :512]], 1)
    )
    mine = (jnp.arange(8) == blk)[:, None, None]
    flux_two = apply(low_w, low_lift) + jnp.where(mine, outer[None], 0.0).reshape(64, 2560)
    flux_two = flux_two + swap_core(flux_two)

    def holder(y, c):
        return 2 if 2 * y + c < 3 else 3

    def block(y):
        number = 2 * y + c
        return cols(flux_two, jnp.clip(6144 + 512 * number - 2560 * z, 0, 2048), 512)

    holds = z == jnp.where(blk < 3, 2, 3)
    parts = [jnp.where(holds, block(y), 0.0)]
    for k in (1, 2, 3):
        parts.append(
            send(
                block(y ^ k),
                lambda x, z, y, c: (x, z, y ^ k, c) if z == holder(y ^ k, c) else None,
            )
        )
    summed = jnp.where(xl == 1, 1.0, -1.0) * total(parts)
    summed = summed + send(
        summed, lambda x, z, y, c: (x ^ 1, z, y, c) if z == holder(y, c) else None
    )
    jump_one = total(
        [summed]
        + [
            send(summed, lambda x, z, y, c: (x, z ^ k, y, c) if z == holder(y, c) else None)
            for k in (1, 2, 3)
        ]
    )

    mid_part = apply(jump_one, mid_inverse)
    mid_sum = sum_y(mid_part + swap_core(mid_part))
    mid_w = send(
        mid_sum, lambda x, z, y, c: (x // 2 * 2 + c, y, x % 2 * 2 + z // 2, z % 2)
    )

    outer_half = lax.dynamic_index_in_dim(flux_two.reshape(4, 2, 8, 2560), c, 1, False)
    outer_half = outer_half.reshape(32, 2560)
    next_z = send(
        cols(outer_half, jnp.where(z == 0, 1024, jnp.where(z == 1, 512, 0)), 1536),
        lambda x, z, y, c: (x, z + 1, y, c) if z < 3 else None,
    )
    far_z = send(
        outer_half[:, 2048:], lambda x, z, y, c: (x, 3, y, c) if z == 1 else None
    )
    outer_one = pick(
        [
            outer_half[:, :1536],
            jnp.concatenate([next_z[:, 512:], outer_half[:, :512]], 1),
            next_z,
            jnp.concatenate([far_z, next_z[:, :1024]], 1),
        ],
        z,
    )

    lift_part = apply(mid_w, mid_lift).reshape(4, 2, 8, 1536)
    flux_one = lax.dynamic_index_in_dim(lift_part, c, 1, False) + swap_core(
        lax.dynamic_index_in_dim(lift_part, 1 - c, 1, False)
    )
    flux_one = jnp.where(xh == 1, 1.0, -1.0) * (flux_one + outer_one.reshape(4, 8, 1536))
    shares = flux_one.reshape(4, 8, 2, 768).transpose(2, 0, 1, 3).reshape(8, 8, 768)
    piece = total(
        list(exchange(shares, lambda x, z, y, c: (x % 2, z, c), lambda x, z, y, c: (x, y)))
    )
    every = over_leaf(copies(piece, 16))
    root_jump = widen(over_blk(every.reshape(2, 8, 8, 768).transpose(1, 0, 2, 3)))

    root_part = apply(root_jump, root_inverse)
    root_values = total(list(over_blk(root_part.reshape(8, 8, 768))))
    root_every = over_leaf(copies(root_values, 16))
    root_block = widen(over_blk(root_every.reshape(8, 2, 8, 768)))

    middle_part = apply(root_block, mid_solve) + mid_part
    middle_values = total(list(over_blk(middle_part.reshape(8, 8, 512))))
    middle_every = over_half(copies(middle_values, 8))

    root_half = lax.dynamic_slice_in_dim(root_every.reshape(2, 8, 8, 768), xl, 1, 0)[0]
    bound = jnp.concatenate(
        [
            root_half.transpose(1, 0, 2).reshape(8, 6144),
            middle_every.transpose(1, 0, 2).reshape(8, 4096),
        ],
        1,
    )
    bound = over_blk(bound.reshape(8, 8, 1280).transpose(1, 0, 2)).reshape(64, 1280)
    lower_part = low_part + apply(bound, low_solve)
    lower_values = total(list(over_blk(lower_part.reshape(8, 8, 1024))))
    return (root_values, middle_values, lower_values)


def solution(mesh):
    placed = (P("blk", "leaf"),) + (P("leaf", "blk"),) * 7
    return jax.shard_map(
        local,
        mesh=mesh,
        in_specs=placed,
        out_specs=(P("blk", "leaf"),) * 3,
        check_vma=False,
    )
```

time: 585 us -> 254 us (0.43)
  waiting for transfers between devices: 317 us -> 64.8 us
  blocking collectives: 184 us -> 98.9 us
  starting transfers between devices: 8.93 us -> 45 us
  matrix products: 41 us -> 24.1 us
  between operations: 14.1 us -> 1.05 us
    reduce_scatter x7 -> x0, waiting for transfers between devices: 192 us -> none  [apply_block(): lax.psum_scatter(lax.dot_general(spread, operator, (((1,), (1,)), ((), ()...]
    all_gather x5 -> x0, blocking collectives: 124 us -> none  [collect(): gathered = lax.all_gather(pieces, 'leaf', axis=1, tiled=True)]
    all_gather x2 -> x0, waiting for transfers between devices: 93.4 us -> none  [collect(): gathered = lax.all_gather(pieces, 'leaf', axis=1, tiled=True)]
    all_to_all x6 -> x8, blocking collectives: 59.4 us -> 98.9 us  [exchange(): return lax.all_to_all(value, AXES, 0, 0, axis_index_groups=members)]
    ppermute x3 -> x22, starting transfers between devices: 5.11 us -> 28.5 us  [send(): return lax.ppermute(value, AXES, pairs)]
    ppermute x3 -> x22, waiting for transfers between devices: 22.6 us -> 41 us  [send(): return lax.ppermute(value, AXES, pairs)]
    dot_general x7, matrix products: 41 us -> 24.1 us  [apply(): lax.dot_general(vectors, operator, (((1,), (1,)), ((), ())), precision=la...]
    all_to_all x1 -> x3, waiting for transfers between devices: 8.8 us -> 23.7 us  [exchange(): return lax.all_to_all(value, AXES, 0, 0, axis_index_groups=members)]
  transfers between devices with their start and end apart: 13 -> 25, of which waited for: 13 -> 11; matrix products, arithmetic and copies ran while one was open for 1% -> 3% of each run, Pallas kernels for 0% -> 0%
where the time goes in v1:
time: 254 us; the launch traced here: 253 us
  blocking collectives  98.9 us (39%)
  waiting for transfers between devices  64.8 us (26%)
  starting transfers between devices  45 us (18%)
  matrix products  24.1 us (9%)
  other arithmetic  9.79 us (4%)
  local copies, waits for them, and re-layouts  9.12 us (4%)
    all_to_all x8, blocking collectives, exchange(): return lax.all_to_all(value, AXES, 0, 0, axis_index_groups=members)  98.9 us
    ppermute x22, waiting for transfers between devices, send(): return lax.ppermute(value, AXES, pairs)  41 us
    ppermute x22, starting transfers between devices, send(): return lax.ppermute(value, AXES, pairs)  28.5 us
    dot_general x7, matrix products, apply(): lax.dot_general(vectors, operator, (((1,), (1,)), ((), ())), precision=la...  24.1 us
    all_to_all x3, waiting for transfers between devices, exchange(): return lax.all_to_all(value, AXES, 0, 0, axis_index_groups=members)  23.7 us
    all_to_all x3, starting transfers between devices, exchange(): return lax.all_to_all(value, AXES, 0, 0, axis_index_groups=members)  16.5 us
  transfers between devices with their start and end apart: 25, of which 11 were waited for; matrix products, arithmetic and copies ran while one was open for 3% of the time, Pallas kernels for 0%

profile of v1, /device:TPU:0, one launch (start us, length us, event | category | flops | bytes accessed | tf_op | source)
XLA Modules:
  0.0 252.7 jit_solution(425905633569217574)
XLA Ops:
  2.7 8.5 %all-to-all-start = ((f32[32,8,512]{2,1,0:T(8,128)}), f32[32,8,512]{2,1,0:T(8,128)}, u32[]{:S(2)}, u32[]{:S(2)}) async-start(f32[32,8,512]{2,1,0:T(8,128)} %bitcast.82), calls=%async_computation | async-start | bytes 1048576 | tf_op jit(solution)/shard_map/all_to_all | solution.py:28
  11.2 11.7 %all-to-all-done = f32[32,8,512]{2,1,0:T(8,128)} async-done(((f32[32,8,512]{2,1,0:T(8,128)}), f32[32,8,512]{2,1,0:T(8,128)}, u32[]{:S(2)}, u32[]{:S(2)}) %all-to-all-start) | async-done | bytes 524320 | tf_op jit(solution)/shard_map/all_to_all | solution.py:28
  23.0 2.8 %fusion.11 = f32[64,1024]{1,0:T(8,128)S(1)} fusion(f32[1024,512]{1,0:T(8,128)} %param.11, f32[32,8,512]{2,1,0:T(8,128)} %all-to-all-done), kind=kOutput, calls=%fused_computation.21 | convolution fusion | flops 201359360 | bytes 2621440 | tf_op jit(solution)/shard_map/dot_general | solution.py:64
  35.1 2.7 %collective-permute-start.5 = (f32[8,2048]{1,0:T(8,128)}, f32[8,2048]{1,0:T(8,128)}, u32[]{:S(2)}, u32[]{:S(2)}) collective-permute-start(f32[8,2048]{1,0:T(8,128)} %slice.37), channel_id=1, source_target_pairs={{0,8},{1,9},{2,10},{3,11},{4,12},{5,13},{6,14},{7,15},{16,24},{17,... | collective-permute-start | bytes 196616 | tf_op jit(solution)/shard_map/ppermute | solution.py:20
  44.5 5.9 %convolution_add_fusion = f32[64,2560]{1,0:T(8,128)} fusion(f32[64,512]{1,0:T(8,128)S(1)} %collective-permute-done.4, f32[2560,512]{1,0:T(8,128)} %param.13, f32[8,2560]{1,0:T(8,128)S(1)} %maximum_select_fusion, pred[64]{0:T(512)(128)(4,1)} %broadcast_in_dim.64), kind=kOutput, calls=%fused_computation.2 | convolution fusion | flops 503644160 | bytes 6111296 | tf_op jit(solution)/shard_map/dot_general | solution.py:64
  50.4 2.4 collective-permute-done.6
  63.7 30.5 %collective-permute-done.12 = f32[64,512]{1,0:T(8,128)S(1)} collective-permute-done((f32[64,512]{1,0:T(8,128)S(1)}, f32[64,512]{1,0:T(8,128)S(1)}, u32[]{:S(2)}, u32[]{:S(2)}) %collective-permute-start.12) | collective-permute-done | bytes 131104 | tf_op jit(solution)/shard_map/ppermute | solution.py:20
  97.7 2.5 collective-permute-start.16
  102.3 3.1 %collective-permute-start.21 = (f32[32,1536]{1,0:T(8,128)S(1)}, f32[32,1536]{1,0:T(8,128)S(1)}, u32[]{:S(2)}, u32[]{:S(2)}) collective-permute-start(f32[32,1536]{1,0:T(8,128)S(1)} %constant_dynamic-slice_fusion.1), channel_id=1, source_target_pairs={{0,8},{1,9},{2,10},{3,11},{4,12},{5,13},{6,14},{7,15},{8,16},{9,17... | collective-permute-start | bytes 589832 | tf_op jit(solution)/shard_map/ppermute | solution.py:20
  112.0 4.5 %collective-permute-start.19 = (f32[4,8,1536]{2,1,0:T(8,128)S(1)}, f32[4,8,1536]{2,1,0:T(8,128)S(1)}, u32[]{:S(2)}, u32[]{:S(2)}) collective-permute-start(f32[4,8,1536]{2,1,0:T(8,128)S(1)} %dynamic-slice_bitcast_fusion.1), channel_id=1, source_target_pairs={{0,1},{1,0},{2,3},{3,2},{4,5},{5,4},{6,7},{7,6},{8,9},{9,8},{10,11... | collective-permute-start | bytes 589832 | tf_op jit(solution)/shard_map/ppermute | solution.py:20
  117.8 21.4 %all_to_all.55 = f32[8,8,768]{2,1,0:T(8,128)S(1)} all-to-all(f32[8,8,768]{2,1,0:T(8,128)S(1)} %bitcast.90), channel_id=1, replica_groups={{0,2,4,6,64,66,68,70},{1,3,5,7,65,67,69,71},{8,10,12,14,72,74,76,78},{9..., dimensions={0} | all-to-all | bytes 393216 | tf_op jit(solution)/shard_map/all_to_all | solution.py:28
  139.2 11.7 %all_to_all.56 = f32[16,8,768]{2,1,0:T(8,128)S(1)} all-to-all(f32[16,8,768]{2,1,0:T(8,128)S(1)} %broadcast_in_dim.71), channel_id=1, replica_groups={{0,8,16,24,32,40,48,56,64,72,80,88,96,104,112,120},{1,9,17,25,33,41,49,..., dimensions={0} | all-to-all | bytes 786432 | tf_op jit(solution)/shard_map/all_to_all | solution.py:28
  151.0 11.6 %all_to_all.57 = f32[8,2,8,768]{3,2,1,0:T(8,128)S(1)} all-to-all(f32[8,2,8,768]{3,2,1,0:T(8,128)S(1)} %copy.15), channel_id=1, replica_groups={{0,1,2,3,4,5,6,7},{8,9,10,11,12,13,14,15},{16,17,18,19,20,21,22,23},{24..., dimensions={0} | all-to-all | bytes 786432 | tf_op jit(solution)/shard_map/all_to_all | solution.py:28
  162.6 4.6 %fusion = f32[8,8,768]{2,1,0:T(8,128)S(1)} fusion(f32[8,8,1536]{2,1,0:T(8,128)S(1)} %bitcast.87, f32[768,1536]{1,0:T(8,128)} %param.9), kind=kOutput, calls=%fused_computation | convolution fusion | flops 452984832 | bytes 5308416 | tf_op jit(solution)/shard_map/dot_general | solution.py:64
  167.2 9.2 %all_to_all.58 = f32[8,8,768]{2,1,0:T(8,128)S(1)} all-to-all(f32[8,8,768]{2,1,0:T(8,128)S(1)} %fusion), channel_id=1, replica_groups={{0,1,2,3,4,5,6,7},{8,9,10,11,12,13,14,15},{16,17,18,19,20,21,22,23},{24..., dimensions={0} | all-to-all | bytes 393216 | tf_op jit(solution)/shard_map/all_to_all | solution.py:28
  176.5 13.1 %all_to_all.59 = f32[16,8,768]{2,1,0:T(8,128)S(1)} all-to-all(f32[16,8,768]{2,1,0:T(8,128)S(1)} %broadcast_in_dim.73), channel_id=1, replica_groups={{0,8,16,24,32,40,48,56,64,72,80,88,96,104,112,120},{1,9,17,25,33,41,49,..., dimensions={0} | all-to-all | bytes 786432 | tf_op jit(solution)/shard_map/all_to_all | solution.py:28
  189.6 11.3 %all_to_all.60 = f32[8,2,8,768]{3,2,1,0:T(8,128)S(1)} all-to-all(f32[8,2,8,768]{3,2,1,0:T(8,128)S(1)} %bitcast.80), channel_id=1, replica_groups={{0,1,2,3,4,5,6,7},{8,9,10,11,12,13,14,15},{16,17,18,19,20,21,22,23},{24..., dimensions={0} | all-to-all | bytes 786432 | tf_op jit(solution)/shard_map/all_to_all | solution.py:28
  203.2 4.0 %all-to-all-start.7 = ((f32[8,8,512]{2,1,0:T(8,128)}), f32[8,8,512]{2,1,0:T(8,128)}, u32[]{:S(2)}, u32[]{:S(2)}) async-start(f32[8,8,512]{2,1,0:T(8,128)} %fusion.3), calls=%async_computation.7 | async-start | bytes 262144 | tf_op jit(solution)/shard_map/all_to_all | solution.py:28
  207.2 6.1 %all-to-all-done.7 = f32[8,8,512]{2,1,0:T(8,128)} async-done(((f32[8,8,512]{2,1,0:T(8,128)}), f32[8,8,512]{2,1,0:T(8,128)}, u32[]{:S(2)}, u32[]{:S(2)}) %all-to-all-start.7) | async-done | bytes 131104 | tf_op jit(solution)/shard_map/all_to_all | solution.py:28
  214.8 4.0 %all-to-all-start.8 = ((f32[8,8,512]{2,1,0:T(8,128)}), f32[8,8,512]{2,1,0:T(8,128)}, u32[]{:S(2)}, u32[]{:S(2)}) async-start(f32[8,8,512]{2,1,0:T(8,128)} %broadcast_in_dim.75), calls=%async_computation.8 | async-start | bytes 262144 | tf_op jit(solution)/shard_map/all_to_all | solution.py:28
  219.5 5.9 %all-to-all-done.8 = f32[8,8,512]{2,1,0:T(8,128)} async-done(((f32[8,8,512]{2,1,0:T(8,128)}), f32[8,8,512]{2,1,0:T(8,128)}, u32[]{:S(2)}, u32[]{:S(2)}) %all-to-all-start.8) | async-done | bytes 131104 | tf_op jit(solution)/shard_map/all_to_all | solution.py:28
  226.5 10.6 %all_to_all.61 = f32[8,8,1280]{2,1,0:T(8,128)S(1)} all-to-all(f32[8,8,1280]{2,1,0:T(8,128)S(1)} %bitcast.88), channel_id=1, replica_groups={{0,1,2,3,4,5,6,7},{8,9,10,11,12,13,14,15},{16,17,18,19,20,21,22,23},{24..., dimensions={0} | all-to-all | bytes 655360 | tf_op jit(solution)/shard_map/all_to_all | solution.py:28
  237.1 5.0 %fusion.2 = f32[8,8,1024]{2,1,0:T(8,128)S(1)} fusion(f32[64,1024]{1,0:T(8,128)} %copy-done.3, f32[1024,1280]{1,0:T(8,128)} %param.15, f32[8,8,1280]{2,1,0:T(8,128)S(1)} %all_to_all.61), kind=kOutput, calls=%fused_computation.4 | convolution fusion | flops 503382016 | bytes 6094848 | tf_op jit(solution)/shard_map/dot_general | solution.py:64
  242.1 9.9 %all_to_all.62 = f32[8,8,1024]{2,1,0:T(8,128)S(1)} all-to-all(f32[8,8,1024]{2,1,0:T(8,128)S(1)} %fusion.2), channel_id=1, replica_groups={{0,1,2,3,4,5,6,7},{8,9,10,11,12,13,14,15},{16,17,18,19,20,21,22,23},{24..., dimensions={0} | all-to-all | bytes 524288 | tf_op jit(solution)/shard_map/all_to_all | solution.py:28
  (94 shorter events, 48.5 us)
Async XLA Ops:
  2.7 20.3 %all-to-all-start = ((f32[32,8,512]{2,1,0:T(8,128)}), f32[32,8,512]{2,1,0:T(8,128)}, u32[]{:S(2)}, u32[]{:S(2)}) async-start(f32[32,8,512]{2,1,0:T(8,128)} %bitcast.82), calls=%async_computation | async-start | bytes 1048576 | tf_op jit(solution)/shard_map/all_to_all | solution.py:28
  26.5 1.7 collective-permute-start
  29.7 10.5 %collective-permute-start.1 = (f32[64,512]{1,0:T(8,128)}, f32[64,512]{1,0:T(8,128)}, u32[]{:S(2)}, u32[]{:S(2)}) collective-permute-start(f32[64,512]{1,0:T(8,128)} %dynamic-slice_add_fusion), channel_id=1, source_target_pairs={{0,2},{1,3},{2,0},{3,1},{4,6},{5,7},{6,4},{7,5},{8,10},{9,11},{10,... | collective-permute-start | bytes 393224 | tf_op jit(solution)/shard_map/ppermute | solution.py:20
  30.3 10.0 %collective-permute-start.2 = (f32[64,512]{1,0:T(8,128)}, f32[64,512]{1,0:T(8,128)}, u32[]{:S(2)}, u32[]{:S(2)}) collective-permute-start(f32[64,512]{1,0:T(8,128)} %dynamic-slice_add_fusion), channel_id=1, source_target_pairs={{0,4},{1,5},{2,6},{3,7},{4,0},{5,1},{6,2},{7,3},{8,12},{9,13},{10,... | collective-permute-start | bytes 393224 | tf_op jit(solution)/shard_map/ppermute | solution.py:20
  32.5 9.3 %collective-permute-start.3 = (f32[64,512]{1,0:T(8,128)}, f32[64,512]{1,0:T(8,128)}, u32[]{:S(2)}, u32[]{:S(2)}) collective-permute-start(f32[64,512]{1,0:T(8,128)} %dynamic-slice_add_fusion), channel_id=1, source_target_pairs={{0,6},{1,7},{2,4},{3,5},{4,2},{5,3},{6,0},{7,1},{8,14},{9,15},{10,... | collective-permute-start | bytes 393224 | tf_op jit(solution)/shard_map/ppermute | solution.py:20
  35.1 8.6 %collective-permute-start.5 = (f32[8,2048]{1,0:T(8,128)}, f32[8,2048]{1,0:T(8,128)}, u32[]{:S(2)}, u32[]{:S(2)}) collective-permute-start(f32[8,2048]{1,0:T(8,128)} %slice.37), channel_id=1, source_target_pairs={{0,8},{1,9},{2,10},{3,11},{4,12},{5,13},{6,14},{7,15},{16,24},{17,... | collective-permute-start | bytes 196616 | tf_op jit(solution)/shard_map/ppermute | solution.py:20
  42.9 1.6 collective-permute-start.4
  50.4 2.4 collective-permute-start.6
  55.9 2.7 %collective-permute-start.7 = (f32[64,512]{1,0:T(8,128)}, f32[64,512]{1,0:T(8,128)S(1)}, u32[]{:S(2)}, u32[]{:S(2)}) collective-permute-start(f32[64,512]{1,0:T(8,128)} %get-tuple-element.3), channel_id=1, source_target_pairs={{16,18},{18,16},{19,17},{25,27},{28,30},{29,31},{30,28},{31,29},{4... | collective-permute-start | bytes 393224 | tf_op jit(solution)/shard_map/ppermute | solution.py:20
  56.6 2.0 collective-permute-start.8
  57.2 1.3 collective-permute-start.9
  60.4 3.3 %collective-permute-start.11 = (f32[64,512]{1,0:T(8,128)S(1)}, f32[64,512]{1,0:T(8,128)S(1)}, u32[]{:S(2)}, u32[]{:S(2)}) collective-permute-start(f32[64,512]{1,0:T(8,128)S(1)} %add.289), channel_id=1, source_target_pairs={{16,24},{17,25},{18,26},{27,19},{28,20},{29,21},{30,22},{31,23},{4... | collective-permute-start | bytes 393224 | tf_op jit(solution)/shard_map/ppermute | solution.py:20
  61.0 33.1 %collective-permute-start.12 = (f32[64,512]{1,0:T(8,128)S(1)}, f32[64,512]{1,0:T(8,128)S(1)}, u32[]{:S(2)}, u32[]{:S(2)}) collective-permute-start(f32[64,512]{1,0:T(8,128)S(1)} %add.289), channel_id=1, source_target_pairs={{16,0},{17,1},{18,2},{27,11},{28,12},{29,13},{30,14},{31,15},{48,3... | collective-permute-start | bytes 393224 | tf_op jit(solution)/shard_map/ppermute | solution.py:20
  62.3 31.8 %collective-permute-start.13 = (f32[64,512]{1,0:T(8,128)S(1)}, f32[64,512]{1,0:T(8,128)}, u32[]{:S(2)}, u32[]{:S(2)}) collective-permute-start(f32[64,512]{1,0:T(8,128)S(1)} %add.289), channel_id=1, source_target_pairs={{16,8},{17,9},{18,10},{27,3},{28,4},{29,5},{30,6},{31,7},{48,40},{... | collective-permute-start | bytes 393224 | tf_op jit(solution)/shard_map/ppermute | solution.py:20
  96.1 1.4 collective-permute-start.14
  97.5 7.9 %collective-permute-start.15 = (f32[64,512]{1,0:T(8,128)S(1)}, f32[64,512]{1,0:T(8,128)S(1)}, u32[]{:S(2)}, u32[]{:S(2)}) collective-permute-start(f32[64,512]{1,0:T(8,128)S(1)} %add.293), channel_id=1, source_target_pairs={{0,2},{1,3},{2,0},{3,1},{4,6},{5,7},{6,4},{7,5},{8,10},{9,11},{10,... | collective-permute-start | bytes 393224 | tf_op jit(solution)/shard_map/ppermute | solution.py:20
  97.7 9.0 %collective-permute-start.16 = (f32[64,512]{1,0:T(8,128)S(1)}, f32[64,512]{1,0:T(8,128)S(1)}, u32[]{:S(2)}, u32[]{:S(2)}) collective-permute-start(f32[64,512]{1,0:T(8,128)S(1)} %add.293), channel_id=1, source_target_pairs={{0,4},{1,5},{2,6},{3,7},{4,0},{5,1},{6,2},{7,3},{8,12},{9,13},{10,... | collective-permute-start | bytes 393224 | tf_op jit(solution)/shard_map/ppermute | solution.py:20
  100.2 8.7 %collective-permute-start.17 = (f32[64,512]{1,0:T(8,128)S(1)}, f32[64,512]{1,0:T(8,128)S(1)}, u32[]{:S(2)}, u32[]{:S(2)}) collective-permute-start(f32[64,512]{1,0:T(8,128)S(1)} %add.293), channel_id=1, source_target_pairs={{0,6},{1,7},{2,4},{3,5},{4,2},{5,3},{6,0},{7,1},{8,14},{9,15},{10,... | collective-permute-start | bytes 393224 | tf_op jit(solution)/shard_map/ppermute | solution.py:20
  102.3 14.2 %collective-permute-start.21 = (f32[32,1536]{1,0:T(8,128)S(1)}, f32[32,1536]{1,0:T(8,128)S(1)}, u32[]{:S(2)}, u32[]{:S(2)}) collective-permute-start(f32[32,1536]{1,0:T(8,128)S(1)} %constant_dynamic-slice_fusion.1), channel_id=1, source_target_pairs={{0,8},{1,9},{2,10},{3,11},{4,12},{5,13},{6,14},{7,15},{8,16},{9,17... | collective-permute-start | bytes 589832 | tf_op jit(solution)/shard_map/ppermute | solution.py:20
  109.0 1.4 collective-permute-start.18
  109.7 6.8 %collective-permute-start.20 = (f32[32,512]{1,0:T(8,128)S(1)}, f32[32,512]{1,0:T(8,128)S(1)}, u32[]{:S(2)}, u32[]{:S(2)}) collective-permute-start(f32[32,512]{1,0:T(8,128)S(1)} %get-tuple-element.7), channel_id=1, source_target_pairs={{8,24},{9,25},{10,26},{11,27},{12,28},{13,29},{14,30},{15,31},{40,... | collective-permute-start | bytes 196616 | tf_op jit(solution)/shard_map/ppermute | solution.py:20
  112.0 5.6 %collective-permute-start.19 = (f32[4,8,1536]{2,1,0:T(8,128)S(1)}, f32[4,8,1536]{2,1,0:T(8,128)S(1)}, u32[]{:S(2)}, u32[]{:S(2)}) collective-permute-start(f32[4,8,1536]{2,1,0:T(8,128)S(1)} %dynamic-slice_bitcast_fusion.1), channel_id=1, source_target_pairs={{0,1},{1,0},{2,3},{3,2},{4,5},{5,4},{6,7},{7,6},{8,9},{9,8},{10,11... | collective-permute-start | bytes 589832 | tf_op jit(solution)/shard_map/ppermute | solution.py:20
  203.2 10.1 %all-to-all-start.7 = ((f32[8,8,512]{2,1,0:T(8,128)}), f32[8,8,512]{2,1,0:T(8,128)}, u32[]{:S(2)}, u32[]{:S(2)}) async-start(f32[8,8,512]{2,1,0:T(8,128)} %fusion.3), calls=%async_computation.7 | async-start | bytes 262144 | tf_op jit(solution)/shard_map/all_to_all | solution.py:28
  214.8 10.6 %all-to-all-start.8 = ((f32[8,8,512]{2,1,0:T(8,128)}), f32[8,8,512]{2,1,0:T(8,128)}, u32[]{:S(2)}, u32[]{:S(2)}) async-start(f32[8,8,512]{2,1,0:T(8,128)} %broadcast_in_dim.75), calls=%async_computation.8 | async-start | bytes 262144 | tf_op jit(solution)/shard_map/all_to_all | solution.py:28
  (10 other events, 339.3 us)

commit v2 on v1

v2 whole, which is shorter than its diff:
```python
import jax
import jax.numpy as jnp
from jax import lax
from jax.experimental import pallas as pl
from jax.experimental.pallas import tpu as pltpu
from jax.sharding import PartitionSpec as P

AXES = ("leaf", "blk")
DEVICES = [(s // 32, s // 8 % 4, s // 2 % 4, s % 2) for s in range(128)]
ROWS = (((1,), (1,)), ((), ()))


def flat(x, z, y, c):
    return ((x * 4 + z) * 4 + y) * 2 + c


def send(value, hop):
    pairs = []
    for source, place in enumerate(DEVICES):
        target = hop(*place)
        if target is not None:
            pairs.append((source, flat(*target)))
    return lax.ppermute(value, AXES, pairs)


def exchange(value, key, order):
    groups = {}
    for source, place in enumerate(DEVICES):
        groups.setdefault(key(*place), []).append((order(*place), source))
    members = [[source for _, source in sorted(group)] for group in groups.values()]
    return lax.all_to_all(value, AXES, 0, 0, axis_index_groups=members)


def over_blk(value):
    return exchange(value, lambda x, z, y, c: (x, z), lambda x, z, y, c: 2 * y + c)


def over_leaf(value):
    return exchange(value, lambda x, z, y, c: (y, c), lambda x, z, y, c: 4 * x + z)


def over_half(value):
    return exchange(value, lambda x, z, y, c: (x // 2, y, c), lambda x, z, y, c: 4 * x + z)


def over_z(value):
    return exchange(value, lambda x, z, y, c: (x, y, c), lambda x, z, y, c: z)


def over_y(value):
    return exchange(value, lambda x, z, y, c: (x, z, c), lambda x, z, y, c: y)


def over_zy(value):
    return exchange(value, lambda x, z, y, c: (x, c), lambda x, z, y, c: 4 * z + y)


def over_sides(value):
    return exchange(value, lambda x, z, y, c: (x % 2, z), lambda x, z, y, c: (x, y, c))


def copies(value, number):
    return jnp.broadcast_to(value[None], (number, *value.shape))


def swap_core(value):
    return send(value, lambda x, z, y, c: (x, z, y, 1 - c))


def sum_y(value):
    return value + total([send(value, lambda x, z, y, c: (x, z, y ^ k, c)) for k in (1, 2, 3)])


def cols(value, start, size):
    return lax.dynamic_slice_in_dim(value, start, size, value.ndim - 1)


def pick(pieces, index):
    out = pieces[0]
    for number in range(1, len(pieces)):
        out = jnp.where(index == number, pieces[number], out)
    return out


def total(parts):
    out = parts[0]
    for part in parts[1:]:
        out = out + part
    return out


def place():
    leaf, blk = lax.axis_index("leaf"), lax.axis_index("blk")
    return leaf // 4, leaf % 4, blk // 2, blk % 2


def halves(value):
    high = value.astype(jnp.bfloat16)
    return high, (value - high.astype(jnp.float32)).astype(jnp.bfloat16)


def product(name, vectors, operator, inputs, outputs, store, tile, fetch=0):
    height, depth = operator.shape
    count, steps = len(inputs), height // tile

    def body(*refs):
        given, held, results = refs[:count], refs[count], refs[count + 1 :]
        moves = []
        if fetch:
            *results, room, sems = results
            for number in range(steps):
                here = pl.ds(number * tile, tile)
                moves.append(pltpu.make_async_copy(held.at[here], room.at[here], sems.at[number]))
                moves[-1].start()
            held = room
        high, low = halves(vectors(*given))
        both = jnp.concatenate([high, low], 0)
        for number in range(steps):
            if fetch:
                moves[number].wait()
            over, under = halves(held[number * tile : (number + 1) * tile, :])
            first = lax.dot_general(both, over, ROWS, preferred_element_type=jnp.float32)
            second = lax.dot_general(high, under, ROWS, preferred_element_type=jnp.float32)
            store(number, first[:64] + (first[64:] + second), *given, *results)

    block = pl.BlockSpec(memory_space=pltpu.VMEM)
    return pl.pallas_call(
        body,
        name=name,
        out_shape=[jax.ShapeDtypeStruct(shape, jnp.float32) for shape in outputs],
        in_specs=[block] * count + [pl.BlockSpec(memory_space=pl.ANY) if fetch else block],
        out_specs=[block] * len(outputs),
        scratch_shapes=[
            pltpu.VMEM((height, depth), jnp.float32),
            pltpu.SemaphoreType.DMA((steps,)),
        ]
        if fetch
        else [],
        compiler_params=pltpu.CompilerParams(vmem_limit_bytes=(fetch or 8) << 20),
        cost_estimate=pl.CostEstimate(
            flops=6 * 64 * height * depth, bytes_accessed=4 * height * depth, transcendentals=0
        ),
    )(*inputs, operator)


def gathered(parts, number):
    def body(parts, value, every):
        summed = total([parts[k] for k in range(parts.shape[0])])
        value[...] = summed
        for k in range(number):
            every[k] = summed

    shape = parts.shape[1:]
    return pl.pallas_call(
        body,
        name="gathered",
        out_shape=[
            jax.ShapeDtypeStruct(shape, jnp.float32),
            jax.ShapeDtypeStruct((number, *shape), jnp.float32),
        ],
        in_specs=[pl.BlockSpec(memory_space=pltpu.VMEM)],
        out_specs=[pl.BlockSpec(memory_space=pltpu.VMEM)] * 2,
        compiler_params=pltpu.CompilerParams(vmem_limit_bytes=8 << 20),
    )(parts)


def added(first, second, number=None):
    def body(first, second, out):
        if number is None:
            out[...] = first[...] + second[...]
        else:
            summed = first[...] + second[...]
            for k in range(number):
                out[k] = summed

    shape = first.shape if number is None else (number, *first.shape)
    return pl.pallas_call(
        body,
        name="added",
        out_shape=jax.ShapeDtypeStruct(shape, jnp.float32),
        in_specs=[pl.BlockSpec(memory_space=pltpu.VMEM)] * 2,
        out_specs=pl.BlockSpec(memory_space=pltpu.VMEM),
        compiler_params=pltpu.CompilerParams(vmem_limit_bytes=8 << 20),
    )(first, second)


def low_product(jump, operator):
    def vectors(jump):
        return (jump[4:8] + jump[12:16]).reshape(64, 512)

    def store(number, tile, jump, part, keep, give):
        part[:, 512 * number : 512 * (number + 1)] = tile
        core = place()[3]

        @pl.when(core == number)
        def _():
            keep[...] = tile

        @pl.when(core != number)
        def _():
            give[...] = tile

    shapes = [(64, 1024), (64, 512), (64, 512)]
    return product("low_w", vectors, operator, [jump], shapes, store, 512)


def lift_product(parts, particular, operator):
    def vectors(parts, particular):
        return parts[0] + parts[1] + (parts[2] + parts[3])

    def store(number, tile, parts, particular, keep, give, mine, other):
        x, z, y, c = place()
        if number == 0:
            keep[...] = jnp.zeros(keep.shape, jnp.float32)
            give[...] = jnp.zeros(give.shape, jnp.float32)
            for block in range(8):
                v, core = block // 2, block % 2
                source = 1024 + 512 * block if block < 7 else 0

                @pl.when((z == (2 if block < 7 else 3)) & (c == core))
                def _():
                    keep[y, v, pl.ds(pl.multiple_of(8 * c, 8), 8)] = particular[:, source : source + 512]

                @pl.when((z == (2 if block < 7 else 3)) & (c != core))
                def _():
                    give[y, v, pl.ds(pl.multiple_of(8 * c, 8), 8)] = particular[:, source : source + 512]

        here = pl.ds(512 * number, 512)
        block = number + jnp.where(z == 3, 3, -2)
        valid = (z == 3) | ((z == 2) & (number >= 2))
        row = jnp.clip(block // 2, 0, 3)

        @pl.when(valid & (block % 2 == c))
        def _():
            for k in range(4):
                keep[k, row] += tile[16 * k : 16 * k + 16]

        @pl.when(valid & (block % 2 != c))
        def _():
            for k in range(4):
                give[k, row] += tile[16 * k : 16 * k + 16]

        pairs = tile.reshape(4, 2, 8, 512)

        @pl.when(c == 0)
        def _():
            mine[:, :, here] = pairs[:, 0]
            other[:, :, here] = pairs[:, 1]

        @pl.when(c == 1)
        def _():
            mine[:, :, here] = pairs[:, 1]
            other[:, :, here] = pairs[:, 0]

    shapes = [(4, 4, 16, 512)] * 2 + [(4, 8, 2560)] * 2
    return product(
        "low_lift", vectors, operator, [parts, particular], shapes, store, 512
    )


def mid_product(parts, operator):
    def vectors(parts):
        return (parts[4:8] - parts[0:4]).reshape(64, 512)

    def store(number, tile, parts, out):
        out[:, 256 * number : 256 * (number + 1)] = tile

    return product("mid_w", vectors, operator, [parts], [(64, 512)], store, 256)[0]


def mid_lift_product(mid_w, outer, operator):
    def vectors(mid_w, outer):
        return mid_w[...]

    def store(number, tile, mid_w, outer, out):
        x, z, y, c = place()
        side, third = number // 3, number % 3
        added = outer[:, :, 256 * number : 256 * (number + 1)]
        sign = jnp.where(x // 2 == 1, 1.0, -1.0)
        pairs = tile.reshape(4, 2, 8, 256)
        for core in range(2):
            whole = sign * (pairs[:, core] + jnp.where(c == core, added, 0.0))
            for v in range(4):
                out[8 * side + 2 * v + core, :, 256 * third : 256 * (third + 1)] = whole[v]

    return product(
        "mid_lift", vectors, operator, [mid_w, outer], [(16, 8, 768)], store, 256
    )[0]


def wide_product(name, parts, operator, added=None):
    height = operator.shape[0]

    def vectors(parts, *added):
        return jnp.concatenate([parts[:, 0].reshape(64, 768), parts[:, 1].reshape(64, 768)], 1)

    def store(number, tile, *refs):
        here = slice(256 * number, 256 * (number + 1))
        if len(refs) == 3:
            tile = tile + refs[1][:, here]
        refs[-1][:, :, here] = tile.reshape(8, 8, 256)

    inputs = [parts] if added is None else [parts, added]
    return product(name, vectors, operator, inputs, [(8, 8, height)], store, 256)[0]


def last_product(bound, operator, added):
    def vectors(bound, added):
        return bound[...].reshape(64, 1280)

    def store(number, tile, bound, added, out):
        here = slice(256 * number, 256 * (number + 1))
        out[:, :, here] = (tile + added[:, here]).reshape(8, 8, 256)

    return product(
        "low_solve", vectors, operator, [bound, added], [(8, 8, 1024)], store, 256
    )[0]


def local(
    particular, root_inverse, mid_inverse, low_inverse, mid_lift, low_lift, mid_solve, low_solve
):
    x, z, y, c = place()
    xh, xl = x // 2, x % 2

    inner = (jnp.where(z == 3, 1.0, -1.0) * particular[:, 512:]).reshape(8, 4, 2, 512)
    keep = lax.dynamic_index_in_dim(inner, c, 2, False).transpose(1, 0, 2)
    got = swap_core(lax.dynamic_index_in_dim(inner, 1 - c, 2, False).transpose(1, 0, 2))
    both = jnp.concatenate([jnp.where(c == 0, keep, got), jnp.where(c == 0, got, keep)], 1)
    jump_two = over_zy(copies(both, 4).reshape(16, 16, 512))

    low_part, keep, give = low_product(jump_two, low_inverse)
    low_w = over_y(over_z(added(keep, swap_core(give), 4)))

    keep, give, mine, other = lift_product(low_w, particular, low_lift)

    blocks = added(keep, swap_core(give)).reshape(16, 16, 512)
    blocks, other, apart = lax.optimization_barrier((blocks, other, particular))
    jump_one = over_half(gathered(over_zy(blocks), 8)[1])

    mid_part = mid_product(jump_one, mid_inverse)
    mid_sum = sum_y(mid_part + swap_core(mid_part))
    mid_w = send(
        mid_sum, lambda x, z, y, c: (x // 2 * 2 + c, y ^ z, x % 2 * 2 + z // 2, z % 2)
    )

    moved = send(
        apart[:, 2560:], lambda x, z, y, c: (x, z + 1, y, c) if z % 2 == 0 else None
    )
    outer = jnp.where(
        z % 2 == 0, apart[:, :2560], jnp.concatenate([moved, apart[:, :512]], 1)
    )
    outer_half = mine + swap_core(other)
    outer_half = outer_half + jnp.where((jnp.arange(4) == y)[:, None, None], outer[None], 0.0)
    outer_half, mid_part = lax.optimization_barrier((outer_half, mid_part))
    next_z = send(
        cols(outer_half, jnp.where(z == 0, 1024, jnp.where(z == 1, 512, 0)), 1536),
        lambda x, z, y, c: (x, z + 1, y, c) if z < 3 else None,
    )
    far_z = send(
        outer_half[:, :, 2048:], lambda x, z, y, c: (x, 3, y, c) if z == 1 else None
    )
    outer_one = pick(
        [
            outer_half[:, :, :1536],
            jnp.concatenate([next_z[:, :, 512:], outer_half[:, :, :512]], 2),
            next_z,
            jnp.concatenate([far_z, next_z[:, :, :1024]], 2),
        ],
        z,
    )

    shares = mid_lift_product(mid_w, outer_one, mid_lift)
    every = over_leaf(gathered(over_sides(shares), 16)[1]).reshape(2, 8, 8, 768).transpose(1, 0, 2, 3)
    root_jump = over_blk(every)

    root_part = wide_product("root", root_jump, root_inverse)
    root_values, root_every = gathered(over_blk(root_part), 16)
    root_every = over_leaf(root_every)
    root_block = over_blk(root_every.reshape(8, 2, 8, 768))

    middle_part = wide_product("middle", root_block, mid_solve, mid_part)
    middle_values, middle_every = gathered(over_blk(middle_part), 8)
    middle_every = over_half(middle_every)

    root_half = lax.dynamic_slice_in_dim(root_every.reshape(2, 8, 8, 768), xl, 1, 0)[0]
    bound = jnp.concatenate(
        [
            root_half.transpose(1, 0, 2).reshape(8, 6144),
            middle_every.transpose(1, 0, 2).reshape(8, 4096),
        ],
        1,
    )
    bound = over_blk(bound.reshape(8, 8, 1280).transpose(1, 0, 2))
    lower_values = total(list(over_blk(last_product(bound, low_solve, low_part))))
    return (root_values, middle_values, lower_values)


def solution(mesh):
    placed = (P("blk", "leaf"),) + (P("leaf", "blk"),) * 7
    return jax.shard_map(
        local,
        mesh=mesh,
        in_specs=placed,
        out_specs=(P("blk", "leaf"),) * 3,
        check_vma=False,
    )
```

time: 254 us -> 238 us (0.937)
  blocking collectives: 98.9 us -> 149 us
  matrix products: 24.1 us -> 0 us
  waiting for transfers between devices: 64.8 us -> 41.4 us
  starting transfers between devices: 45 us -> 24.9 us
  Pallas kernels: 0 us -> 13.6 us
  other arithmetic: 9.79 us -> 1.85 us
  local copies, waits for them, and re-layouts: 9.12 us -> 5.03 us
    all_to_all x8 -> x11, blocking collectives: 98.9 us -> 149 us  [exchange(): return lax.all_to_all(value, AXES, 0, 0, axis_index_groups=members)]
    ppermute x22 -> x12, waiting for transfers between devices: 41 us -> 10.5 us  [send(): return lax.ppermute(value, AXES, pairs)]
    dot_general x7 -> x0, matrix products: 24.1 us -> none  [apply(): lax.dot_general(vectors, operator, (((1,), (1,)), ((), ())), precision=la...]
    ppermute x22 -> x12, starting transfers between devices: 28.5 us -> 10.6 us  [send(): return lax.ppermute(value, AXES, pairs)]
    pallas_call x0 -> x13, Pallas kernels: none -> 13.6 us  [the longest x7 10 us: product(): pl.pallas_call(body, name=name, out_shape=[jax.ShapeDtypeStruct(shape, jn...]
    all_to_all x3 -> x4, waiting for transfers between devices: 23.7 us -> 31 us  [exchange(): return lax.all_to_all(value, AXES, 0, 0, axis_index_groups=members)]
    unnamed x18 -> x20, local copies, waits for them, and re-layouts: 0.89 us -> 4.85 us
    add x3 -> x1, other arithmetic: 2.93 us -> 0.1 us  [local(): outer_half + jnp.where((jnp.arange(4) == y)[:, None, None], outer[None],...]
  transfers between devices with their start and end apart: 25 -> 16, of which waited for: 11 -> 9; matrix products, arithmetic and copies ran while one was open for 3% -> 0% of each run, Pallas kernels for 0% -> 0%
where the time goes in v2:
time: 238 us; the launch traced here: 237 us
  blocking collectives  149 us (63%)
  waiting for transfers between devices  41.4 us (17%)
  starting transfers between devices  24.9 us (10%)
  Pallas kernels  13.6 us (6%)
  local copies, waits for them, and re-layouts  5.03 us (2%)
    all_to_all x11, blocking collectives, exchange(): return lax.all_to_all(value, AXES, 0, 0, axis_index_groups=members)  149 us
    all_to_all x4, waiting for transfers between devices, exchange(): return lax.all_to_all(value, AXES, 0, 0, axis_index_groups=members)  31 us
    all_to_all x4, starting transfers between devices, exchange(): return lax.all_to_all(value, AXES, 0, 0, axis_index_groups=members)  14.4 us
    ppermute x12, starting transfers between devices, send(): return lax.ppermute(value, AXES, pairs)  10.6 us
    ppermute x12, waiting for transfers between devices, send(): return lax.ppermute(value, AXES, pairs)  10.5 us
    pallas_call x7, Pallas kernels, product(): pl.pallas_call(body, name=name, out_shape=[jax.ShapeDtypeStruct(shape, jn...  10 us
    unnamed x20, local copies, waits for them, and re-layouts  4.85 us
  transfers between devices with their start and end apart: 16, of which 9 were waited for; matrix products, arithmetic and copies ran while one was open for 0% of the time, Pallas kernels for 0%

profile of v2, /device:TPU:0, one launch (start us, length us, event | category | flops | bytes accessed | tf_op | source)
XLA Modules:
  0.0 236.8 jit_solution(1255923470890322374)
XLA Ops:
  3.1 19.9 %all_to_all.75.refs_0_ = f32[16,16,512]{2,1,0:T(8,128)S(1)} all-to-all(f32[16,16,512]{2,1,0:T(8,128)S(1)} %bitcast.35), channel_id=1, replica_groups={{0,2,4,6,8,10,12,14,16,18,20,22,24,26,28,30},{1,3,5,7,9,11,13,15,17,19,..., dimensions={0} | all-to-all | bytes 1048576 | tf_op jit(solution)/shard_map/all_to_all | solution.py:31
  27.0 12.5 %all_to_all.76 = f32[4,64,512]{2,1,0:T(8,128)S(1)} all-to-all(f32[4,64,512]{2,1,0:T(8,128)S(1)} %added.2), channel_id=1, replica_groups={{0,8,16,24},{1,9,17,25},{2,10,18,26},{3,11,19,27},{4,12,20,28},{5,13,21..., dimensions={0} | all-to-all | bytes 1048576 | tf_op jit(solution)/shard_map/all_to_all | solution.py:31
  39.5 11.8 %all_to_all.77.refs_0_ = f32[4,64,512]{2,1,0:T(8,128)S(1)} all-to-all(f32[4,64,512]{2,1,0:T(8,128)S(1)} %all_to_all.76), channel_id=1, replica_groups={{0,2,4,6},{1,3,5,7},{8,10,12,14},{9,11,13,15},{16,18,20,22},{17,19,21,2..., dimensions={0} | all-to-all | bytes 1048576 | tf_op jit(solution)/shard_map/all_to_all | solution.py:31
  51.2 2.4 %low_lift.1 = (f32[4,4,16,512]{3,2,1,0:T(8,128)S(1)}, f32[4,4,16,512]{3,2,1,0:T(8,128)S(1)}, f32[4,8,2560]{2,1,0:T(8,128)S(1)}, f32[4,8,2560]{2,1,0:T(8,128)S(1)}) custom-call(f32[4,64,512]{2,1,0:T(8,128)S(1)} %all_to_all.77.refs_0_, f32[8,4608]{1,0:T(8,128)S(1)} %copy-done.5, f32[2560,512]{1,0:T(8,128)S(1)} %copy-done), custom_call_target="tpu_custom_call" | custom-call | flops 503316480 | bytes 5242880 | tf_op jit(solution)/shard_map/low_lift/pallas_call | solution.py:127
  57.1 2.5 %collective-permute-start.9 = (f32[8,2048]{1,0:T(8,128)S(1)}, f32[8,2048]{1,0:T(8,128)S(1)}, u32[]{:S(2)}, u32[]{:S(2)}) collective-permute-start(f32[8,2048]{1,0:T(8,128)S(1)} %slice.29), channel_id=1, source_target_pairs={{0,8},{1,9},{2,10},{3,11},{4,12},{5,13},{6,14},{7,15},{16,24},{17,... | collective-permute-start | bytes 196616 | tf_op jit(solution)/shard_map/ppermute | solution.py:23
  59.6 4.2 %all-to-all-start.3 = ((f32[16,16,512]{2,1,0:T(8,128)}), f32[16,16,512]{2,1,0:T(8,128)S(1)}, u32[]{:S(2)}, u32[]{:S(2)}) async-start(f32[16,16,512]{2,1,0:T(8,128)} %bitcast.7), calls=%async_computation.3 | async-start | bytes 1048576 | tf_op jit(solution)/shard_map/all_to_all | solution.py:31
  64.0 11.4 %all-to-all-done.3.parts = f32[16,16,512]{2,1,0:T(8,128)S(1)} async-done(((f32[16,16,512]{2,1,0:T(8,128)}), f32[16,16,512]{2,1,0:T(8,128)S(1)}, u32[]{:S(2)}, u32[]{:S(2)}) %all-to-all-start.3) | async-done | bytes 524320 | tf_op jit(solution)/shard_map/all_to_all | solution.py:31
  76.1 3.4 %all-to-all-start.4 = ((f32[8,16,512]{2,1,0:T(8,128)}), f32[8,16,512]{2,1,0:T(8,128)S(1)}, u32[]{:S(2)}, u32[]{:S(2)}) async-start(f32[8,16,512]{2,1,0:T(8,128)} %get-tuple-element.27), calls=%async_computation.4 | async-start | bytes 524288 | tf_op jit(solution)/shard_map/all_to_all | solution.py:31
  79.7 7.0 %all-to-all-done.4.refs_0_ = f32[8,16,512]{2,1,0:T(8,128)S(1)} async-done(((f32[8,16,512]{2,1,0:T(8,128)}), f32[8,16,512]{2,1,0:T(8,128)S(1)}, u32[]{:S(2)}, u32[]{:S(2)}) %all-to-all-start.4) | async-done | bytes 262176 | tf_op jit(solution)/shard_map/all_to_all | solution.py:31
  87.3 2.3 collective-permute-start.11
  94.5 5.4 %collective-permute-done.6 = f32[64,512]{1,0:T(8,128)S(1)} collective-permute-done((f32[64,512]{1,0:T(8,128)S(1)}, f32[64,512]{1,0:T(8,128)S(1)}, u32[]{:S(2)}, u32[]{:S(2)}) %collective-permute-start.6) | collective-permute-done | bytes 131104 | tf_op jit(solution)/shard_map/ppermute | solution.py:23
  102.5 26.1 %all_to_all.78.parts = f32[16,8,768]{2,1,0:T(8,128)S(1)} all-to-all(f32[16,8,768]{2,1,0:T(8,128)S(1)} %mid_lift.1), channel_id=1, replica_groups={{0,1,2,3,4,5,6,7,64,65,66,67,68,69,70,71},{8,9,10,11,12,13,14,15,72,73,..., dimensions={0} | all-to-all | bytes 786432 | tf_op jit(solution)/shard_map/all_to_all | solution.py:31
  129.2 12.3 %all_to_all.79 = f32[16,8,768]{2,1,0:T(8,128)S(1)} all-to-all(f32[16,8,768]{2,1,0:T(8,128)S(1)} %get-tuple-element.32), channel_id=1, replica_groups={{0,8,16,24,32,40,48,56,64,72,80,88,96,104,112,120},{1,9,17,25,33,41,49,..., dimensions={0} | all-to-all | bytes 786432 | tf_op jit(solution)/shard_map/all_to_all | solution.py:31
  141.5 12.1 %all_to_all.80.refs_0_ = f32[8,2,8,768]{3,2,1,0:T(8,128)S(1)} all-to-all(f32[8,2,8,768]{3,2,1,0:T(8,128)S(1)} %bitcast.37), channel_id=1, replica_groups={{0,1,2,3,4,5,6,7},{8,9,10,11,12,13,14,15},{16,17,18,19,20,21,22,23},{24..., dimensions={0} | all-to-all | bytes 786432 | tf_op jit(solution)/shard_map/all_to_all | solution.py:31
  155.3 9.2 %all_to_all.81.parts = f32[8,8,768]{2,1,0:T(8,128)S(1)} all-to-all(f32[8,8,768]{2,1,0:T(8,128)S(1)} %root.1), channel_id=1, replica_groups={{0,1,2,3,4,5,6,7},{8,9,10,11,12,13,14,15},{16,17,18,19,20,21,22,23},{24..., dimensions={0} | all-to-all | bytes 393216 | tf_op jit(solution)/shard_map/all_to_all | solution.py:31
  165.1 13.1 %all_to_all.82 = f32[16,8,768]{2,1,0:T(8,128)S(1)} all-to-all(f32[16,8,768]{2,1,0:T(8,128)S(1)} %get-tuple-element.34), channel_id=1, replica_groups={{0,8,16,24,32,40,48,56,64,72,80,88,96,104,112,120},{1,9,17,25,33,41,49,..., dimensions={0} | all-to-all | bytes 786432 | tf_op jit(solution)/shard_map/all_to_all | solution.py:31
  178.2 11.3 %all_to_all.83.refs_0_ = f32[8,2,8,768]{3,2,1,0:T(8,128)S(1)} all-to-all(f32[8,2,8,768]{3,2,1,0:T(8,128)S(1)} %bitcast.33), channel_id=1, replica_groups={{0,1,2,3,4,5,6,7},{8,9,10,11,12,13,14,15},{16,17,18,19,20,21,22,23},{24..., dimensions={0} | all-to-all | bytes 786432 | tf_op jit(solution)/shard_map/all_to_all | solution.py:31
  191.3 3.4 %all-to-all-start.11 = ((f32[8,8,512]{2,1,0:T(8,128)}), f32[8,8,512]{2,1,0:T(8,128)S(1)}, u32[]{:S(2)}, u32[]{:S(2)}) async-start(f32[8,8,512]{2,1,0:T(8,128)} %middle.1), calls=%async_computation.11 | async-start | bytes 262144 | tf_op jit(solution)/shard_map/all_to_all | solution.py:31
  194.7 6.0 %all-to-all-done.11.parts = f32[8,8,512]{2,1,0:T(8,128)S(1)} async-done(((f32[8,8,512]{2,1,0:T(8,128)}), f32[8,8,512]{2,1,0:T(8,128)S(1)}, u32[]{:S(2)}, u32[]{:S(2)}) %all-to-all-start.11) | async-done | bytes 131104 | tf_op jit(solution)/shard_map/all_to_all | solution.py:31
  201.4 3.4 %all-to-all-start.12 = ((f32[8,8,512]{2,1,0:T(8,128)}), f32[8,8,512]{2,1,0:T(8,128)S(1)}, u32[]{:S(2)}, u32[]{:S(2)}) async-start(f32[8,8,512]{2,1,0:T(8,128)} %get-tuple-element.37), calls=%async_computation.12 | async-start | bytes 262144 | tf_op jit(solution)/shard_map/all_to_all | solution.py:31
  204.8 6.5 %all-to-all-done.12 = f32[8,8,512]{2,1,0:T(8,128)S(1)} async-done(((f32[8,8,512]{2,1,0:T(8,128)}), f32[8,8,512]{2,1,0:T(8,128)S(1)}, u32[]{:S(2)}, u32[]{:S(2)}) %all-to-all-start.12) | async-done | bytes 131104 | tf_op jit(solution)/shard_map/all_to_all | solution.py:31
  211.3 10.6 %all_to_all.84.refs_0_ = f32[8,8,1280]{2,1,0:T(8,128)S(1)} all-to-all(f32[8,8,1280]{2,1,0:T(8,128)S(1)} %bitcast.38), channel_id=1, replica_groups={{0,1,2,3,4,5,6,7},{8,9,10,11,12,13,14,15},{16,17,18,19,20,21,22,23},{24..., dimensions={0} | all-to-all | bytes 655360 | tf_op jit(solution)/shard_map/all_to_all | solution.py:31
  221.9 2.5 %copy-done.1 = f32[1024,1280]{1,0:T(8,128)S(1)} copy-done((f32[1024,1280]{1,0:T(8,128)S(1)}, f32[1024,1280]{1,0:T(8,128)}, u32[]{:S(2)}) %copy-start.1) | copy-done | bytes 5242904
  226.2 9.9 %all_to_all.85 = f32[8,8,1024]{2,1,0:T(8,128)S(1)} all-to-all(f32[8,8,1024]{2,1,0:T(8,128)S(1)} %low_solve.1), channel_id=1, replica_groups={{0,1,2,3,4,5,6,7},{8,9,10,11,12,13,14,15},{16,17,18,19,20,21,22,23},{24..., dimensions={0} | all-to-all | bytes 524288 | tf_op jit(solution)/shard_map/all_to_all | solution.py:31
  (74 shorter events, 26.6 us)
Async XLA Ops:
  0.6 50.6 %copy-start.5 = (f32[8,4608]{1,0:T(8,128)S(1)}, f32[8,4608]{1,0:T(8,128)}, u32[]{:S(2)}) copy-start(f32[8,4608]{1,0:T(8,128)} %refs_1_.5) | copy-start | bytes 442372
  1.6 1.3 collective-permute-start
  1.8 49.5 %copy-start = (f32[2560,512]{1,0:T(8,128)S(1)}, f32[2560,512]{1,0:T(8,128)}, u32[]{:S(2)}) copy-start(f32[2560,512]{1,0:T(8,128)} %refs_2_.4) | copy-start | bytes 15728644
  25.5 1.4 collective-permute-start.1
  39.5 24.5 %slice-start.2 = ((f32[8,4608]{1,0:T(8,128)}), f32[8,512]{1,0:T(8,128)S(1)}, s32[]{:S(2)}) async-start(f32[8,4608]{1,0:T(8,128)} %refs_1_.5), calls=%async_computation.17 | async-start | bytes 32768 | tf_op jit(solution)/shard_map/slice | solution.py:351
  51.2 35.5 %copy-start.6 = (f32[512,512]{1,0:T(8,128)S(1)}, f32[512,512]{1,0:T(8,128)}, u32[]{:S(2)}) copy-start(f32[512,512]{1,0:T(8,128)} %refs_1_.6) | copy-start | bytes 3145732
  54.4 1.9 collective-permute-start.2
  57.1 6.8 %collective-permute-start.9 = (f32[8,2048]{1,0:T(8,128)S(1)}, f32[8,2048]{1,0:T(8,128)S(1)}, u32[]{:S(2)}, u32[]{:S(2)}) collective-permute-start(f32[8,2048]{1,0:T(8,128)S(1)} %slice.29), channel_id=1, source_target_pairs={{0,8},{1,9},{2,10},{3,11},{4,12},{5,13},{6,14},{7,15},{16,24},{17,... | collective-permute-start | bytes 196616 | tf_op jit(solution)/shard_map/ppermute | solution.py:23
  59.6 94.1 %slice-start = ((s8[4718592]{0:T(1024)(128)(4,1)}), s8[524288]{0:T(1024)(128)(4,1)S(1)}, s32[]{:S(2)}) async-start(s8[4718592]{0:T(1024)(128)(4,1)} %bitcast.31), calls=%async_computation.15 | async-start | bytes 1048576
  59.6 15.8 %all-to-all-start.3 = ((f32[16,16,512]{2,1,0:T(8,128)}), f32[16,16,512]{2,1,0:T(8,128)S(1)}, u32[]{:S(2)}, u32[]{:S(2)}) async-start(f32[16,16,512]{2,1,0:T(8,128)} %bitcast.7), calls=%async_computation.3 | async-start | bytes 1048576 | tf_op jit(solution)/shard_map/all_to_all | solution.py:31
  63.8 15.7 %collective-permute-start.8 = (f32[4,8,2560]{2,1,0:T(8,128)}, f32[4,8,2560]{2,1,0:T(8,128)S(1)}, u32[]{:S(2)}, u32[]{:S(2)}) collective-permute-start(f32[4,8,2560]{2,1,0:T(8,128)} %copy-done.7), channel_id=1, source_target_pairs={{0,1},{1,0},{2,3},{3,2},{4,5},{5,4},{6,7},{7,6},{8,9},{9,8},{10,11... | collective-permute-start | bytes 983048 | tf_op jit(solution)/shard_map/ppermute | solution.py:23
  76.1 10.6 %all-to-all-start.4 = ((f32[8,16,512]{2,1,0:T(8,128)}), f32[8,16,512]{2,1,0:T(8,128)S(1)}, u32[]{:S(2)}, u32[]{:S(2)}) async-start(f32[8,16,512]{2,1,0:T(8,128)} %get-tuple-element.27), calls=%async_computation.4 | async-start | bytes 524288 | tf_op jit(solution)/shard_map/all_to_all | solution.py:31
  86.7 14.6 %copy-start.2 = (f32[1536,512]{1,0:T(8,128)S(1)}, f32[1536,512]{1,0:T(8,128)}, u32[]{:S(2)}) copy-start(f32[1536,512]{1,0:T(8,128)} %refs_2_.5) | copy-start | bytes 9437188
  87.2 3.1 %collective-permute-start.3 = (f32[64,512]{1,0:T(8,128)S(1)}, f32[64,512]{1,0:T(8,128)S(1)}, u32[]{:S(2)}, u32[]{:S(2)}) collective-permute-start(f32[64,512]{1,0:T(8,128)S(1)} %mid_w.1.refs_1_), channel_id=1, source_target_pairs={{0,1},{1,0},{2,3},{3,2},{4,5},{5,4},{6,7},{7,6},{8,9},{9,8},{10,11... | collective-permute-start | bytes 393224 | tf_op jit(solution)/shard_map/ppermute | solution.py:23
  87.3 7.2 %collective-permute-start.11 = (f32[4,8,1536]{2,1,0:T(8,128)S(1)}, f32[4,8,1536]{2,1,0:T(8,128)S(1)}, u32[]{:S(2)}, u32[]{:S(2)}) collective-permute-start(f32[4,8,1536]{2,1,0:T(8,128)S(1)} %constant_dynamic-slice_fusion.1), channel_id=1, source_target_pairs={{0,8},{1,9},{2,10},{3,11},{4,12},{5,13},{6,14},{7,15},{8,16},{9,17... | collective-permute-start | bytes 589832 | tf_op jit(solution)/shard_map/ppermute | solution.py:23
  89.6 11.6 %collective-permute-start.10 = (f32[4,8,512]{2,1,0:T(8,128)S(1)}, f32[4,8,512]{2,1,0:T(8,128)S(1)}, u32[]{:S(2)}, u32[]{:S(2)}) collective-permute-start(f32[4,8,512]{2,1,0:T(8,128)S(1)} %get-tuple-element.40), channel_id=1, source_target_pairs={{8,24},{9,25},{10,26},{11,27},{12,28},{13,29},{14,30},{15,31},{40,... | collective-permute-start | bytes 196616 | tf_op jit(solution)/shard_map/ppermute | solution.py:23
  90.3 9.6 %collective-permute-start.6 = (f32[64,512]{1,0:T(8,128)S(1)}, f32[64,512]{1,0:T(8,128)S(1)}, u32[]{:S(2)}, u32[]{:S(2)}) collective-permute-start(f32[64,512]{1,0:T(8,128)S(1)} %add.76), channel_id=1, source_target_pairs={{0,6},{1,7},{2,4},{3,5},{4,2},{5,3},{6,0},{7,1},{8,14},{9,15},{10,... | collective-permute-start | bytes 393224 | tf_op jit(solution)/shard_map/ppermute | solution.py:23
  91.3 8.6 %collective-permute-start.5 = (f32[64,512]{1,0:T(8,128)S(1)}, f32[64,512]{1,0:T(8,128)S(1)}, u32[]{:S(2)}, u32[]{:S(2)}) collective-permute-start(f32[64,512]{1,0:T(8,128)S(1)} %add.76), channel_id=1, source_target_pairs={{0,4},{1,5},{2,6},{3,7},{4,0},{5,1},{6,2},{7,3},{8,12},{9,13},{10,... | collective-permute-start | bytes 393224 | tf_op jit(solution)/shard_map/ppermute | solution.py:23
  93.0 7.5 %collective-permute-start.4 = (f32[64,512]{1,0:T(8,128)S(1)}, f32[64,512]{1,0:T(8,128)S(1)}, u32[]{:S(2)}, u32[]{:S(2)}) collective-permute-start(f32[64,512]{1,0:T(8,128)S(1)} %add.76), channel_id=1, source_target_pairs={{0,2},{1,3},{2,0},{3,1},{4,6},{5,7},{6,4},{7,5},{8,10},{9,11},{10,... | collective-permute-start | bytes 393224 | tf_op jit(solution)/shard_map/ppermute | solution.py:23
  100.5 0.8 collective-permute-start.7
  101.2 52.5 %slice-start.1 = ((s8[4718592]{0:T(1024)(128)(4,1)}), s8[4194304]{0:T(1024)(128)(4,1)S(1)}, s32[]{:S(2)}) async-start(s8[4718592]{0:T(1024)(128)(4,1)} %bitcast.31), calls=%async_computation.16 | async-start | bytes 8388608
  141.5 48.0 %copy-start.3 = (f32[512,1536]{1,0:T(8,128)S(1)}, f32[512,1536]{1,0:T(8,128)}, u32[]{:S(2)}) copy-start(f32[512,1536]{1,0:T(8,128)} %refs_2_.6) | copy-start | bytes 9437188
  191.3 9.4 %all-to-all-start.11 = ((f32[8,8,512]{2,1,0:T(8,128)}), f32[8,8,512]{2,1,0:T(8,128)S(1)}, u32[]{:S(2)}, u32[]{:S(2)}) async-start(f32[8,8,512]{2,1,0:T(8,128)} %middle.1), calls=%async_computation.11 | async-start | bytes 262144 | tf_op jit(solution)/shard_map/all_to_all | solution.py:31
  201.4 9.9 %all-to-all-start.12 = ((f32[8,8,512]{2,1,0:T(8,128)}), f32[8,8,512]{2,1,0:T(8,128)S(1)}, u32[]{:S(2)}, u32[]{:S(2)}) async-start(f32[8,8,512]{2,1,0:T(8,128)} %get-tuple-element.37), calls=%async_computation.12 | async-start | bytes 262144 | tf_op jit(solution)/shard_map/all_to_all | solution.py:31
  (3 other events, 4.8 us)

commit v3 on v2

--- a/solution.py
+++ b/solution.py
@@ -55,8 +55,8 @@
     return exchange(value, lambda x, z, y, c: (x, c), lambda x, z, y, c: 4 * z + y)
 
 
-def over_sides(value):
-    return exchange(value, lambda x, z, y, c: (x % 2, z), lambda x, z, y, c: (x, y, c))
+def over_all(value):
+    return exchange(value, lambda x, z, y, c: 0, flat)
 
 
 def copies(value, number):
@@ -136,7 +136,7 @@
         ]
         if fetch
         else [],
-        compiler_params=pltpu.CompilerParams(vmem_limit_bytes=(fetch or 8) << 20),
+        compiler_params=pltpu.CompilerParams(vmem_limit_bytes=(fetch or 4) << 20),
         cost_estimate=pl.CostEstimate(
             flops=6 * 64 * height * depth, bytes_accessed=4 * height * depth, transcendentals=0
         ),
@@ -160,7 +160,7 @@
         ],
         in_specs=[pl.BlockSpec(memory_space=pltpu.VMEM)],
         out_specs=[pl.BlockSpec(memory_space=pltpu.VMEM)] * 2,
-        compiler_params=pltpu.CompilerParams(vmem_limit_bytes=8 << 20),
+        compiler_params=pltpu.CompilerParams(vmem_limit_bytes=4 << 20),
     )(parts)
 
 
@@ -180,13 +180,13 @@
         out_shape=jax.ShapeDtypeStruct(shape, jnp.float32),
         in_specs=[pl.BlockSpec(memory_space=pltpu.VMEM)] * 2,
         out_specs=pl.BlockSpec(memory_space=pltpu.VMEM),
-        compiler_params=pltpu.CompilerParams(vmem_limit_bytes=8 << 20),
+        compiler_params=pltpu.CompilerParams(vmem_limit_bytes=4 << 20),
     )(first, second)
 
 
 def low_product(jump, operator):
     def vectors(jump):
-        return (jump[4:8] + jump[12:16]).reshape(64, 512)
+        return (jump[12:16] - jump[4:8]).reshape(64, 512)
 
     def store(number, tile, jump, part, keep, give):
         part[:, 512 * number : 512 * (number + 1)] = tile
@@ -274,24 +274,50 @@
 
     def store(number, tile, mid_w, outer, out):
         x, z, y, c = place()
-        side, third = number // 3, number % 3
+        if number == 0:
+            out[96:] = jnp.zeros((32, 8, 128), jnp.float32)
         added = outer[:, :, 256 * number : 256 * (number + 1)]
         sign = jnp.where(x // 2 == 1, 1.0, -1.0)
         pairs = tile.reshape(4, 2, 8, 256)
         for core in range(2):
             whole = sign * (pairs[:, core] + jnp.where(c == core, added, 0.0))
             for v in range(4):
-                out[8 * side + 2 * v + core, :, 256 * third : 256 * (third + 1)] = whole[v]
+                first = 12 * (2 * v + core) + 2 * number
+                out[first] = whole[v, :, :128]
+                out[first + 1] = whole[v, :, 128:]
 
     return product(
-        "mid_lift", vectors, operator, [mid_w, outer], [(16, 8, 768)], store, 256
+        "mid_lift", vectors, operator, [mid_w, outer], [(128, 8, 128)], store, 256
     )[0]
+
+
+def mixed(parts):
+    def body(parts, out):
+        for block in range(8):
+            given = [parts[64 * side + 8 * block + k] for side in range(2) for k in range(8)]
+            summed = total(given)
+            for leaf in range(16):
+                out[8 * leaf + block] = summed
+
+    return pl.pallas_call(
+        body,
+        name="mixed",
+        out_shape=jax.ShapeDtypeStruct((128, 8, 128), jnp.float32),
+        in_specs=[pl.BlockSpec(memory_space=pltpu.VMEM)],
+        out_specs=pl.BlockSpec(memory_space=pltpu.VMEM),
+        compiler_params=pltpu.CompilerParams(vmem_limit_bytes=4 << 20),
+    )(parts)
 
 
 def wide_product(name, parts, operator, added=None):
     height = operator.shape[0]
 
     def vectors(parts, *added):
+        if parts.shape[0] == 128:
+            lines = [
+                jnp.concatenate([parts[12 * k + n] for n in range(12)], 1) for k in range(8)
+            ]
+            return jnp.concatenate(lines, 0)
         return jnp.concatenate([parts[:, 0].reshape(64, 768), parts[:, 1].reshape(64, 768)], 1)
 
     def store(number, tile, *refs):
@@ -304,17 +330,41 @@
     return product(name, vectors, operator, inputs, [(8, 8, height)], store, 256)[0]
 
 
-def last_product(bound, operator, added):
-    def vectors(bound, added):
-        return bound[...].reshape(64, 1280)
-
-    def store(number, tile, bound, added, out):
-        here = slice(256 * number, 256 * (number + 1))
-        out[:, :, here] = (tile + added[:, here]).reshape(8, 8, 256)
-
-    return product(
-        "low_solve", vectors, operator, [bound, added], [(8, 8, 1024)], store, 256
-    )[0]
+def split_ahead(operator):
+    def body(held, over, under):
+        for number in range(4):
+            here = slice(256 * number, 256 * (number + 1))
+            over[here, :], under[here, :] = halves(held[here, :])
+
+    return pl.pallas_call(
+        body,
+        name="split_ahead",
+        out_shape=[jax.ShapeDtypeStruct(operator.shape, jnp.bfloat16)] * 2,
+        in_specs=[pl.BlockSpec(memory_space=pltpu.VMEM)],
+        out_specs=[pl.BlockSpec(memory_space=pltpu.VMEM)] * 2,
+        compiler_params=pltpu.CompilerParams(vmem_limit_bytes=4 << 20),
+    )(operator)
+
+
+def last_product(bound, over, under, added):
+    def body(bound, added, over, under, out):
+        high, low = halves(bound[...].reshape(64, 1280))
+        both = jnp.concatenate([high, low], 0)
+        for number in range(4):
+            here = slice(256 * number, 256 * (number + 1))
+            first = lax.dot_general(both, over[here, :], ROWS, preferred_element_type=jnp.float32)
+            second = lax.dot_general(high, under[here, :], ROWS, preferred_element_type=jnp.float32)
+            tile = first[:64] + (first[64:] + second) + added[:, here]
+            out[:, :, here] = tile.reshape(8, 8, 256)
+
+    return pl.pallas_call(
+        body,
+        name="low_solve",
+        out_shape=jax.ShapeDtypeStruct((8, 8, 1024), jnp.float32),
+        in_specs=[pl.BlockSpec(memory_space=pltpu.VMEM)] * 4,
+        out_specs=pl.BlockSpec(memory_space=pltpu.VMEM),
+        compiler_params=pltpu.CompilerParams(vmem_limit_bytes=4 << 20),
+    )(bound, added, over, under)
 
 
 def local(
@@ -323,7 +373,7 @@
     x, z, y, c = place()
     xh, xl = x // 2, x % 2
 
-    inner = (jnp.where(z == 3, 1.0, -1.0) * particular[:, 512:]).reshape(8, 4, 2, 512)
+    inner = particular[:, 512:].reshape(8, 4, 2, 512)
     keep = lax.dynamic_index_in_dim(inner, c, 2, False).transpose(1, 0, 2)
     got = swap_core(lax.dynamic_index_in_dim(inner, 1 - c, 2, False).transpose(1, 0, 2))
     both = jnp.concatenate([jnp.where(c == 0, keep, got), jnp.where(c == 0, got, keep)], 1)
@@ -344,35 +394,46 @@
         mid_sum, lambda x, z, y, c: (x // 2 * 2 + c, y ^ z, x % 2 * 2 + z // 2, z % 2)
     )
 
-    moved = send(
-        apart[:, 2560:], lambda x, z, y, c: (x, z + 1, y, c) if z % 2 == 0 else None
-    )
+    here = (jnp.arange(4) == y)[:, None, None]
+    nothing = jnp.zeros((8, 2048), jnp.float32)
     outer = jnp.where(
-        z % 2 == 0, apart[:, :2560], jnp.concatenate([moved, apart[:, :512]], 1)
-    )
-    outer_half = mine + swap_core(other)
-    outer_half = outer_half + jnp.where((jnp.arange(4) == y)[:, None, None], outer[None], 0.0)
-    outer_half, mid_part = lax.optimization_barrier((outer_half, mid_part))
+        z == 1, jnp.concatenate([nothing, apart[:, :512]], 1), apart[:, :2560]
+    )
+    outer_half = mine + swap_core(other) + jnp.where(here, outer[None], 0.0)
+    beyond = jnp.where(here, apart[None, :, 2560:3072], 0.0)
     next_z = send(
-        cols(outer_half, jnp.where(z == 0, 1024, jnp.where(z == 1, 512, 0)), 1536),
+        pick(
+            [
+                jnp.concatenate([beyond, outer_half[:, :, 1536:]], 2),
+                outer_half[:, :, 512:2048],
+                outer_half[:, :, :1536],
+            ],
+            z,
+        ),
         lambda x, z, y, c: (x, z + 1, y, c) if z < 3 else None,
     )
+    thirds = apart[:, 3072:].reshape(8, 3, 512).transpose(1, 0, 2)
     far_z = send(
-        outer_half[:, :, 2048:], lambda x, z, y, c: (x, 3, y, c) if z == 1 else None
-    )
+        jnp.where(
+            z == 0,
+            jnp.concatenate([thirds, jnp.zeros((1, 8, 512), jnp.float32)], 0),
+            outer_half[:, :, 2048:],
+        ),
+        lambda x, z, y, c: (x, z + 2, y, c) if z < 2 else None,
+    )
+    wide = jnp.concatenate([far_z[0], far_z[1], far_z[2]], 1)
     outer_one = pick(
         [
             outer_half[:, :, :1536],
-            jnp.concatenate([next_z[:, :, 512:], outer_half[:, :, :512]], 2),
-            next_z,
+            jnp.concatenate([next_z[:, :, 512:], outer_half[:, :, :512] + next_z[:, :, :512]], 2),
+            next_z + jnp.where(here, wide[None], 0.0),
             jnp.concatenate([far_z, next_z[:, :, :1024]], 2),
         ],
         z,
     )
 
     shares = mid_lift_product(mid_w, outer_one, mid_lift)
-    every = over_leaf(gathered(over_sides(shares), 16)[1]).reshape(2, 8, 8, 768).transpose(1, 0, 2, 3)
-    root_jump = over_blk(every)
+    root_jump = over_all(mixed(over_all(shares)))
 
     root_part = wide_product("root", root_jump, root_inverse)
     root_values, root_every = gathered(over_blk(root_part), 16)
@@ -381,7 +442,9 @@
 
     middle_part = wide_product("middle", root_block, mid_solve, mid_part)
     middle_values, middle_every = gathered(over_blk(middle_part), 8)
+    middle_every, low_solve = lax.optimization_barrier((middle_every, low_solve))
     middle_every = over_half(middle_every)
+    over, under = split_ahead(low_solve)
 
     root_half = lax.dynamic_slice_in_dim(root_every.reshape(2, 8, 8, 768), xl, 1, 0)[0]
     bound = jnp.concatenate(
@@ -392,7 +455,7 @@
         1,
     )
     bound = over_blk(bound.reshape(8, 8, 1280).transpose(1, 0, 2))
-    lower_values = total(list(over_blk(last_product(bound, low_solve, low_part))))
+    lower_values = total(list(over_blk(last_product(bound, over, under, low_part))))
     return (root_values, middle_values, lower_values)
 
 

time: 238 us -> 230 us (0.966)
  blocking collectives: 149 us -> 135 us
  starting transfers between devices: 24.9 us -> 31.7 us
  waiting for transfers between devices: 41.4 us -> 37.4 us
  local copies, waits for them, and re-layouts: 5.03 us -> 7.68 us
    all_to_all x11 -> x9, blocking collectives: 149 us -> 135 us  [exchange(): return lax.all_to_all(value, AXES, 0, 0, axis_index_groups=members)]
    all_to_all x4 -> x5, waiting for transfers between devices: 31 us -> 23.9 us  [exchange(): return lax.all_to_all(value, AXES, 0, 0, axis_index_groups=members)]
    ppermute x12 -> x11, starting transfers between devices: 10.6 us -> 14.4 us  [send(): return lax.ppermute(value, AXES, pairs)]
    ppermute x12 -> x11, waiting for transfers between devices: 10.5 us -> 13.5 us  [send(): return lax.ppermute(value, AXES, pairs)]
    all_to_all x4 -> x5, starting transfers between devices: 14.4 us -> 17.3 us  [exchange(): return lax.all_to_all(value, AXES, 0, 0, axis_index_groups=members)]
    pallas_call x0 -> x3, Pallas kernels: none -> 2.52 us  [the longest x1 1.75 us: last_product(): pl.pallas_call(body, name='low_solve', out_shape=jax.ShapeDtypeStruct((8,...]
    pallas_call x7 -> x6, Pallas kernels: 10 us -> 8.28 us  [product(): pl.pallas_call(body, name=name, out_shape=[jax.ShapeDtypeStruct(shape, jn...]
    unnamed x20 -> x28, local copies, waits for them, and re-layouts: 4.85 us -> 6.49 us
  transfers between devices with their start and end apart: 16 -> 16, of which waited for: 9 -> 12; matrix products, arithmetic and copies ran while one was open for 0% -> 0% of each run, Pallas kernels for 0% -> 1%
where the time goes in v3:
time: 230 us; the launch traced here: 229 us
  blocking collectives  135 us (59%)
  waiting for transfers between devices  37.4 us (16%)
  starting transfers between devices  31.7 us (14%)
  Pallas kernels  13.8 us (6%)
  local copies, waits for them, and re-layouts  7.68 us (3%)
    all_to_all x9, blocking collectives, exchange(): return lax.all_to_all(value, AXES, 0, 0, axis_index_groups=members)  135 us
    all_to_all x5, waiting for transfers between devices, exchange(): return lax.all_to_all(value, AXES, 0, 0, axis_index_groups=members)  23.9 us
    all_to_all x5, starting transfers between devices, exchange(): return lax.all_to_all(value, AXES, 0, 0, axis_index_groups=members)  17.3 us
    ppermute x11, starting transfers between devices, send(): return lax.ppermute(value, AXES, pairs)  14.4 us
    ppermute x11, waiting for transfers between devices, send(): return lax.ppermute(value, AXES, pairs)  13.5 us
    pallas_call x6, Pallas kernels, product(): pl.pallas_call(body, name=name, out_shape=[jax.ShapeDtypeStruct(shape, jn...  8.28 us
    unnamed x28, local copies, waits for them, and re-layouts  6.49 us
  transfers between devices with their start and end apart: 16, of which 12 were waited for; matrix products, arithmetic and copies ran while one was open for 0% of the time, Pallas kernels for 1%

profile of v3, /device:TPU:0, one launch (start us, length us, event | category | flops | bytes accessed | tf_op | source)
XLA Modules:
  0.0 228.6 jit_solution(6439780272105698145)
XLA Ops:
  3.2 20.1 %all_to_all.70.refs_0_ = f32[16,16,512]{2,1,0:T(8,128)S(1)} all-to-all(f32[16,16,512]{2,1,0:T(8,128)S(1)} %bitcast.41), channel_id=1, replica_groups={{0,2,4,6,8,10,12,14,16,18,20,22,24,26,28,30},{1,3,5,7,9,11,13,15,17,19,..., dimensions={0} | all-to-all | bytes 1048576 | tf_op jit(solution)/shard_map/all_to_all | solution.py:31
  25.7 12.5 %all_to_all.71 = f32[4,64,512]{2,1,0:T(8,128)S(1)} all-to-all(f32[4,64,512]{2,1,0:T(8,128)S(1)} %added.2), channel_id=1, replica_groups={{0,8,16,24},{1,9,17,25},{2,10,18,26},{3,11,19,27},{4,12,20,28},{5,13,21..., dimensions={0} | all-to-all | bytes 1048576 | tf_op jit(solution)/shard_map/all_to_all | solution.py:31
  38.1 11.6 %all_to_all.72.refs_0_ = f32[4,64,512]{2,1,0:T(8,128)S(1)} all-to-all(f32[4,64,512]{2,1,0:T(8,128)S(1)} %all_to_all.71), channel_id=1, replica_groups={{0,2,4,6},{1,3,5,7},{8,10,12,14},{9,11,13,15},{16,18,20,22},{17,19,21,2..., dimensions={0} | all-to-all | bytes 1048576 | tf_op jit(solution)/shard_map/all_to_all | solution.py:31
  49.8 2.4 %low_lift.1 = (f32[4,4,16,512]{3,2,1,0:T(8,128)S(1)}, f32[4,4,16,512]{3,2,1,0:T(8,128)S(1)}, f32[4,8,2560]{2,1,0:T(8,128)S(1)}, f32[4,8,2560]{2,1,0:T(8,128)S(1)}) custom-call(f32[4,64,512]{2,1,0:T(8,128)S(1)} %all_to_all.72.refs_0_, f32[8,4608]{1,0:T(8,128)S(1)} %copy-done.7, f32[2560,512]{1,0:T(8,128)S(1)} %copy-done), custom_call_target="tpu_custom_call" | custom-call | flops 503316480 | bytes 5242880 | tf_op jit(solution)/shard_map/low_lift/pallas_call | solution.py:127
  52.9 1.9 collective-permute-done.2.second
  55.7 3.7 %all-to-all-start.3 = ((f32[16,16,512]{2,1,0:T(8,128)}), f32[16,16,512]{2,1,0:T(8,128)S(1)}, u32[]{:S(2)}, u32[]{:S(2)}) async-start(f32[16,16,512]{2,1,0:T(8,128)} %bitcast.7), calls=%async_computation.3 | async-start | bytes 1048576 | tf_op jit(solution)/shard_map/all_to_all | solution.py:31
  61.5 3.7 %collective-permute-start.10 = (f32[4,8,1536]{2,1,0:T(8,128)S(1)}, f32[4,8,1536]{2,1,0:T(8,128)S(1)}, u32[]{:S(2)}, u32[]{:S(2)}) collective-permute-start(f32[4,8,1536]{2,1,0:T(8,128)S(1)} %fusion), channel_id=1, source_target_pairs={{0,8},{1,9},{2,10},{3,11},{4,12},{5,13},{6,14},{7,15},{8,16},{9,17... | collective-permute-start | bytes 589832 | tf_op jit(solution)/shard_map/ppermute | solution.py:23
  65.2 6.2 %all-to-all-done.3.parts = f32[16,16,512]{2,1,0:T(8,128)S(1)} async-done(((f32[16,16,512]{2,1,0:T(8,128)}), f32[16,16,512]{2,1,0:T(8,128)S(1)}, u32[]{:S(2)}, u32[]{:S(2)}) %all-to-all-start.3) | async-done | bytes 524320 | tf_op jit(solution)/shard_map/all_to_all | solution.py:31
  72.2 3.4 %all-to-all-start.4 = ((f32[8,16,512]{2,1,0:T(8,128)}), f32[8,16,512]{2,1,0:T(8,128)S(1)}, u32[]{:S(2)}, u32[]{:S(2)}) async-start(f32[8,16,512]{2,1,0:T(8,128)} %get-tuple-element.28), calls=%async_computation.4 | async-start | bytes 524288 | tf_op jit(solution)/shard_map/all_to_all | solution.py:31
  75.7 5.3 %collective-permute-start.9 = (f32[4,8,512]{2,1,0:T(8,128)S(1)}, f32[4,8,512]{2,1,0:T(8,128)S(1)}, u32[]{:S(2)}, u32[]{:S(2)}) collective-permute-start(f32[4,8,512]{2,1,0:T(8,128)S(1)} %get-tuple-element.42), channel_id=1, source_target_pairs={{0,16},{1,17},{2,18},{3,19},{4,20},{5,21},{6,22},{7,23},{8,24},{9,... | collective-permute-start | bytes 196616 | tf_op jit(solution)/shard_map/ppermute | solution.py:23
  88.9 5.5 %collective-permute-done.6 = f32[64,512]{1,0:T(8,128)S(1)} collective-permute-done((f32[64,512]{1,0:T(8,128)S(1)}, f32[64,512]{1,0:T(8,128)S(1)}, u32[]{:S(2)}, u32[]{:S(2)}) %collective-permute-start.6) | collective-permute-done | bytes 131104 | tf_op jit(solution)/shard_map/ppermute | solution.py:23
  97.0 29.7 %all_to_all.73.parts = f32[128,8,128]{2,1,0:T(8,128)S(1)} all-to-all(f32[128,8,128]{2,1,0:T(8,128)S(1)} %mid_lift.1), channel_id=1, replica_groups={{0,1,2,3,4,5,6,7,8,9,10,11,12,13,14,15,16,17,18,19,20,21,22,23,24,25,26..., dimensions={0} | all-to-all | bytes 1048576 | tf_op jit(solution)/shard_map/all_to_all | solution.py:31
  126.8 18.1 %all_to_all.74.refs_0_ = f32[128,8,128]{2,1,0:T(8,128)S(1)} all-to-all(f32[128,8,128]{2,1,0:T(8,128)S(1)} %mixed.1), channel_id=1, replica_groups={{0,1,2,3,4,5,6,7,8,9,10,11,12,13,14,15,16,17,18,19,20,21,22,23,24,25,26..., dimensions={0} | all-to-all | bytes 1048576 | tf_op jit(solution)/shard_map/all_to_all | solution.py:31
  146.5 9.2 %all_to_all.75.parts = f32[8,8,768]{2,1,0:T(8,128)S(1)} all-to-all(f32[8,8,768]{2,1,0:T(8,128)S(1)} %root.1), channel_id=1, replica_groups={{0,1,2,3,4,5,6,7},{8,9,10,11,12,13,14,15},{16,17,18,19,20,21,22,23},{24..., dimensions={0} | all-to-all | bytes 393216 | tf_op jit(solution)/shard_map/all_to_all | solution.py:31
  156.3 12.7 %all_to_all.76 = f32[16,8,768]{2,1,0:T(8,128)S(1)} all-to-all(f32[16,8,768]{2,1,0:T(8,128)S(1)} %get-tuple-element.33), channel_id=1, replica_groups={{0,8,16,24,32,40,48,56,64,72,80,88,96,104,112,120},{1,9,17,25,33,41,49,..., dimensions={0} | all-to-all | bytes 786432 | tf_op jit(solution)/shard_map/all_to_all | solution.py:31
  169.1 11.3 %all_to_all.77.refs_0_ = f32[8,2,8,768]{3,2,1,0:T(8,128)S(1)} all-to-all(f32[8,2,8,768]{3,2,1,0:T(8,128)S(1)} %bitcast.39), channel_id=1, replica_groups={{0,1,2,3,4,5,6,7},{8,9,10,11,12,13,14,15},{16,17,18,19,20,21,22,23},{24..., dimensions={0} | all-to-all | bytes 786432 | tf_op jit(solution)/shard_map/all_to_all | solution.py:31
  182.2 3.4 %all-to-all-start.10 = ((f32[8,8,512]{2,1,0:T(8,128)}), f32[8,8,512]{2,1,0:T(8,128)S(1)}, u32[]{:S(2)}, u32[]{:S(2)}) async-start(f32[8,8,512]{2,1,0:T(8,128)} %middle.1), calls=%async_computation.10 | async-start | bytes 262144 | tf_op jit(solution)/shard_map/all_to_all | solution.py:31
  185.6 6.0 %all-to-all-done.10.parts = f32[8,8,512]{2,1,0:T(8,128)S(1)} async-done(((f32[8,8,512]{2,1,0:T(8,128)}), f32[8,8,512]{2,1,0:T(8,128)S(1)}, u32[]{:S(2)}, u32[]{:S(2)}) %all-to-all-start.10) | async-done | bytes 131104 | tf_op jit(solution)/shard_map/all_to_all | solution.py:31
  192.3 3.4 %all-to-all-start.11 = ((f32[8,8,512]{2,1,0:T(8,128)}), f32[8,8,512]{2,1,0:T(8,128)S(1)}, u32[]{:S(2)}, u32[]{:S(2)}) async-start(f32[8,8,512]{2,1,0:T(8,128)} %get-tuple-element.36), calls=%async_computation.11 | async-start | bytes 262144 | tf_op jit(solution)/shard_map/all_to_all | solution.py:31
  195.7 6.5 %all-to-all-done.11 = f32[8,8,512]{2,1,0:T(8,128)S(1)} async-done(((f32[8,8,512]{2,1,0:T(8,128)}), f32[8,8,512]{2,1,0:T(8,128)S(1)}, u32[]{:S(2)}, u32[]{:S(2)}) %all-to-all-start.11) | async-done | bytes 131104 | tf_op jit(solution)/shard_map/all_to_all | solution.py:31
  202.9 3.4 %all-to-all-start.12 = ((f32[8,8,1280]{2,1,0:T(8,128)}), f32[8,8,1280]{2,1,0:T(8,128)S(1)}, u32[]{:S(2)}, u32[]{:S(2)}) async-start(f32[8,8,1280]{2,1,0:T(8,128)} %bitcast.21), calls=%async_computation.12 | async-start | bytes 655360 | tf_op jit(solution)/shard_map/all_to_all | solution.py:31
  206.4 2.5 %copy-done.1 = f32[1024,1280]{1,0:T(8,128)S(1)} copy-done((f32[1024,1280]{1,0:T(8,128)S(1)}, f32[1024,1280]{1,0:T(8,128)}, u32[]{:S(2)}) %copy-start.1) | copy-done | bytes 5242904
  211.1 3.5 %all-to-all-done.12.bound = f32[8,8,1280]{2,1,0:T(8,128)S(1)} async-done(((f32[8,8,1280]{2,1,0:T(8,128)}), f32[8,8,1280]{2,1,0:T(8,128)S(1)}, u32[]{:S(2)}, u32[]{:S(2)}) %all-to-all-start.12) | async-done | bytes 327712 | tf_op jit(solution)/shard_map/all_to_all | solution.py:31
  218.0 9.9 %all_to_all.78 = f32[8,8,1024]{2,1,0:T(8,128)S(1)} all-to-all(f32[8,8,1024]{2,1,0:T(8,128)S(1)} %low_solve.1), channel_id=1, replica_groups={{0,1,2,3,4,5,6,7},{8,9,10,11,12,13,14,15},{16,17,18,19,20,21,22,23},{24..., dimensions={0} | all-to-all | bytes 524288 | tf_op jit(solution)/shard_map/all_to_all | solution.py:31
  (84 shorter events, 31.6 us)
Async XLA Ops:
  1.7 1.3 collective-permute-start
  3.2 46.6 %copy-start = (f32[2560,512]{1,0:T(8,128)S(1)}, f32[2560,512]{1,0:T(8,128)}, u32[]{:S(2)}) copy-start(f32[2560,512]{1,0:T(8,128)} %refs_2_.3) | copy-start | bytes 15728644
  3.2 46.6 %copy-start.7 = (f32[8,4608]{1,0:T(8,128)S(1)}, f32[8,4608]{1,0:T(8,128)}, u32[]{:S(2)}) copy-start(f32[8,4608]{1,0:T(8,128)} %refs_1_.5) | copy-start | bytes 442372
  24.2 1.4 collective-permute-start.1
  52.9 22.8 %slice-start.2 = ((f32[8,4608]{1,0:T(8,128)}), f32[8,1536]{1,0:T(8,128)S(1)}, s32[]{:S(2)}) async-start(f32[8,4608]{1,0:T(8,128)} %refs_1_.5), calls=%async_computation.16 | async-start | bytes 98304 | tf_op jit(solution)/shard_map/slice | solution.py:415
  52.9 1.9 collective-permute-start.2
  52.9 22.8 %copy-start.10 = (pred[4]{0:T(512)(128)(4,1)}, pred[4]{0:T(512)(128)(4,1)S(1)}, u32[]{:S(2)}) copy-start(pred[4]{0:T(512)(128)(4,1)S(1)} %iota_compare_fusion) | copy-start | bytes 16
  55.6 27.1 %copy-start.8 = (f32[512,512]{1,0:T(8,128)S(1)}, f32[512,512]{1,0:T(8,128)}, u32[]{:S(2)}) copy-start(f32[512,512]{1,0:T(8,128)} %refs_1_.6) | copy-start | bytes 3145732
  55.7 15.8 %all-to-all-start.3 = ((f32[16,16,512]{2,1,0:T(8,128)}), f32[16,16,512]{2,1,0:T(8,128)S(1)}, u32[]{:S(2)}, u32[]{:S(2)}) async-start(f32[16,16,512]{2,1,0:T(8,128)} %bitcast.7), calls=%async_computation.3 | async-start | bytes 1048576 | tf_op jit(solution)/shard_map/all_to_all | solution.py:31
  59.4 1.9 collective-permute-start.8
  61.3 83.6 %slice-start = ((s8[4718592]{0:T(1024)(128)(4,1)}), s8[524288]{0:T(1024)(128)(4,1)S(1)}, s32[]{:S(2)}) async-start(s8[4718592]{0:T(1024)(128)(4,1)} %bitcast.36), calls=%async_computation.14 | async-start | bytes 1048576
  61.5 14.2 %collective-permute-start.10 = (f32[4,8,1536]{2,1,0:T(8,128)S(1)}, f32[4,8,1536]{2,1,0:T(8,128)S(1)}, u32[]{:S(2)}, u32[]{:S(2)}) collective-permute-start(f32[4,8,1536]{2,1,0:T(8,128)S(1)} %fusion), channel_id=1, source_target_pairs={{0,8},{1,9},{2,10},{3,11},{4,12},{5,13},{6,14},{7,15},{8,16},{9,17... | collective-permute-start | bytes 589832 | tf_op jit(solution)/shard_map/ppermute | solution.py:23
  72.2 10.6 %all-to-all-start.4 = ((f32[8,16,512]{2,1,0:T(8,128)}), f32[8,16,512]{2,1,0:T(8,128)S(1)}, u32[]{:S(2)}, u32[]{:S(2)}) async-start(f32[8,16,512]{2,1,0:T(8,128)} %get-tuple-element.28), calls=%async_computation.4 | async-start | bytes 524288 | tf_op jit(solution)/shard_map/all_to_all | solution.py:31
  75.7 7.6 %collective-permute-start.9 = (f32[4,8,512]{2,1,0:T(8,128)S(1)}, f32[4,8,512]{2,1,0:T(8,128)S(1)}, u32[]{:S(2)}, u32[]{:S(2)}) collective-permute-start(f32[4,8,512]{2,1,0:T(8,128)S(1)} %get-tuple-element.42), channel_id=1, source_target_pairs={{0,16},{1,17},{2,18},{3,19},{4,20},{5,21},{6,22},{7,23},{8,24},{9,... | collective-permute-start | bytes 196616 | tf_op jit(solution)/shard_map/ppermute | solution.py:23
  83.2 1.4 collective-permute-start.3
  84.7 9.6 %collective-permute-start.6 = (f32[64,512]{1,0:T(8,128)S(1)}, f32[64,512]{1,0:T(8,128)S(1)}, u32[]{:S(2)}, u32[]{:S(2)}) collective-permute-start(f32[64,512]{1,0:T(8,128)S(1)} %add.81), channel_id=1, source_target_pairs={{0,6},{1,7},{2,4},{3,5},{4,2},{5,3},{6,0},{7,1},{8,14},{9,15},{10,... | collective-permute-start | bytes 393224 | tf_op jit(solution)/shard_map/ppermute | solution.py:23
  85.7 8.7 %collective-permute-start.5 = (f32[64,512]{1,0:T(8,128)S(1)}, f32[64,512]{1,0:T(8,128)S(1)}, u32[]{:S(2)}, u32[]{:S(2)}) collective-permute-start(f32[64,512]{1,0:T(8,128)S(1)} %add.81), channel_id=1, source_target_pairs={{0,4},{1,5},{2,6},{3,7},{4,0},{5,1},{6,2},{7,3},{8,12},{9,13},{10,... | collective-permute-start | bytes 393224 | tf_op jit(solution)/shard_map/ppermute | solution.py:23
  87.4 7.6 %collective-permute-start.4 = (f32[64,512]{1,0:T(8,128)S(1)}, f32[64,512]{1,0:T(8,128)S(1)}, u32[]{:S(2)}, u32[]{:S(2)}) collective-permute-start(f32[64,512]{1,0:T(8,128)S(1)} %add.81), channel_id=1, source_target_pairs={{0,2},{1,3},{2,0},{3,1},{4,6},{5,7},{6,4},{7,5},{8,10},{9,11},{10,... | collective-permute-start | bytes 393224 | tf_op jit(solution)/shard_map/ppermute | solution.py:23
  95.0 0.8 collective-permute-start.7
  95.7 49.2 %slice-start.1 = ((s8[4718592]{0:T(1024)(128)(4,1)}), s8[4194304]{0:T(1024)(128)(4,1)S(1)}, s32[]{:S(2)}) async-start(s8[4718592]{0:T(1024)(128)(4,1)} %bitcast.36), calls=%async_computation.15 | async-start | bytes 8388608
  144.9 35.5 %copy-start.3 = (f32[512,1536]{1,0:T(8,128)S(1)}, f32[512,1536]{1,0:T(8,128)}, u32[]{:S(2)}) copy-start(f32[512,1536]{1,0:T(8,128)} %refs_2_.5) | copy-start | bytes 9437188
  182.2 9.4 %all-to-all-start.10 = ((f32[8,8,512]{2,1,0:T(8,128)}), f32[8,8,512]{2,1,0:T(8,128)S(1)}, u32[]{:S(2)}, u32[]{:S(2)}) async-start(f32[8,8,512]{2,1,0:T(8,128)} %middle.1), calls=%async_computation.10 | async-start | bytes 262144 | tf_op jit(solution)/shard_map/all_to_all | solution.py:31
  192.3 9.9 %all-to-all-start.11 = ((f32[8,8,512]{2,1,0:T(8,128)}), f32[8,8,512]{2,1,0:T(8,128)S(1)}, u32[]{:S(2)}, u32[]{:S(2)}) async-start(f32[8,8,512]{2,1,0:T(8,128)} %get-tuple-element.36), calls=%async_computation.11 | async-start | bytes 262144 | tf_op jit(solution)/shard_map/all_to_all | solution.py:31
  202.9 11.6 %all-to-all-start.12 = ((f32[8,8,1280]{2,1,0:T(8,128)}), f32[8,8,1280]{2,1,0:T(8,128)S(1)}, u32[]{:S(2)}, u32[]{:S(2)}) async-start(f32[8,8,1280]{2,1,0:T(8,128)} %bitcast.21), calls=%async_computation.12 | async-start | bytes 655360 | tf_op jit(solution)/shard_map/all_to_all | solution.py:31
  (7 other events, 62.1 us)

commit v4 on v3

--- a/solution.py
+++ b/solution.py
@@ -43,12 +43,8 @@
     return exchange(value, lambda x, z, y, c: (x // 2, y, c), lambda x, z, y, c: 4 * x + z)
 
 
-def over_z(value):
-    return exchange(value, lambda x, z, y, c: (x, y, c), lambda x, z, y, c: z)
-
-
-def over_y(value):
-    return exchange(value, lambda x, z, y, c: (x, z, c), lambda x, z, y, c: y)
+def over_low(value):
+    return exchange(value, lambda x, z, y, c: (x // 2, c), lambda x, z, y, c: (x, z, y))
 
 
 def over_zy(value):
@@ -144,13 +140,21 @@
 
 
 def gathered(parts, number):
-    def body(parts, value, every):
-        summed = total([parts[k] for k in range(parts.shape[0])])
+    parts = parts if isinstance(parts, list) else [parts]
+    count = len(parts)
+
+    def body(*refs):
+        value, every = refs[count:]
+        if count == 1:
+            summed = total([refs[0][k] for k in range(refs[0].shape[0])])
+        else:
+            summed = total([ref[...] for ref in refs[:count]])
         value[...] = summed
         for k in range(number):
             every[k] = summed
 
-    shape = parts.shape[1:]
+    shape = parts[0].shape[1:] if count == 1 else parts[0].shape
+    block = pl.BlockSpec(memory_space=pltpu.VMEM)
     return pl.pallas_call(
         body,
         name="gathered",
@@ -158,10 +162,10 @@
             jax.ShapeDtypeStruct(shape, jnp.float32),
             jax.ShapeDtypeStruct((number, *shape), jnp.float32),
         ],
-        in_specs=[pl.BlockSpec(memory_space=pltpu.VMEM)],
-        out_specs=[pl.BlockSpec(memory_space=pltpu.VMEM)] * 2,
-        compiler_params=pltpu.CompilerParams(vmem_limit_bytes=4 << 20),
-    )(parts)
+        in_specs=[block] * count,
+        out_specs=[block] * 2,
+        compiler_params=pltpu.CompilerParams(vmem_limit_bytes=4 << 20),
+    )(*parts)
 
 
 def added(first, second, number=None):
@@ -190,26 +194,43 @@
 
     def store(number, tile, jump, part, keep, give):
         part[:, 512 * number : 512 * (number + 1)] = tile
-        core = place()[3]
-
-        @pl.when(core == number)
-        def _():
-            keep[...] = tile
-
-        @pl.when(core != number)
-        def _():
-            give[...] = tile
+        mine = place()[3] == number
+        keep[...] = jnp.where(mine, tile, keep[...])
+        give[...] = jnp.where(mine, give[...], tile)
 
     shapes = [(64, 1024), (64, 512), (64, 512)]
     return product("low_w", vectors, operator, [jump], shapes, store, 512)
 
 
+def turned(parts):
+    def body(*refs):
+        x, z, y, c = place()
+        for shift in range(4):
+
+            @pl.when(z ^ y == shift)
+            def _():
+                for k in range(4):
+                    refs[4 + k][...] = refs[shift ^ k][...]
+
+    block = pl.BlockSpec(memory_space=pltpu.VMEM)
+    return pl.pallas_call(
+        body,
+        name="turned",
+        out_shape=[jax.ShapeDtypeStruct(parts[0].shape, jnp.float32)] * 4,
+        in_specs=[block] * 4,
+        out_specs=[block] * 4,
+        compiler_params=pltpu.CompilerParams(vmem_limit_bytes=4 << 20),
+    )(*parts)
+
+
 def lift_product(parts, particular, operator):
-    def vectors(parts, particular):
-        return parts[0] + parts[1] + (parts[2] + parts[3])
-
-    def store(number, tile, parts, particular, keep, give, mine, other):
+    def vectors(*refs):
+        return refs[0][...] + refs[1][...] + (refs[2][...] + refs[3][...])
+
+    def store(number, tile, *refs):
+        particular, keep, give, mine, other = refs[4:]
         x, z, y, c = place()
+        sign = jnp.where(x % 2 == 1, 1.0, -1.0)
         if number == 0:
             keep[...] = jnp.zeros(keep.shape, jnp.float32)
             give[...] = jnp.zeros(give.shape, jnp.float32)
@@ -219,11 +240,11 @@
 
                 @pl.when((z == (2 if block < 7 else 3)) & (c == core))
                 def _():
-                    keep[y, v, pl.ds(pl.multiple_of(8 * c, 8), 8)] = particular[:, source : source + 512]
+                    keep[2 * y + c, v] = sign * particular[:, source : source + 512]
 
                 @pl.when((z == (2 if block < 7 else 3)) & (c != core))
                 def _():
-                    give[y, v, pl.ds(pl.multiple_of(8 * c, 8), 8)] = particular[:, source : source + 512]
+                    give[2 * y + c, v] = sign * particular[:, source : source + 512]
 
         here = pl.ds(512 * number, 512)
         block = number + jnp.where(z == 3, 3, -2)
@@ -232,35 +253,25 @@
 
         @pl.when(valid & (block % 2 == c))
         def _():
-            for k in range(4):
-                keep[k, row] += tile[16 * k : 16 * k + 16]
+            for k in range(8):
+                keep[k, row] += sign * tile[8 * k : 8 * k + 8]
 
         @pl.when(valid & (block % 2 != c))
         def _():
-            for k in range(4):
-                give[k, row] += tile[16 * k : 16 * k + 16]
-
-        pairs = tile.reshape(4, 2, 8, 512)
-
-        @pl.when(c == 0)
-        def _():
-            mine[:, :, here] = pairs[:, 0]
-            other[:, :, here] = pairs[:, 1]
-
-        @pl.when(c == 1)
-        def _():
-            mine[:, :, here] = pairs[:, 1]
-            other[:, :, here] = pairs[:, 0]
-
-    shapes = [(4, 4, 16, 512)] * 2 + [(4, 8, 2560)] * 2
+            for k in range(8):
+                give[k, row] += sign * tile[8 * k : 8 * k + 8]
+
+        shared(tile, here, mine, other)
+
+    shapes = [(8, 4, 8, 512)] * 2 + [(4, 8, 2560)] * 2
     return product(
-        "low_lift", vectors, operator, [parts, particular], shapes, store, 512
+        "low_lift", vectors, operator, [*parts, particular], shapes, store, 512
     )
 
 
 def mid_product(parts, operator):
     def vectors(parts):
-        return (parts[4:8] - parts[0:4]).reshape(64, 512)
+        return parts[...].reshape(64, 512)
 
     def store(number, tile, parts, out):
         out[:, 256 * number : 256 * (number + 1)] = tile
@@ -309,6 +320,37 @@
     )(parts)
 
 
+def shared(tile, here, keep, give):
+    first = place()[3] == 0
+    pairs = tile.reshape(4, 2, 8, tile.shape[1])
+    keep[:, :, here] = jnp.where(first, pairs[:, 0], pairs[:, 1])
+    give[:, :, here] = jnp.where(first, pairs[:, 1], pairs[:, 0])
+
+
+def over_columns(keep, give):
+    def body(keep, got, *out):
+        y = place()[2]
+        for mine in range(4):
+
+            @pl.when(y == mine)
+            def _():
+                for k in range(4):
+                    out[k][...] = keep[mine ^ k] + got[mine ^ k]
+
+    block = pl.BlockSpec(memory_space=pltpu.VMEM)
+    parts = pl.pallas_call(
+        body,
+        name="over_columns",
+        out_shape=[jax.ShapeDtypeStruct(keep.shape[1:], jnp.float32)] * 4,
+        in_specs=[block] * 2,
+        out_specs=[block] * 4,
+        compiler_params=pltpu.CompilerParams(vmem_limit_bytes=4 << 20),
+    )(keep, swap_core(give))
+    return [parts[0]] + [
+        send(parts[k], lambda x, z, y, c: (x, z, y ^ k, c)) for k in (1, 2, 3)
+    ]
+
+
 def wide_product(name, parts, operator, added=None):
     height = operator.shape[0]
 
@@ -322,12 +364,12 @@
 
     def store(number, tile, *refs):
         here = slice(256 * number, 256 * (number + 1))
-        if len(refs) == 3:
+        if len(refs) == 4:
             tile = tile + refs[1][:, here]
-        refs[-1][:, :, here] = tile.reshape(8, 8, 256)
+        shared(tile, here, *refs[-2:])
 
     inputs = [parts] if added is None else [parts, added]
-    return product(name, vectors, operator, inputs, [(8, 8, height)], store, 256)[0]
+    return product(name, vectors, operator, inputs, [(4, 8, height)] * 2, store, 256)
 
 
 def split_ahead(operator):
@@ -347,7 +389,7 @@
 
 
 def last_product(bound, over, under, added):
-    def body(bound, added, over, under, out):
+    def body(bound, added, over, under, keep, give):
         high, low = halves(bound[...].reshape(64, 1280))
         both = jnp.concatenate([high, low], 0)
         for number in range(4):
@@ -355,14 +397,14 @@
             first = lax.dot_general(both, over[here, :], ROWS, preferred_element_type=jnp.float32)
             second = lax.dot_general(high, under[here, :], ROWS, preferred_element_type=jnp.float32)
             tile = first[:64] + (first[64:] + second) + added[:, here]
-            out[:, :, here] = tile.reshape(8, 8, 256)
+            shared(tile, here, keep, give)
 
     return pl.pallas_call(
         body,
         name="low_solve",
-        out_shape=jax.ShapeDtypeStruct((8, 8, 1024), jnp.float32),
+        out_shape=[jax.ShapeDtypeStruct((4, 8, 1024), jnp.float32)] * 2,
         in_specs=[pl.BlockSpec(memory_space=pltpu.VMEM)] * 4,
-        out_specs=pl.BlockSpec(memory_space=pltpu.VMEM),
+        out_specs=[pl.BlockSpec(memory_space=pltpu.VMEM)] * 2,
         compiler_params=pltpu.CompilerParams(vmem_limit_bytes=4 << 20),
     )(bound, added, over, under)
 
@@ -380,13 +422,18 @@
     jump_two = over_zy(copies(both, 4).reshape(16, 16, 512))
 
     low_part, keep, give = low_product(jump_two, low_inverse)
-    low_w = over_y(over_z(added(keep, swap_core(give), 4)))
+    half = added(keep, swap_core(give))
+    blocks = [half] + [send(half, lambda x, z, y, c: (x, z ^ k, y, c)) for k in (1, 2, 3)]
+    blocks = list(turned(blocks))
+    low_w = blocks[:1] + [
+        send(blocks[k], lambda x, z, y, c: (x, z, y ^ k, c)) for k in (1, 2, 3)
+    ]
 
     keep, give, mine, other = lift_product(low_w, particular, low_lift)
 
-    blocks = added(keep, swap_core(give)).reshape(16, 16, 512)
+    blocks = added(keep, swap_core(give)).reshape(32, 8, 512)
     blocks, other, apart = lax.optimization_barrier((blocks, other, particular))
-    jump_one = over_half(gathered(over_zy(blocks), 8)[1])
+    jump_one = over_half(gathered(over_low(blocks), 8)[1])
 
     mid_part = mid_product(jump_one, mid_inverse)
     mid_sum = sum_y(mid_part + swap_core(mid_part))
@@ -436,12 +483,12 @@
     root_jump = over_all(mixed(over_all(shares)))
 
     root_part = wide_product("root", root_jump, root_inverse)
-    root_values, root_every = gathered(over_blk(root_part), 16)
+    root_values, root_every = gathered(over_columns(*root_part), 16)
     root_every = over_leaf(root_every)
     root_block = over_blk(root_every.reshape(8, 2, 8, 768))
 
     middle_part = wide_product("middle", root_block, mid_solve, mid_part)
-    middle_values, middle_every = gathered(over_blk(middle_part), 8)
+    middle_values, middle_every = gathered(over_columns(*middle_part), 8)
     middle_every, low_solve = lax.optimization_barrier((middle_every, low_solve))
     middle_every = over_half(middle_every)
     over, under = split_ahead(low_solve)
@@ -455,7 +502,7 @@
         1,
     )
     bound = over_blk(bound.reshape(8, 8, 1280).transpose(1, 0, 2))
-    lower_values = total(list(over_blk(last_product(bound, over, under, low_part))))
+    lower_values = total(over_columns(*last_product(bound, over, under, low_part)))
     return (root_values, middle_values, lower_values)
 
 

time: 230 us -> 224 us (0.974)
  blocking collectives: 135 us -> 92 us
  starting transfers between devices: 31.7 us -> 53.4 us
  waiting for transfers between devices: 37.4 us -> 53.8 us
    all_to_all x9 -> x5, blocking collectives: 135 us -> 92 us  [exchange(): return lax.all_to_all(value, AXES, 0, 0, axis_index_groups=members)]
    ppermute x11 -> x29, starting transfers between devices: 14.4 us -> 38 us  [send(): return lax.ppermute(value, AXES, pairs)]
    ppermute x11 -> x29, waiting for transfers between devices: 13.5 us -> 36.5 us  [send(): return lax.ppermute(value, AXES, pairs)]
    all_to_all x5 -> x4, waiting for transfers between devices: 23.9 us -> 17.4 us  [exchange(): return lax.all_to_all(value, AXES, 0, 0, axis_index_groups=members)]
    all_to_all x5 -> x4, starting transfers between devices: 17.3 us -> 15.4 us  [exchange(): return lax.all_to_all(value, AXES, 0, 0, axis_index_groups=members)]
    unnamed x28 -> x22, local copies, waits for them, and re-layouts: 6.49 us -> 7.31 us
  transfers between devices with their start and end apart: 16 -> 33, of which waited for: 12 -> 26; matrix products, arithmetic and copies ran while one was open for 0% -> 0% of each run, Pallas kernels for 1% -> 1%
where the time goes in v4:
time: 224 us
  blocking collectives  92 us (41%)
  waiting for transfers between devices  53.8 us (24%)
  starting transfers between devices  53.4 us (24%)
  Pallas kernels  12.9 us (6%)
  local copies, waits for them, and re-layouts  8.4 us (4%)
    all_to_all x5, blocking collectives, exchange(): return lax.all_to_all(value, AXES, 0, 0, axis_index_groups=members)  92 us
    ppermute x29, starting transfers between devices, send(): return lax.ppermute(value, AXES, pairs)  38 us
    ppermute x29, waiting for transfers between devices, send(): return lax.ppermute(value, AXES, pairs)  36.5 us
    all_to_all x4, waiting for transfers between devices, exchange(): return lax.all_to_all(value, AXES, 0, 0, axis_index_groups=members)  17.4 us
    all_to_all x4, starting transfers between devices, exchange(): return lax.all_to_all(value, AXES, 0, 0, axis_index_groups=members)  15.4 us
    pallas_call x6, Pallas kernels, product(): pl.pallas_call(body, name=name, out_shape=[jax.ShapeDtypeStruct(shape, jn...  7.43 us
    unnamed x22, local copies, waits for them, and re-layouts  7.31 us
  transfers between devices with their start and end apart: 33, of which 26 were waited for; matrix products, arithmetic and copies ran while one was open for 0% of the time, Pallas kernels for 1%

profile of v4, /device:TPU:0, one launch (start us, length us, event | category | flops | bytes accessed | tf_op | source)
XLA Modules:
  0.0 223.6 jit_solution(1314765324396493868)
XLA Ops:
  3.1 19.9 %all_to_all.45.refs_0_ = f32[16,16,512]{2,1,0:T(8,128)S(1)} all-to-all(f32[16,16,512]{2,1,0:T(8,128)S(1)} %bitcast.39), channel_id=1, replica_groups={{0,2,4,6,8,10,12,14,16,18,20,22,24,26,28,30},{1,3,5,7,9,11,13,15,17,19,..., dimensions={0} | all-to-all | bytes 1048576 | tf_op jit(solution)/shard_map/all_to_all | solution.py:31
  28.3 2.7 %collective-permute-start.2 = (f32[64,512]{1,0:T(8,128)S(1)}, f32[64,512]{1,0:T(8,128)S(1)}, u32[]{:S(2)}, u32[]{:S(2)}) collective-permute-start(f32[64,512]{1,0:T(8,128)S(1)} %added.2.refs_0_), channel_id=1, source_target_pairs={{0,8},{1,9},{2,10},{3,11},{4,12},{5,13},{6,14},{7,15},{8,0},{9,1},... | collective-permute-start | bytes 393224 | tf_op jit(solution)/shard_map/ppermute | solution.py:23
  31.0 5.5 %collective-permute-done.4.refs_3_ = f32[64,512]{1,0:T(8,128)S(1)} collective-permute-done((f32[64,512]{1,0:T(8,128)S(1)}, f32[64,512]{1,0:T(8,128)S(1)}, u32[]{:S(2)}, u32[]{:S(2)}) %collective-permute-start.4) | collective-permute-done | bytes 131104 | tf_op jit(solution)/shard_map/ppermute | solution.py:23
  39.2 2.7 %collective-permute-start.7 = (f32[64,512]{1,0:T(8,128)S(1)}, f32[64,512]{1,0:T(8,128)S(1)}, u32[]{:S(2)}, u32[]{:S(2)}) collective-permute-start(f32[64,512]{1,0:T(8,128)S(1)} %get-tuple-element.49), channel_id=1, source_target_pairs={{0,6},{1,7},{2,4},{3,5},{4,2},{5,3},{6,0},{7,1},{8,14},{9,15},{10,... | collective-permute-start | bytes 393224 | tf_op jit(solution)/shard_map/ppermute | solution.py:23
  46.7 2.3 %low_lift.1 = (f32[8,4,8,512]{3,2,1,0:T(8,128)S(1)}, f32[8,4,8,512]{3,2,1,0:T(8,128)S(1)}, f32[4,8,2560]{2,1,0:T(8,128)S(1)}, f32[4,8,2560]{2,1,0:T(8,128)S(1)}) custom-call(f32[64,512]{1,0:T(8,128)S(1)} %get-tuple-element.46.refs_0_, f32[64,512]{1,0:T(8,128)S(1)} %collective-permute-done.5.refs_1_, f32[64,512]{1,0:T(8,128)S(1)} %collective-permute-done.6.refs_2_, ...), custom_call_target="tpu_custom_call" | custom-call | flops 503316480 | bytes 5242880 | tf_op jit(solution)/shard_map/low_lift/pallas_call | solution.py:123
  51.9 5.2 %all-to-all-start.1 = ((f32[32,8,512]{2,1,0:T(8,128)}), f32[32,8,512]{2,1,0:T(8,128)S(1)}, u32[]{:S(2)}, u32[]{:S(2)}) async-start(f32[32,8,512]{2,1,0:T(8,128)} %bitcast.7), calls=%async_computation.1 | async-start | bytes 1048576 | tf_op jit(solution)/shard_map/all_to_all | solution.py:31
  59.0 3.7 %collective-permute-start.16 = (f32[4,8,1536]{2,1,0:T(8,128)S(1)}, f32[4,8,1536]{2,1,0:T(8,128)S(1)}, u32[]{:S(2)}, u32[]{:S(2)}) collective-permute-start(f32[4,8,1536]{2,1,0:T(8,128)S(1)} %fusion), channel_id=1, source_target_pairs={{0,8},{1,9},{2,10},{3,11},{4,12},{5,13},{6,14},{7,15},{8,16},{9,17... | collective-permute-start | bytes 589832 | tf_op jit(solution)/shard_map/ppermute | solution.py:23
  62.7 6.3 %all-to-all-done.1.refs_0_ = f32[32,8,512]{2,1,0:T(8,128)S(1)} async-done(((f32[32,8,512]{2,1,0:T(8,128)}), f32[32,8,512]{2,1,0:T(8,128)S(1)}, u32[]{:S(2)}, u32[]{:S(2)}) %all-to-all-start.1) | async-done | bytes 524320 | tf_op jit(solution)/shard_map/all_to_all | solution.py:31
  69.7 3.4 %all-to-all-start.2 = ((f32[8,8,512]{2,1,0:T(8,128)}), f32[8,8,512]{2,1,0:T(8,128)S(1)}, u32[]{:S(2)}, u32[]{:S(2)}) async-start(f32[8,8,512]{2,1,0:T(8,128)} %get-tuple-element.54), calls=%async_computation.2 | async-start | bytes 262144 | tf_op jit(solution)/shard_map/all_to_all | solution.py:31
  73.2 5.3 %collective-permute-start.15 = (f32[4,8,512]{2,1,0:T(8,128)S(1)}, f32[4,8,512]{2,1,0:T(8,128)S(1)}, u32[]{:S(2)}, u32[]{:S(2)}) collective-permute-start(f32[4,8,512]{2,1,0:T(8,128)S(1)} %get-tuple-element.86), channel_id=1, source_target_pairs={{0,16},{1,17},{2,18},{3,19},{4,20},{5,21},{6,22},{7,23},{8,24},{9,... | collective-permute-start | bytes 196616 | tf_op jit(solution)/shard_map/ppermute | solution.py:23
  85.7 5.5 %collective-permute-done.12 = f32[64,512]{1,0:T(8,128)S(1)} collective-permute-done((f32[64,512]{1,0:T(8,128)S(1)}, f32[64,512]{1,0:T(8,128)S(1)}, u32[]{:S(2)}, u32[]{:S(2)}) %collective-permute-start.12) | collective-permute-done | bytes 131104 | tf_op jit(solution)/shard_map/ppermute | solution.py:23
  93.8 29.6 %all_to_all.46.parts = f32[128,8,128]{2,1,0:T(8,128)S(1)} all-to-all(f32[128,8,128]{2,1,0:T(8,128)S(1)} %mid_lift.1), channel_id=1, replica_groups={{0,1,2,3,4,5,6,7,8,9,10,11,12,13,14,15,16,17,18,19,20,21,22,23,24,25,26..., dimensions={0} | all-to-all | bytes 1048576 | tf_op jit(solution)/shard_map/all_to_all | solution.py:31
  123.5 18.1 %all_to_all.47.refs_0_ = f32[128,8,128]{2,1,0:T(8,128)S(1)} all-to-all(f32[128,8,128]{2,1,0:T(8,128)S(1)} %mixed.1), channel_id=1, replica_groups={{0,1,2,3,4,5,6,7,8,9,10,11,12,13,14,15,16,17,18,19,20,21,22,23,24,25,26..., dimensions={0} | all-to-all | bytes 1048576 | tf_op jit(solution)/shard_map/all_to_all | solution.py:31
  147.0 2.5 %collective-permute-start.20 = (f32[8,768]{1,0:T(8,128)S(1)}, f32[8,768]{1,0:T(8,128)S(1)}, u32[]{:S(2)}, u32[]{:S(2)}) collective-permute-start(f32[8,768]{1,0:T(8,128)S(1)} %get-tuple-element.63), channel_id=1, source_target_pairs={{0,6},{1,7},{2,4},{3,5},{4,2},{5,3},{6,0},{7,1},{8,14},{9,15},{10,... | collective-permute-start | bytes 73736 | tf_op jit(solution)/shard_map/ppermute | solution.py:23
  152.7 12.8 %all_to_all.48 = f32[16,8,768]{2,1,0:T(8,128)S(1)} all-to-all(f32[16,8,768]{2,1,0:T(8,128)S(1)} %get-tuple-element.65), channel_id=1, replica_groups={{0,8,16,24,32,40,48,56,64,72,80,88,96,104,112,120},{1,9,17,25,33,41,49,..., dimensions={0} | all-to-all | bytes 786432 | tf_op jit(solution)/shard_map/all_to_all | solution.py:31
  165.5 11.7 %all_to_all.49.refs_0_ = f32[8,2,8,768]{3,2,1,0:T(8,128)S(1)} all-to-all(f32[8,2,8,768]{3,2,1,0:T(8,128)S(1)} %bitcast.37), channel_id=1, replica_groups={{0,1,2,3,4,5,6,7},{8,9,10,11,12,13,14,15},{16,17,18,19,20,21,22,23},{24..., dimensions={0} | all-to-all | bytes 786432 | tf_op jit(solution)/shard_map/all_to_all | solution.py:31
  182.3 2.1 collective-permute-start.24
  187.9 3.4 %all-to-all-start.7 = ((f32[8,8,512]{2,1,0:T(8,128)}), f32[8,8,512]{2,1,0:T(8,128)S(1)}, u32[]{:S(2)}, u32[]{:S(2)}) async-start(f32[8,8,512]{2,1,0:T(8,128)} %get-tuple-element.74), calls=%async_computation.7 | async-start | bytes 262144 | tf_op jit(solution)/shard_map/all_to_all | solution.py:31
  191.3 6.5 %all-to-all-done.7 = f32[8,8,512]{2,1,0:T(8,128)S(1)} async-done(((f32[8,8,512]{2,1,0:T(8,128)}), f32[8,8,512]{2,1,0:T(8,128)S(1)}, u32[]{:S(2)}, u32[]{:S(2)}) %all-to-all-start.7) | async-done | bytes 131104 | tf_op jit(solution)/shard_map/all_to_all | solution.py:31
  198.6 3.4 %all-to-all-start.8 = ((f32[8,8,1280]{2,1,0:T(8,128)}), f32[8,8,1280]{2,1,0:T(8,128)S(1)}, u32[]{:S(2)}, u32[]{:S(2)}) async-start(f32[8,8,1280]{2,1,0:T(8,128)} %bitcast.21), calls=%async_computation.8 | async-start | bytes 655360 | tf_op jit(solution)/shard_map/all_to_all | solution.py:31
  202.0 2.5 %copy-done.1 = f32[1024,1280]{1,0:T(8,128)S(1)} copy-done((f32[1024,1280]{1,0:T(8,128)S(1)}, f32[1024,1280]{1,0:T(8,128)}, u32[]{:S(2)}) %copy-start.1) | copy-done | bytes 5242904
  206.7 3.5 %all-to-all-done.8.bound = f32[8,8,1280]{2,1,0:T(8,128)S(1)} async-done(((f32[8,8,1280]{2,1,0:T(8,128)}), f32[8,8,1280]{2,1,0:T(8,128)S(1)}, u32[]{:S(2)}, u32[]{:S(2)}) %all-to-all-start.8) | async-done | bytes 327712 | tf_op jit(solution)/shard_map/all_to_all | solution.py:31
  215.8 2.1 collective-permute-start.27
  217.8 2.1 collective-permute-start.28
  (112 shorter events, 59.8 us)
Async XLA Ops:
  26.8 9.6 %collective-permute-start.4 = (f32[64,512]{1,0:T(8,128)S(1)}, f32[64,512]{1,0:T(8,128)S(1)}, u32[]{:S(2)}, u32[]{:S(2)}) collective-permute-start(f32[64,512]{1,0:T(8,128)S(1)} %added.2.refs_0_), channel_id=1, source_target_pairs={{0,24},{1,25},{2,26},{3,27},{4,28},{5,29},{6,30},{7,31},{8,16},{9,... | collective-permute-start | bytes 393224 | tf_op jit(solution)/shard_map/ppermute | solution.py:23
  27.8 8.7 %collective-permute-start.3 = (f32[64,512]{1,0:T(8,128)S(1)}, f32[64,512]{1,0:T(8,128)S(1)}, u32[]{:S(2)}, u32[]{:S(2)}) collective-permute-start(f32[64,512]{1,0:T(8,128)S(1)} %added.2.refs_0_), channel_id=1, source_target_pairs={{0,16},{1,17},{2,18},{3,19},{4,20},{5,21},{6,22},{7,23},{8,24},{9,... | collective-permute-start | bytes 393224 | tf_op jit(solution)/shard_map/ppermute | solution.py:23
  28.3 8.8 %collective-permute-start.2 = (f32[64,512]{1,0:T(8,128)S(1)}, f32[64,512]{1,0:T(8,128)S(1)}, u32[]{:S(2)}, u32[]{:S(2)}) collective-permute-start(f32[64,512]{1,0:T(8,128)S(1)} %added.2.refs_0_), channel_id=1, source_target_pairs={{0,8},{1,9},{2,10},{3,11},{4,12},{5,13},{6,14},{7,15},{8,0},{9,1},... | collective-permute-start | bytes 393224 | tf_op jit(solution)/shard_map/ppermute | solution.py:23
  37.2 5.9 %collective-permute-start.5 = (f32[64,512]{1,0:T(8,128)S(1)}, f32[64,512]{1,0:T(8,128)S(1)}, u32[]{:S(2)}, u32[]{:S(2)}) collective-permute-start(f32[64,512]{1,0:T(8,128)S(1)} %get-tuple-element.47), channel_id=1, source_target_pairs={{0,2},{1,3},{2,0},{3,1},{4,6},{5,7},{6,4},{7,5},{8,10},{9,11},{10,... | collective-permute-start | bytes 393224 | tf_op jit(solution)/shard_map/ppermute | solution.py:23
  37.8 7.2 %collective-permute-start.6 = (f32[64,512]{1,0:T(8,128)S(1)}, f32[64,512]{1,0:T(8,128)S(1)}, u32[]{:S(2)}, u32[]{:S(2)}) collective-permute-start(f32[64,512]{1,0:T(8,128)S(1)} %get-tuple-element.48), channel_id=1, source_target_pairs={{0,4},{1,5},{2,6},{3,7},{4,0},{5,1},{6,2},{7,3},{8,12},{9,13},{10,... | collective-permute-start | bytes 393224 | tf_op jit(solution)/shard_map/ppermute | solution.py:23
  39.2 7.5 %collective-permute-start.7 = (f32[64,512]{1,0:T(8,128)S(1)}, f32[64,512]{1,0:T(8,128)S(1)}, u32[]{:S(2)}, u32[]{:S(2)}) collective-permute-start(f32[64,512]{1,0:T(8,128)S(1)} %get-tuple-element.49), channel_id=1, source_target_pairs={{0,6},{1,7},{2,4},{3,5},{4,2},{5,3},{6,0},{7,1},{8,14},{9,15},{10,... | collective-permute-start | bytes 393224 | tf_op jit(solution)/shard_map/ppermute | solution.py:23
  51.9 17.2 %all-to-all-start.1 = ((f32[32,8,512]{2,1,0:T(8,128)}), f32[32,8,512]{2,1,0:T(8,128)S(1)}, u32[]{:S(2)}, u32[]{:S(2)}) async-start(f32[32,8,512]{2,1,0:T(8,128)} %bitcast.7), calls=%async_computation.1 | async-start | bytes 1048576 | tf_op jit(solution)/shard_map/all_to_all | solution.py:31
  59.0 14.1 %collective-permute-start.16 = (f32[4,8,1536]{2,1,0:T(8,128)S(1)}, f32[4,8,1536]{2,1,0:T(8,128)S(1)}, u32[]{:S(2)}, u32[]{:S(2)}) collective-permute-start(f32[4,8,1536]{2,1,0:T(8,128)S(1)} %fusion), channel_id=1, source_target_pairs={{0,8},{1,9},{2,10},{3,11},{4,12},{5,13},{6,14},{7,15},{8,16},{9,17... | collective-permute-start | bytes 589832 | tf_op jit(solution)/shard_map/ppermute | solution.py:23
  69.7 9.9 %all-to-all-start.2 = ((f32[8,8,512]{2,1,0:T(8,128)}), f32[8,8,512]{2,1,0:T(8,128)S(1)}, u32[]{:S(2)}, u32[]{:S(2)}) async-start(f32[8,8,512]{2,1,0:T(8,128)} %get-tuple-element.54), calls=%async_computation.2 | async-start | bytes 262144 | tf_op jit(solution)/shard_map/all_to_all | solution.py:31
  73.2 7.2 %collective-permute-start.15 = (f32[4,8,512]{2,1,0:T(8,128)S(1)}, f32[4,8,512]{2,1,0:T(8,128)S(1)}, u32[]{:S(2)}, u32[]{:S(2)}) collective-permute-start(f32[4,8,512]{2,1,0:T(8,128)S(1)} %get-tuple-element.86), channel_id=1, source_target_pairs={{0,16},{1,17},{2,18},{3,19},{4,20},{5,21},{6,22},{7,23},{8,24},{9,... | collective-permute-start | bytes 196616 | tf_op jit(solution)/shard_map/ppermute | solution.py:23
  81.5 9.6 %collective-permute-start.12 = (f32[64,512]{1,0:T(8,128)S(1)}, f32[64,512]{1,0:T(8,128)S(1)}, u32[]{:S(2)}, u32[]{:S(2)}) collective-permute-start(f32[64,512]{1,0:T(8,128)S(1)} %add.63), channel_id=1, source_target_pairs={{0,6},{1,7},{2,4},{3,5},{4,2},{5,3},{6,0},{7,1},{8,14},{9,15},{10,... | collective-permute-start | bytes 393224 | tf_op jit(solution)/shard_map/ppermute | solution.py:23
  82.9 8.3 %collective-permute-start.11 = (f32[64,512]{1,0:T(8,128)S(1)}, f32[64,512]{1,0:T(8,128)S(1)}, u32[]{:S(2)}, u32[]{:S(2)}) collective-permute-start(f32[64,512]{1,0:T(8,128)S(1)} %add.63), channel_id=1, source_target_pairs={{0,4},{1,5},{2,6},{3,7},{4,0},{5,1},{6,2},{7,3},{8,12},{9,13},{10,... | collective-permute-start | bytes 393224 | tf_op jit(solution)/shard_map/ppermute | solution.py:23
  84.2 7.6 %collective-permute-start.10 = (f32[64,512]{1,0:T(8,128)S(1)}, f32[64,512]{1,0:T(8,128)S(1)}, u32[]{:S(2)}, u32[]{:S(2)}) collective-permute-start(f32[64,512]{1,0:T(8,128)S(1)} %add.63), channel_id=1, source_target_pairs={{0,2},{1,3},{2,0},{3,1},{4,6},{5,7},{6,4},{7,5},{8,10},{9,11},{10,... | collective-permute-start | bytes 393224 | tf_op jit(solution)/shard_map/ppermute | solution.py:23
  144.8 4.8 %collective-permute-start.18 = (f32[8,768]{1,0:T(8,128)S(1)}, f32[8,768]{1,0:T(8,128)S(1)}, u32[]{:S(2)}, u32[]{:S(2)}) collective-permute-start(f32[8,768]{1,0:T(8,128)S(1)} %get-tuple-element.61), channel_id=1, source_target_pairs={{0,2},{1,3},{2,0},{3,1},{4,6},{5,7},{6,4},{7,5},{8,10},{9,11},{10,... | collective-permute-start | bytes 73736 | tf_op jit(solution)/shard_map/ppermute | solution.py:23
  145.2 5.3 %collective-permute-start.19 = (f32[8,768]{1,0:T(8,128)S(1)}, f32[8,768]{1,0:T(8,128)S(1)}, u32[]{:S(2)}, u32[]{:S(2)}) collective-permute-start(f32[8,768]{1,0:T(8,128)S(1)} %get-tuple-element.62), channel_id=1, source_target_pairs={{0,4},{1,5},{2,6},{3,7},{4,0},{5,1},{6,2},{7,3},{8,12},{9,13},{10,... | collective-permute-start | bytes 73736 | tf_op jit(solution)/shard_map/ppermute | solution.py:23
  147.0 5.0 %collective-permute-start.20 = (f32[8,768]{1,0:T(8,128)S(1)}, f32[8,768]{1,0:T(8,128)S(1)}, u32[]{:S(2)}, u32[]{:S(2)}) collective-permute-start(f32[8,768]{1,0:T(8,128)S(1)} %get-tuple-element.63), channel_id=1, source_target_pairs={{0,6},{1,7},{2,4},{3,5},{4,2},{5,3},{6,0},{7,1},{8,14},{9,15},{10,... | collective-permute-start | bytes 73736 | tf_op jit(solution)/shard_map/ppermute | solution.py:23
  179.6 4.8 %collective-permute-start.22 = (f32[8,512]{1,0:T(8,128)S(1)}, f32[8,512]{1,0:T(8,128)S(1)}, u32[]{:S(2)}, u32[]{:S(2)}) collective-permute-start(f32[8,512]{1,0:T(8,128)S(1)} %get-tuple-element.69), channel_id=1, source_target_pairs={{0,2},{1,3},{2,0},{3,1},{4,6},{5,7},{6,4},{7,5},{8,10},{9,11},{10,... | collective-permute-start | bytes 49160 | tf_op jit(solution)/shard_map/ppermute | solution.py:23
  180.3 5.2 %collective-permute-start.23 = (f32[8,512]{1,0:T(8,128)S(1)}, f32[8,512]{1,0:T(8,128)S(1)}, u32[]{:S(2)}, u32[]{:S(2)}) collective-permute-start(f32[8,512]{1,0:T(8,128)S(1)} %get-tuple-element.70), channel_id=1, source_target_pairs={{0,4},{1,5},{2,6},{3,7},{4,0},{5,1},{6,2},{7,3},{8,12},{9,13},{10,... | collective-permute-start | bytes 49160 | tf_op jit(solution)/shard_map/ppermute | solution.py:23
  182.3 4.9 %collective-permute-start.24 = (f32[8,512]{1,0:T(8,128)S(1)}, f32[8,512]{1,0:T(8,128)S(1)}, u32[]{:S(2)}, u32[]{:S(2)}) collective-permute-start(f32[8,512]{1,0:T(8,128)S(1)} %get-tuple-element.71), channel_id=1, source_target_pairs={{0,6},{1,7},{2,4},{3,5},{4,2},{5,3},{6,0},{7,1},{8,14},{9,15},{10,... | collective-permute-start | bytes 49160 | tf_op jit(solution)/shard_map/ppermute | solution.py:23
  187.9 9.9 %all-to-all-start.7 = ((f32[8,8,512]{2,1,0:T(8,128)}), f32[8,8,512]{2,1,0:T(8,128)S(1)}, u32[]{:S(2)}, u32[]{:S(2)}) async-start(f32[8,8,512]{2,1,0:T(8,128)} %get-tuple-element.74), calls=%async_computation.7 | async-start | bytes 262144 | tf_op jit(solution)/shard_map/all_to_all | solution.py:31
  198.6 11.6 %all-to-all-start.8 = ((f32[8,8,1280]{2,1,0:T(8,128)}), f32[8,8,1280]{2,1,0:T(8,128)S(1)}, u32[]{:S(2)}, u32[]{:S(2)}) async-start(f32[8,8,1280]{2,1,0:T(8,128)} %bitcast.21), calls=%async_computation.8 | async-start | bytes 655360 | tf_op jit(solution)/shard_map/all_to_all | solution.py:31
  215.1 4.8 %collective-permute-start.26 = (f32[8,1024]{1,0:T(8,128)S(1)}, f32[8,1024]{1,0:T(8,128)S(1)}, u32[]{:S(2)}, u32[]{:S(2)}) collective-permute-start(f32[8,1024]{1,0:T(8,128)S(1)} %get-tuple-element.82), channel_id=1, source_target_pairs={{0,2},{1,3},{2,0},{3,1},{4,6},{5,7},{6,4},{7,5},{8,10},{9,11},{10,... | collective-permute-start | bytes 98312 | tf_op jit(solution)/shard_map/ppermute | solution.py:23
  215.8 5.4 %collective-permute-start.27 = (f32[8,1024]{1,0:T(8,128)S(1)}, f32[8,1024]{1,0:T(8,128)S(1)}, u32[]{:S(2)}, u32[]{:S(2)}) collective-permute-start(f32[8,1024]{1,0:T(8,128)S(1)} %get-tuple-element.83), channel_id=1, source_target_pairs={{0,4},{1,5},{2,6},{3,7},{4,0},{5,1},{6,2},{7,3},{8,12},{9,13},{10,... | collective-permute-start | bytes 98312 | tf_op jit(solution)/shard_map/ppermute | solution.py:23
  217.8 5.1 %collective-permute-start.28 = (f32[8,1024]{1,0:T(8,128)S(1)}, f32[8,1024]{1,0:T(8,128)S(1)}, u32[]{:S(2)}, u32[]{:S(2)}) collective-permute-start(f32[8,1024]{1,0:T(8,128)S(1)} %get-tuple-element.84), channel_id=1, source_target_pairs={{0,6},{1,7},{2,4},{3,5},{4,2},{5,3},{6,0},{7,1},{8,14},{9,15},{10,... | collective-permute-start | bytes 98312 | tf_op jit(solution)/shard_map/ppermute | solution.py:23
  (21 other events, 344.4 us)

commit v5 on v4

--- a/solution.py
+++ b/solution.py
@@ -351,25 +351,113 @@
     ]
 
 
-def wide_product(name, parts, operator, added=None):
-    height = operator.shape[0]
-
-    def vectors(parts, *added):
-        if parts.shape[0] == 128:
-            lines = [
-                jnp.concatenate([parts[12 * k + n] for n in range(12)], 1) for k in range(8)
-            ]
-            return jnp.concatenate(lines, 0)
-        return jnp.concatenate([parts[:, 0].reshape(64, 768), parts[:, 1].reshape(64, 768)], 1)
+def to_columns(keep, give):
+    def body(keep, got, *out):
+        x, z, y, c = place()
+        for mine in range(4):
+
+            @pl.when(y == mine)
+            def _():
+                for k in range(4):
+                    own, other = keep[mine ^ k], got[mine ^ k]
+                    out[k][0:8] = jnp.where(c == 0, own, other)
+                    out[k][8:16] = jnp.where(c == 0, other, own)
+
+    block = pl.BlockSpec(memory_space=pltpu.VMEM)
+    parts = pl.pallas_call(
+        body,
+        name="to_columns",
+        out_shape=[jax.ShapeDtypeStruct((16, keep.shape[2]), jnp.float32)] * 4,
+        in_specs=[block] * 2,
+        out_specs=[block] * 4,
+        compiler_params=pltpu.CompilerParams(vmem_limit_bytes=4 << 20),
+    )(keep, swap_core(give))
+    return [parts[0]] + [
+        send(parts[k], lambda x, z, y, c: (x, z, y ^ k, c)) for k in (1, 2, 3)
+    ]
+
+
+def in_order(parts):
+    y = place()[2]
+    parts = [part[...] for part in parts]
+    return jnp.concatenate([pick(parts, y ^ v) for v in range(4)], 0)
+
+
+def root_columns(every):
+    def body(every, keep, give):
+        first = place()[3] == 0
+        for v in range(4):
+            for half in range(2):
+                here = slice(768 * half, 768 * (half + 1))
+                own, other = every[4 * v + half], every[4 * v + 2 + half]
+                keep[v, :, here] = jnp.where(first, own, other)
+                give[v, :, here] = jnp.where(first, other, own)
+
+    block = pl.BlockSpec(memory_space=pltpu.VMEM)
+    return to_columns(
+        *pl.pallas_call(
+            body,
+            name="root_columns",
+            out_shape=[jax.ShapeDtypeStruct((4, 8, 1536), jnp.float32)] * 2,
+            in_specs=[block],
+            out_specs=[block] * 2,
+            compiler_params=pltpu.CompilerParams(vmem_limit_bytes=4 << 20),
+        )(every)
+    )
+
+
+def bound_columns(root, middle):
+    def body(root, middle, keep, give):
+        x, z, y, c = place()
+
+        def piece(number):
+            here = slice(128 * (number % 6), 128 * (number % 6 + 1))
+            if number < 48:
+                return jnp.where(x % 2 == 1, root[8 + number // 6, :, here], root[number // 6, :, here])
+            number -= 48
+            return middle[number // 4, :, 128 * (number % 4) : 128 * (number % 4 + 1)]
+
+        for v in range(4):
+            for k in range(10):
+                here = slice(128 * k, 128 * (k + 1))
+                own, other = piece(20 * v + k), piece(20 * v + 10 + k)
+                keep[v, :, here] = jnp.where(c == 0, own, other)
+                give[v, :, here] = jnp.where(c == 0, other, own)
+
+    block = pl.BlockSpec(memory_space=pltpu.VMEM)
+    return to_columns(
+        *pl.pallas_call(
+            body,
+            name="bound_columns",
+            out_shape=[jax.ShapeDtypeStruct((4, 8, 1280), jnp.float32)] * 2,
+            in_specs=[block] * 2,
+            out_specs=[block] * 2,
+            compiler_params=pltpu.CompilerParams(vmem_limit_bytes=4 << 20),
+        )(root, middle)
+    )
+
+
+def root_product(parts, operator):
+    def vectors(parts):
+        lines = [jnp.concatenate([parts[12 * k + n] for n in range(12)], 1) for k in range(8)]
+        return jnp.concatenate(lines, 0)
+
+    def store(number, tile, parts, keep, give):
+        shared(tile, slice(256 * number, 256 * (number + 1)), keep, give)
+
+    return product("root", vectors, operator, [parts], [(4, 8, 768)] * 2, store, 256)
+
+
+def middle_product(parts, operator, added):
+    def vectors(*refs):
+        return in_order(refs[:4])
 
     def store(number, tile, *refs):
         here = slice(256 * number, 256 * (number + 1))
-        if len(refs) == 4:
-            tile = tile + refs[1][:, here]
-        shared(tile, here, *refs[-2:])
-
-    inputs = [parts] if added is None else [parts, added]
-    return product(name, vectors, operator, inputs, [(4, 8, height)] * 2, store, 256)
+        shared(tile + refs[4][:, here], here, *refs[-2:])
+
+    shapes = [(4, 8, 512)] * 2
+    return product("middle", vectors, operator, [*parts, added], shapes, store, 256)
 
 
 def split_ahead(operator):
@@ -389,8 +477,9 @@
 
 
 def last_product(bound, over, under, added):
-    def body(bound, added, over, under, keep, give):
-        high, low = halves(bound[...].reshape(64, 1280))
+    def body(*refs):
+        added, over, under, keep, give = refs[4:]
+        high, low = halves(in_order(refs[:4]))
         both = jnp.concatenate([high, low], 0)
         for number in range(4):
             here = slice(256 * number, 256 * (number + 1))
@@ -403,10 +492,10 @@
         body,
         name="low_solve",
         out_shape=[jax.ShapeDtypeStruct((4, 8, 1024), jnp.float32)] * 2,
-        in_specs=[pl.BlockSpec(memory_space=pltpu.VMEM)] * 4,
+        in_specs=[pl.BlockSpec(memory_space=pltpu.VMEM)] * 7,
         out_specs=[pl.BlockSpec(memory_space=pltpu.VMEM)] * 2,
         compiler_params=pltpu.CompilerParams(vmem_limit_bytes=4 << 20),
-    )(bound, added, over, under)
+    )(*bound, added, over, under)
 
 
 def local(
@@ -482,26 +571,18 @@
     shares = mid_lift_product(mid_w, outer_one, mid_lift)
     root_jump = over_all(mixed(over_all(shares)))
 
-    root_part = wide_product("root", root_jump, root_inverse)
+    root_part = root_product(root_jump, root_inverse)
     root_values, root_every = gathered(over_columns(*root_part), 16)
     root_every = over_leaf(root_every)
-    root_block = over_blk(root_every.reshape(8, 2, 8, 768))
-
-    middle_part = wide_product("middle", root_block, mid_solve, mid_part)
+    root_block = root_columns(root_every)
+
+    middle_part = middle_product(root_block, mid_solve, mid_part)
     middle_values, middle_every = gathered(over_columns(*middle_part), 8)
     middle_every, low_solve = lax.optimization_barrier((middle_every, low_solve))
     middle_every = over_half(middle_every)
     over, under = split_ahead(low_solve)
 
-    root_half = lax.dynamic_slice_in_dim(root_every.reshape(2, 8, 8, 768), xl, 1, 0)[0]
-    bound = jnp.concatenate(
-        [
-            root_half.transpose(1, 0, 2).reshape(8, 6144),
-            middle_every.transpose(1, 0, 2).reshape(8, 4096),
-        ],
-        1,
-    )
-    bound = over_blk(bound.reshape(8, 8, 1280).transpose(1, 0, 2))
+    bound = bound_columns(root_every, middle_every)
     lower_values = total(over_columns(*last_product(bound, over, under, low_part)))
     return (root_values, middle_values, lower_values)
 

time: 224 us -> 221 us (0.987)
  local copies, waits for them, and re-layouts: 8.4 us -> 2.71 us
  starting transfers between devices: 53.4 us -> 56.3 us
  waiting for transfers between devices: 53.8 us -> 56.5 us
  blocking collectives: 92 us -> 89.5 us
    ppermute x29 -> x37, waiting for transfers between devices: 36.5 us -> 49.1 us  [send(): return lax.ppermute(value, AXES, pairs)]
    all_to_all x4 -> x2, waiting for transfers between devices: 17.4 us -> 7.42 us  [exchange(): return lax.all_to_all(value, AXES, 0, 0, axis_index_groups=members)]
    ppermute x29 -> x37, starting transfers between devices: 38 us -> 47.7 us  [send(): return lax.ppermute(value, AXES, pairs)]
    all_to_all x4 -> x2, starting transfers between devices: 15.4 us -> 8.62 us  [exchange(): return lax.all_to_all(value, AXES, 0, 0, axis_index_groups=members)]
    unnamed x22 -> x20, local copies, waits for them, and re-layouts: 7.31 us -> 1.64 us
    all_to_all x5, blocking collectives: 92 us -> 89.5 us  [exchange(): return lax.all_to_all(value, AXES, 0, 0, axis_index_groups=members)]
  transfers between devices with their start and end apart: 33 -> 39, of which waited for: 26 -> 31; matrix products, arithmetic and copies ran while one was open for 0% -> 0% of each run, Pallas kernels for 1% -> 1%
where the time goes in v5:
time: 221 us; the launch traced here: 220 us
  blocking collectives  89.5 us (40%)
  waiting for transfers between devices  56.5 us (26%)
  starting transfers between devices  56.3 us (25%)
  Pallas kernels  13.1 us (6%)
  local copies, waits for them, and re-layouts  2.71 us (1%)
    all_to_all x5, blocking collectives, exchange(): return lax.all_to_all(value, AXES, 0, 0, axis_index_groups=members)  89.5 us
    ppermute x37, waiting for transfers between devices, send(): return lax.ppermute(value, AXES, pairs)  49.1 us
    ppermute x37, starting transfers between devices, send(): return lax.ppermute(value, AXES, pairs)  47.7 us
    all_to_all x2, starting transfers between devices, exchange(): return lax.all_to_all(value, AXES, 0, 0, axis_index_groups=members)  8.62 us
    pallas_call x6, Pallas kernels, product(): pl.pallas_call(body, name=name, out_shape=[jax.ShapeDtypeStruct(shape, jn...  7.45 us
    all_to_all x2, waiting for transfers between devices, exchange(): return lax.all_to_all(value, AXES, 0, 0, axis_index_groups=members)  7.42 us
  transfers between devices with their start and end apart: 39, of which 31 were waited for; matrix products, arithmetic and copies ran while one was open for 0% of the time, Pallas kernels for 1%

profile of v5, /device:TPU:0, one launch (start us, length us, event | category | flops | bytes accessed | tf_op | source)
XLA Modules:
  0.0 220.3 jit_solution(7767296841354781618)
XLA Ops:
  3.1 19.9 %all_to_all.35.refs_0_ = f32[16,16,512]{2,1,0:T(8,128)S(1)} all-to-all(f32[16,16,512]{2,1,0:T(8,128)S(1)} %bitcast.26), channel_id=1, replica_groups={{0,2,4,6,8,10,12,14,16,18,20,22,24,26,28,30},{1,3,5,7,9,11,13,15,17,19,..., dimensions={0} | all-to-all | bytes 1048576 | tf_op jit(solution)/shard_map/all_to_all | solution.py:31
  28.3 2.7 %collective-permute-start.2 = (f32[64,512]{1,0:T(8,128)S(1)}, f32[64,512]{1,0:T(8,128)S(1)}, u32[]{:S(2)}, u32[]{:S(2)}) collective-permute-start(f32[64,512]{1,0:T(8,128)S(1)} %added.2.refs_0_), channel_id=1, source_target_pairs={{0,8},{1,9},{2,10},{3,11},{4,12},{5,13},{6,14},{7,15},{8,0},{9,1},... | collective-permute-start | bytes 393224 | tf_op jit(solution)/shard_map/ppermute | solution.py:23
  31.0 5.5 %collective-permute-done.4.refs_3_ = f32[64,512]{1,0:T(8,128)S(1)} collective-permute-done((f32[64,512]{1,0:T(8,128)S(1)}, f32[64,512]{1,0:T(8,128)S(1)}, u32[]{:S(2)}, u32[]{:S(2)}) %collective-permute-start.4) | collective-permute-done | bytes 131104 | tf_op jit(solution)/shard_map/ppermute | solution.py:23
  39.2 2.7 %collective-permute-start.7 = (f32[64,512]{1,0:T(8,128)S(1)}, f32[64,512]{1,0:T(8,128)S(1)}, u32[]{:S(2)}, u32[]{:S(2)}) collective-permute-start(f32[64,512]{1,0:T(8,128)S(1)} %get-tuple-element.61), channel_id=1, source_target_pairs={{0,6},{1,7},{2,4},{3,5},{4,2},{5,3},{6,0},{7,1},{8,14},{9,15},{10,... | collective-permute-start | bytes 393224 | tf_op jit(solution)/shard_map/ppermute | solution.py:23
  46.7 2.3 %low_lift.1 = (f32[8,4,8,512]{3,2,1,0:T(8,128)S(1)}, f32[8,4,8,512]{3,2,1,0:T(8,128)S(1)}, f32[4,8,2560]{2,1,0:T(8,128)S(1)}, f32[4,8,2560]{2,1,0:T(8,128)S(1)}) custom-call(f32[64,512]{1,0:T(8,128)S(1)} %get-tuple-element.58.refs_0_, f32[64,512]{1,0:T(8,128)S(1)} %collective-permute-done.5.refs_1_, f32[64,512]{1,0:T(8,128)S(1)} %collective-permute-done.6.refs_2_, ...), custom_call_target="tpu_custom_call" | custom-call | flops 503316480 | bytes 5242880 | tf_op jit(solution)/shard_map/low_lift/pallas_call | solution.py:123
  51.9 5.2 %all-to-all-start.1 = ((f32[32,8,512]{2,1,0:T(8,128)}), f32[32,8,512]{2,1,0:T(8,128)S(1)}, u32[]{:S(2)}, u32[]{:S(2)}) async-start(f32[32,8,512]{2,1,0:T(8,128)} %bitcast.7), calls=%async_computation.1 | async-start | bytes 1048576 | tf_op jit(solution)/shard_map/all_to_all | solution.py:31
  59.0 3.7 %collective-permute-start.16 = (f32[4,8,1536]{2,1,0:T(8,128)S(1)}, f32[4,8,1536]{2,1,0:T(8,128)S(1)}, u32[]{:S(2)}, u32[]{:S(2)}) collective-permute-start(f32[4,8,1536]{2,1,0:T(8,128)S(1)} %fusion), channel_id=1, source_target_pairs={{0,8},{1,9},{2,10},{3,11},{4,12},{5,13},{6,14},{7,15},{8,16},{9,17... | collective-permute-start | bytes 589832 | tf_op jit(solution)/shard_map/ppermute | solution.py:23
  62.8 6.3 %all-to-all-done.1.refs_0_ = f32[32,8,512]{2,1,0:T(8,128)S(1)} async-done(((f32[32,8,512]{2,1,0:T(8,128)}), f32[32,8,512]{2,1,0:T(8,128)S(1)}, u32[]{:S(2)}, u32[]{:S(2)}) %all-to-all-start.1) | async-done | bytes 524320 | tf_op jit(solution)/shard_map/all_to_all | solution.py:31
  69.8 3.4 %all-to-all-start.2 = ((f32[8,8,512]{2,1,0:T(8,128)}), f32[8,8,512]{2,1,0:T(8,128)S(1)}, u32[]{:S(2)}, u32[]{:S(2)}) async-start(f32[8,8,512]{2,1,0:T(8,128)} %get-tuple-element.66), calls=%async_computation.2 | async-start | bytes 262144 | tf_op jit(solution)/shard_map/all_to_all | solution.py:31
  73.2 5.3 %collective-permute-start.15 = (f32[4,8,512]{2,1,0:T(8,128)S(1)}, f32[4,8,512]{2,1,0:T(8,128)S(1)}, u32[]{:S(2)}, u32[]{:S(2)}) collective-permute-start(f32[4,8,512]{2,1,0:T(8,128)S(1)} %get-tuple-element.110), channel_id=1, source_target_pairs={{0,16},{1,17},{2,18},{3,19},{4,20},{5,21},{6,22},{7,23},{8,24},{9,... | collective-permute-start | bytes 196616 | tf_op jit(solution)/shard_map/ppermute | solution.py:23
  85.8 5.5 %collective-permute-done.12 = f32[64,512]{1,0:T(8,128)S(1)} collective-permute-done((f32[64,512]{1,0:T(8,128)S(1)}, f32[64,512]{1,0:T(8,128)S(1)}, u32[]{:S(2)}, u32[]{:S(2)}) %collective-permute-start.12) | collective-permute-done | bytes 131104 | tf_op jit(solution)/shard_map/ppermute | solution.py:23
  93.9 29.6 %all_to_all.36.parts = f32[128,8,128]{2,1,0:T(8,128)S(1)} all-to-all(f32[128,8,128]{2,1,0:T(8,128)S(1)} %mid_lift.1), channel_id=1, replica_groups={{0,1,2,3,4,5,6,7,8,9,10,11,12,13,14,15,16,17,18,19,20,21,22,23,24,25,26..., dimensions={0} | all-to-all | bytes 1048576 | tf_op jit(solution)/shard_map/all_to_all | solution.py:31
  123.5 18.1 %all_to_all.37.refs_0_ = f32[128,8,128]{2,1,0:T(8,128)S(1)} all-to-all(f32[128,8,128]{2,1,0:T(8,128)S(1)} %mixed.1), channel_id=1, replica_groups={{0,1,2,3,4,5,6,7,8,9,10,11,12,13,14,15,16,17,18,19,20,21,22,23,24,25,26..., dimensions={0} | all-to-all | bytes 1048576 | tf_op jit(solution)/shard_map/all_to_all | solution.py:31
  147.1 2.5 %collective-permute-start.20 = (f32[8,768]{1,0:T(8,128)S(1)}, f32[8,768]{1,0:T(8,128)S(1)}, u32[]{:S(2)}, u32[]{:S(2)}) collective-permute-start(f32[8,768]{1,0:T(8,128)S(1)} %get-tuple-element.75), channel_id=1, source_target_pairs={{0,6},{1,7},{2,4},{3,5},{4,2},{5,3},{6,0},{7,1},{8,14},{9,15},{10,... | collective-permute-start | bytes 73736 | tf_op jit(solution)/shard_map/ppermute | solution.py:23
  152.7 12.8 %all_to_all.38.every.root = f32[16,8,768]{2,1,0:T(8,128)S(1)} all-to-all(f32[16,8,768]{2,1,0:T(8,128)S(1)} %get-tuple-element.77), channel_id=1, replica_groups={{0,8,16,24,32,40,48,56,64,72,80,88,96,104,112,120},{1,9,17,25,33,41,49,..., dimensions={0} | all-to-all | bytes 786432 | tf_op jit(solution)/shard_map/all_to_all | solution.py:31
  167.2 3.1 %collective-permute-start.23 = (f32[16,1536]{1,0:T(8,128)S(1)}, f32[16,1536]{1,0:T(8,128)S(1)}, u32[]{:S(2)}, u32[]{:S(2)}) collective-permute-start(f32[16,1536]{1,0:T(8,128)S(1)} %get-tuple-element.82), channel_id=1, source_target_pairs={{0,4},{1,5},{2,6},{3,7},{4,0},{5,1},{6,2},{7,3},{8,12},{9,13},{10,... | collective-permute-start | bytes 294920 | tf_op jit(solution)/shard_map/ppermute | solution.py:23
  172.9 2.5 %collective-permute-done.23.refs_2_ = f32[16,1536]{1,0:T(8,128)S(1)} collective-permute-done((f32[16,1536]{1,0:T(8,128)S(1)}, f32[16,1536]{1,0:T(8,128)S(1)}, u32[]{:S(2)}, u32[]{:S(2)}) %collective-permute-start.23) | collective-permute-done | bytes 98336 | tf_op jit(solution)/shard_map/ppermute | solution.py:23
  179.8 3.0 %collective-permute-start.27 = (f32[8,512]{1,0:T(8,128)S(1)}, f32[8,512]{1,0:T(8,128)S(1)}, u32[]{:S(2)}, u32[]{:S(2)}) collective-permute-start(f32[8,512]{1,0:T(8,128)S(1)} %get-tuple-element.88), channel_id=1, source_target_pairs={{0,4},{1,5},{2,6},{3,7},{4,0},{5,1},{6,2},{7,3},{8,12},{9,13},{10,... | collective-permute-start | bytes 49160 | tf_op jit(solution)/shard_map/ppermute | solution.py:23
  185.1 2.7 %collective-permute-done.28.refs_3_ = f32[8,512]{1,0:T(8,128)S(1)} collective-permute-done((f32[8,512]{1,0:T(8,128)S(1)}, f32[8,512]{1,0:T(8,128)S(1)}, u32[]{:S(2)}, u32[]{:S(2)}) %collective-permute-start.28) | collective-permute-done | bytes 16416 | tf_op jit(solution)/shard_map/ppermute | solution.py:23
  188.4 9.1 %all_to_all.39.middle = f32[8,8,512]{2,1,0:T(8,128)S(1)} all-to-all(f32[8,8,512]{2,1,0:T(8,128)S(1)} %get-tuple-element.92), channel_id=1, replica_groups={{0,8,16,24,32,40,48,56},{1,9,17,25,33,41,49,57},{2,10,18,26,34,42,50,58..., dimensions={0} | all-to-all | bytes 262144 | tf_op jit(solution)/shard_map/all_to_all | solution.py:31
  199.2 3.1 %collective-permute-start.31 = (f32[16,1280]{1,0:T(8,128)S(1)}, f32[16,1280]{1,0:T(8,128)S(1)}, u32[]{:S(2)}, u32[]{:S(2)}) collective-permute-start(f32[16,1280]{1,0:T(8,128)S(1)} %get-tuple-element.97), channel_id=1, source_target_pairs={{0,4},{1,5},{2,6},{3,7},{4,0},{5,1},{6,2},{7,3},{8,12},{9,13},{10,... | collective-permute-start | bytes 245768 | tf_op jit(solution)/shard_map/ppermute | solution.py:23
  204.6 2.0 collective-permute-done.31.refs_2_
  211.6 3.0 %collective-permute-start.35 = (f32[8,1024]{1,0:T(8,128)S(1)}, f32[8,1024]{1,0:T(8,128)S(1)}, u32[]{:S(2)}, u32[]{:S(2)}) collective-permute-start(f32[8,1024]{1,0:T(8,128)S(1)} %get-tuple-element.107), channel_id=1, source_target_pairs={{0,4},{1,5},{2,6},{3,7},{4,0},{5,1},{6,2},{7,3},{8,12},{9,13},{10,... | collective-permute-start | bytes 98312 | tf_op jit(solution)/shard_map/ppermute | solution.py:23
  217.1 2.7 %collective-permute-done.36 = f32[8,1024]{1,0:T(8,128)S(1)} collective-permute-done((f32[8,1024]{1,0:T(8,128)S(1)}, f32[8,1024]{1,0:T(8,128)S(1)}, u32[]{:S(2)}, u32[]{:S(2)}) %collective-permute-start.36) | collective-permute-done | bytes 32800 | tf_op jit(solution)/shard_map/ppermute | solution.py:23
  (125 shorter events, 62.5 us)
Async XLA Ops:
  26.8 9.6 %collective-permute-start.4 = (f32[64,512]{1,0:T(8,128)S(1)}, f32[64,512]{1,0:T(8,128)S(1)}, u32[]{:S(2)}, u32[]{:S(2)}) collective-permute-start(f32[64,512]{1,0:T(8,128)S(1)} %added.2.refs_0_), channel_id=1, source_target_pairs={{0,24},{1,25},{2,26},{3,27},{4,28},{5,29},{6,30},{7,31},{8,16},{9,... | collective-permute-start | bytes 393224 | tf_op jit(solution)/shard_map/ppermute | solution.py:23
  27.8 8.7 %collective-permute-start.3 = (f32[64,512]{1,0:T(8,128)S(1)}, f32[64,512]{1,0:T(8,128)S(1)}, u32[]{:S(2)}, u32[]{:S(2)}) collective-permute-start(f32[64,512]{1,0:T(8,128)S(1)} %added.2.refs_0_), channel_id=1, source_target_pairs={{0,16},{1,17},{2,18},{3,19},{4,20},{5,21},{6,22},{7,23},{8,24},{9,... | collective-permute-start | bytes 393224 | tf_op jit(solution)/shard_map/ppermute | solution.py:23
  28.3 8.8 %collective-permute-start.2 = (f32[64,512]{1,0:T(8,128)S(1)}, f32[64,512]{1,0:T(8,128)S(1)}, u32[]{:S(2)}, u32[]{:S(2)}) collective-permute-start(f32[64,512]{1,0:T(8,128)S(1)} %added.2.refs_0_), channel_id=1, source_target_pairs={{0,8},{1,9},{2,10},{3,11},{4,12},{5,13},{6,14},{7,15},{8,0},{9,1},... | collective-permute-start | bytes 393224 | tf_op jit(solution)/shard_map/ppermute | solution.py:23
  37.2 5.9 %collective-permute-start.5 = (f32[64,512]{1,0:T(8,128)S(1)}, f32[64,512]{1,0:T(8,128)S(1)}, u32[]{:S(2)}, u32[]{:S(2)}) collective-permute-start(f32[64,512]{1,0:T(8,128)S(1)} %get-tuple-element.59), channel_id=1, source_target_pairs={{0,2},{1,3},{2,0},{3,1},{4,6},{5,7},{6,4},{7,5},{8,10},{9,11},{10,... | collective-permute-start | bytes 393224 | tf_op jit(solution)/shard_map/ppermute | solution.py:23
  37.8 7.2 %collective-permute-start.6 = (f32[64,512]{1,0:T(8,128)S(1)}, f32[64,512]{1,0:T(8,128)S(1)}, u32[]{:S(2)}, u32[]{:S(2)}) collective-permute-start(f32[64,512]{1,0:T(8,128)S(1)} %get-tuple-element.60), channel_id=1, source_target_pairs={{0,4},{1,5},{2,6},{3,7},{4,0},{5,1},{6,2},{7,3},{8,12},{9,13},{10,... | collective-permute-start | bytes 393224 | tf_op jit(solution)/shard_map/ppermute | solution.py:23
  39.2 7.5 %collective-permute-start.7 = (f32[64,512]{1,0:T(8,128)S(1)}, f32[64,512]{1,0:T(8,128)S(1)}, u32[]{:S(2)}, u32[]{:S(2)}) collective-permute-start(f32[64,512]{1,0:T(8,128)S(1)} %get-tuple-element.61), channel_id=1, source_target_pairs={{0,6},{1,7},{2,4},{3,5},{4,2},{5,3},{6,0},{7,1},{8,14},{9,15},{10,... | collective-permute-start | bytes 393224 | tf_op jit(solution)/shard_map/ppermute | solution.py:23
  51.9 17.2 %all-to-all-start.1 = ((f32[32,8,512]{2,1,0:T(8,128)}), f32[32,8,512]{2,1,0:T(8,128)S(1)}, u32[]{:S(2)}, u32[]{:S(2)}) async-start(f32[32,8,512]{2,1,0:T(8,128)} %bitcast.7), calls=%async_computation.1 | async-start | bytes 1048576 | tf_op jit(solution)/shard_map/all_to_all | solution.py:31
  59.0 14.1 %collective-permute-start.16 = (f32[4,8,1536]{2,1,0:T(8,128)S(1)}, f32[4,8,1536]{2,1,0:T(8,128)S(1)}, u32[]{:S(2)}, u32[]{:S(2)}) collective-permute-start(f32[4,8,1536]{2,1,0:T(8,128)S(1)} %fusion), channel_id=1, source_target_pairs={{0,8},{1,9},{2,10},{3,11},{4,12},{5,13},{6,14},{7,15},{8,16},{9,17... | collective-permute-start | bytes 589832 | tf_op jit(solution)/shard_map/ppermute | solution.py:23
  69.8 9.9 %all-to-all-start.2 = ((f32[8,8,512]{2,1,0:T(8,128)}), f32[8,8,512]{2,1,0:T(8,128)S(1)}, u32[]{:S(2)}, u32[]{:S(2)}) async-start(f32[8,8,512]{2,1,0:T(8,128)} %get-tuple-element.66), calls=%async_computation.2 | async-start | bytes 262144 | tf_op jit(solution)/shard_map/all_to_all | solution.py:31
  73.2 7.2 %collective-permute-start.15 = (f32[4,8,512]{2,1,0:T(8,128)S(1)}, f32[4,8,512]{2,1,0:T(8,128)S(1)}, u32[]{:S(2)}, u32[]{:S(2)}) collective-permute-start(f32[4,8,512]{2,1,0:T(8,128)S(1)} %get-tuple-element.110), channel_id=1, source_target_pairs={{0,16},{1,17},{2,18},{3,19},{4,20},{5,21},{6,22},{7,23},{8,24},{9,... | collective-permute-start | bytes 196616 | tf_op jit(solution)/shard_map/ppermute | solution.py:23
  81.6 9.6 %collective-permute-start.12 = (f32[64,512]{1,0:T(8,128)S(1)}, f32[64,512]{1,0:T(8,128)S(1)}, u32[]{:S(2)}, u32[]{:S(2)}) collective-permute-start(f32[64,512]{1,0:T(8,128)S(1)} %add.56), channel_id=1, source_target_pairs={{0,6},{1,7},{2,4},{3,5},{4,2},{5,3},{6,0},{7,1},{8,14},{9,15},{10,... | collective-permute-start | bytes 393224 | tf_op jit(solution)/shard_map/ppermute | solution.py:23
  82.9 8.3 %collective-permute-start.11 = (f32[64,512]{1,0:T(8,128)S(1)}, f32[64,512]{1,0:T(8,128)S(1)}, u32[]{:S(2)}, u32[]{:S(2)}) collective-permute-start(f32[64,512]{1,0:T(8,128)S(1)} %add.56), channel_id=1, source_target_pairs={{0,4},{1,5},{2,6},{3,7},{4,0},{5,1},{6,2},{7,3},{8,12},{9,13},{10,... | collective-permute-start | bytes 393224 | tf_op jit(solution)/shard_map/ppermute | solution.py:23
  84.3 7.6 %collective-permute-start.10 = (f32[64,512]{1,0:T(8,128)S(1)}, f32[64,512]{1,0:T(8,128)S(1)}, u32[]{:S(2)}, u32[]{:S(2)}) collective-permute-start(f32[64,512]{1,0:T(8,128)S(1)} %add.56), channel_id=1, source_target_pairs={{0,2},{1,3},{2,0},{3,1},{4,6},{5,7},{6,4},{7,5},{8,10},{9,11},{10,... | collective-permute-start | bytes 393224 | tf_op jit(solution)/shard_map/ppermute | solution.py:23
  145.3 5.3 %collective-permute-start.19 = (f32[8,768]{1,0:T(8,128)S(1)}, f32[8,768]{1,0:T(8,128)S(1)}, u32[]{:S(2)}, u32[]{:S(2)}) collective-permute-start(f32[8,768]{1,0:T(8,128)S(1)} %get-tuple-element.74), channel_id=1, source_target_pairs={{0,4},{1,5},{2,6},{3,7},{4,0},{5,1},{6,2},{7,3},{8,12},{9,13},{10,... | collective-permute-start | bytes 73736 | tf_op jit(solution)/shard_map/ppermute | solution.py:23
  147.1 5.0 %collective-permute-start.20 = (f32[8,768]{1,0:T(8,128)S(1)}, f32[8,768]{1,0:T(8,128)S(1)}, u32[]{:S(2)}, u32[]{:S(2)}) collective-permute-start(f32[8,768]{1,0:T(8,128)S(1)} %get-tuple-element.75), channel_id=1, source_target_pairs={{0,6},{1,7},{2,4},{3,5},{4,2},{5,3},{6,0},{7,1},{8,14},{9,15},{10,... | collective-permute-start | bytes 73736 | tf_op jit(solution)/shard_map/ppermute | solution.py:23
  167.1 5.7 %collective-permute-start.22 = (f32[16,1536]{1,0:T(8,128)S(1)}, f32[16,1536]{1,0:T(8,128)S(1)}, u32[]{:S(2)}, u32[]{:S(2)}) collective-permute-start(f32[16,1536]{1,0:T(8,128)S(1)} %get-tuple-element.81), channel_id=1, source_target_pairs={{0,2},{1,3},{2,0},{3,1},{4,6},{5,7},{6,4},{7,5},{8,10},{9,11},{10,... | collective-permute-start | bytes 294920 | tf_op jit(solution)/shard_map/ppermute | solution.py:23
  167.2 8.1 %collective-permute-start.23 = (f32[16,1536]{1,0:T(8,128)S(1)}, f32[16,1536]{1,0:T(8,128)S(1)}, u32[]{:S(2)}, u32[]{:S(2)}) collective-permute-start(f32[16,1536]{1,0:T(8,128)S(1)} %get-tuple-element.82), channel_id=1, source_target_pairs={{0,4},{1,5},{2,6},{3,7},{4,0},{5,1},{6,2},{7,3},{8,12},{9,13},{10,... | collective-permute-start | bytes 294920 | tf_op jit(solution)/shard_map/ppermute | solution.py:23
  170.3 6.9 %collective-permute-start.24 = (f32[16,1536]{1,0:T(8,128)S(1)}, f32[16,1536]{1,0:T(8,128)S(1)}, u32[]{:S(2)}, u32[]{:S(2)}) collective-permute-start(f32[16,1536]{1,0:T(8,128)S(1)} %get-tuple-element.83), channel_id=1, source_target_pairs={{0,6},{1,7},{2,4},{3,5},{4,2},{5,3},{6,0},{7,1},{8,14},{9,15},{10,... | collective-permute-start | bytes 294920 | tf_op jit(solution)/shard_map/ppermute | solution.py:23
  179.8 5.3 %collective-permute-start.27 = (f32[8,512]{1,0:T(8,128)S(1)}, f32[8,512]{1,0:T(8,128)S(1)}, u32[]{:S(2)}, u32[]{:S(2)}) collective-permute-start(f32[8,512]{1,0:T(8,128)S(1)} %get-tuple-element.88), channel_id=1, source_target_pairs={{0,4},{1,5},{2,6},{3,7},{4,0},{5,1},{6,2},{7,3},{8,12},{9,13},{10,... | collective-permute-start | bytes 49160 | tf_op jit(solution)/shard_map/ppermute | solution.py:23
  199.1 5.5 %collective-permute-start.30 = (f32[16,1280]{1,0:T(8,128)S(1)}, f32[16,1280]{1,0:T(8,128)S(1)}, u32[]{:S(2)}, u32[]{:S(2)}) collective-permute-start(f32[16,1280]{1,0:T(8,128)S(1)} %get-tuple-element.96), channel_id=1, source_target_pairs={{0,2},{1,3},{2,0},{3,1},{4,6},{5,7},{6,4},{7,5},{8,10},{9,11},{10,... | collective-permute-start | bytes 245768 | tf_op jit(solution)/shard_map/ppermute | solution.py:23
  199.2 7.4 %collective-permute-start.31 = (f32[16,1280]{1,0:T(8,128)S(1)}, f32[16,1280]{1,0:T(8,128)S(1)}, u32[]{:S(2)}, u32[]{:S(2)}) collective-permute-start(f32[16,1280]{1,0:T(8,128)S(1)} %get-tuple-element.97), channel_id=1, source_target_pairs={{0,4},{1,5},{2,6},{3,7},{4,0},{5,1},{6,2},{7,3},{8,12},{9,13},{10,... | collective-permute-start | bytes 245768 | tf_op jit(solution)/shard_map/ppermute | solution.py:23
  202.3 6.0 %collective-permute-start.32 = (f32[16,1280]{1,0:T(8,128)S(1)}, f32[16,1280]{1,0:T(8,128)S(1)}, u32[]{:S(2)}, u32[]{:S(2)}) collective-permute-start(f32[16,1280]{1,0:T(8,128)S(1)} %get-tuple-element.98), channel_id=1, source_target_pairs={{0,6},{1,7},{2,4},{3,5},{4,2},{5,3},{6,0},{7,1},{8,14},{9,15},{10,... | collective-permute-start | bytes 245768 | tf_op jit(solution)/shard_map/ppermute | solution.py:23
  211.6 5.5 %collective-permute-start.35 = (f32[8,1024]{1,0:T(8,128)S(1)}, f32[8,1024]{1,0:T(8,128)S(1)}, u32[]{:S(2)}, u32[]{:S(2)}) collective-permute-start(f32[8,1024]{1,0:T(8,128)S(1)} %get-tuple-element.107), channel_id=1, source_target_pairs={{0,4},{1,5},{2,6},{3,7},{4,0},{5,1},{6,2},{7,3},{8,12},{9,13},{10,... | collective-permute-start | bytes 98312 | tf_op jit(solution)/shard_map/ppermute | solution.py:23
  214.6 5.1 %collective-permute-start.36 = (f32[8,1024]{1,0:T(8,128)S(1)}, f32[8,1024]{1,0:T(8,128)S(1)}, u32[]{:S(2)}, u32[]{:S(2)}) collective-permute-start(f32[8,1024]{1,0:T(8,128)S(1)} %get-tuple-element.108), channel_id=1, source_target_pairs={{0,6},{1,7},{2,4},{3,5},{4,2},{5,3},{6,0},{7,1},{8,14},{9,15},{10,... | collective-permute-start | bytes 98312 | tf_op jit(solution)/shard_map/ppermute | solution.py:23
  (26 other events, 503.8 us)

commit v6 on v5

--- a/solution.py
+++ b/solution.py
@@ -47,8 +47,8 @@
     return exchange(value, lambda x, z, y, c: (x // 2, c), lambda x, z, y, c: (x, z, y))
 
 
-def over_zy(value):
-    return exchange(value, lambda x, z, y, c: (x, c), lambda x, z, y, c: 4 * z + y)
+def over_plane(value):
+    return exchange(value, lambda x, z, y, c: x, lambda x, z, y, c: (z, y, c))
 
 
 def over_all(value):
@@ -188,9 +188,26 @@
     )(first, second)
 
 
+def fanned(particular):
+    def body(particular, out):
+        for block in range(8):
+            piece = particular[:, 512 + 512 * block : 1024 + 512 * block]
+            for k in range(4):
+                out[8 * k + block] = piece
+
+    return pl.pallas_call(
+        body,
+        name="fanned",
+        out_shape=jax.ShapeDtypeStruct((32, 8, 512), jnp.float32),
+        in_specs=[pl.BlockSpec(memory_space=pltpu.VMEM)],
+        out_specs=pl.BlockSpec(memory_space=pltpu.VMEM),
+        compiler_params=pltpu.CompilerParams(vmem_limit_bytes=4 << 20),
+    )(particular)
+
+
 def low_product(jump, operator):
     def vectors(jump):
-        return (jump[12:16] - jump[4:8]).reshape(64, 512)
+        return (jump[24:32] - jump[8:16]).reshape(64, 512)
 
     def store(number, tile, jump, part, keep, give):
         part[:, 512 * number : 512 * (number + 1)] = tile
@@ -504,11 +521,7 @@
     x, z, y, c = place()
     xh, xl = x // 2, x % 2
 
-    inner = particular[:, 512:].reshape(8, 4, 2, 512)
-    keep = lax.dynamic_index_in_dim(inner, c, 2, False).transpose(1, 0, 2)
-    got = swap_core(lax.dynamic_index_in_dim(inner, 1 - c, 2, False).transpose(1, 0, 2))
-    both = jnp.concatenate([jnp.where(c == 0, keep, got), jnp.where(c == 0, got, keep)], 1)
-    jump_two = over_zy(copies(both, 4).reshape(16, 16, 512))
+    jump_two = over_plane(fanned(particular))
 
     low_part, keep, give = low_product(jump_two, low_inverse)
     half = added(keep, swap_core(give))

time: 221 us -> 221 us (level)
    ppermute x37 -> x36, waiting for transfers between devices: 49.1 us -> 48.6 us  [send(): return lax.ppermute(value, AXES, pairs)]
    ppermute x37 -> x36, starting transfers between devices: 47.7 us -> 47.7 us  [send(): return lax.ppermute(value, AXES, pairs)]
  transfers between devices with their start and end apart: 39 -> 38, of which waited for: 31 -> 30; matrix products, arithmetic and copies ran while one was open for 0% -> 0% of each run, Pallas kernels for 1% -> 1%
where the time goes in v6:
time: 221 us
  blocking collectives  89.7 us (41%)
  starting transfers between devices  56.3 us (25%)
  waiting for transfers between devices  56 us (25%)
  Pallas kernels  13.1 us (6%)
  local copies, waits for them, and re-layouts  3.65 us (2%)
    all_to_all x5, blocking collectives, exchange(): return lax.all_to_all(value, AXES, 0, 0, axis_index_groups=members)  89.7 us
    ppermute x36, waiting for transfers between devices, send(): return lax.ppermute(value, AXES, pairs)  48.6 us
    ppermute x36, starting transfers between devices, send(): return lax.ppermute(value, AXES, pairs)  47.7 us
    all_to_all x2, starting transfers between devices, exchange(): return lax.all_to_all(value, AXES, 0, 0, axis_index_groups=members)  8.6 us
    pallas_call x6, Pallas kernels, product(): pl.pallas_call(body, name=name, out_shape=[jax.ShapeDtypeStruct(shape, jn...  7.44 us
    all_to_all x2, waiting for transfers between devices, exchange(): return lax.all_to_all(value, AXES, 0, 0, axis_index_groups=members)  7.41 us
  transfers between devices with their start and end apart: 38, of which 30 were waited for; matrix products, arithmetic and copies ran while one was open for 0% of the time, Pallas kernels for 1%

profile of v6, /device:TPU:0, one launch (start us, length us, event | category | flops | bytes accessed | tf_op | source)
XLA Modules:
  0.0 220.9 jit_solution(16822009247074944667)
XLA Ops:
  1.7 20.1 %all_to_all.35.refs_0_ = f32[32,8,512]{2,1,0:T(8,128)S(1)} all-to-all(f32[32,8,512]{2,1,0:T(8,128)S(1)} %fanned.1), channel_id=1, replica_groups={{0,1,2,3,4,5,6,7,8,9,10,11,12,13,14,15,16,17,18,19,20,21,22,23,24,25,26..., dimensions={0} | all-to-all | bytes 1048576 | tf_op jit(solution)/shard_map/all_to_all | solution.py:31
  29.9 5.5 %collective-permute-done.3.refs_3_ = f32[64,512]{1,0:T(8,128)S(1)} collective-permute-done((f32[64,512]{1,0:T(8,128)S(1)}, f32[64,512]{1,0:T(8,128)S(1)}, u32[]{:S(2)}, u32[]{:S(2)}) %collective-permute-start.3) | collective-permute-done | bytes 131104 | tf_op jit(solution)/shard_map/ppermute | solution.py:23
  36.8 2.2 %collective-permute-start.5 = (f32[64,512]{1,0:T(8,128)S(1)}, f32[64,512]{1,0:T(8,128)S(1)}, u32[]{:S(2)}, u32[]{:S(2)}) collective-permute-start(f32[64,512]{1,0:T(8,128)S(1)} %get-tuple-element.60), channel_id=1, source_target_pairs={{0,4},{1,5},{2,6},{3,7},{4,0},{5,1},{6,2},{7,3},{8,12},{9,13},{10,... | collective-permute-start | bytes 393224 | tf_op jit(solution)/shard_map/ppermute | solution.py:23
  42.0 2.6 %collective-permute-done.5.refs_2_ = f32[64,512]{1,0:T(8,128)S(1)} collective-permute-done((f32[64,512]{1,0:T(8,128)S(1)}, f32[64,512]{1,0:T(8,128)S(1)}, u32[]{:S(2)}, u32[]{:S(2)}) %collective-permute-start.5) | collective-permute-done | bytes 131104 | tf_op jit(solution)/shard_map/ppermute | solution.py:23
  47.2 2.3 %low_lift.1 = (f32[8,4,8,512]{3,2,1,0:T(8,128)S(1)}, f32[8,4,8,512]{3,2,1,0:T(8,128)S(1)}, f32[4,8,2560]{2,1,0:T(8,128)S(1)}, f32[4,8,2560]{2,1,0:T(8,128)S(1)}) custom-call(f32[64,512]{1,0:T(8,128)S(1)} %get-tuple-element.58.refs_0_, f32[64,512]{1,0:T(8,128)S(1)} %collective-permute-done.4.refs_1_, f32[64,512]{1,0:T(8,128)S(1)} %collective-permute-done.5.refs_2_, ...), custom_call_target="tpu_custom_call" | custom-call | flops 503316480 | bytes 5242880 | tf_op jit(solution)/shard_map/low_lift/pallas_call | solution.py:123
  52.4 5.2 %all-to-all-start.1 = ((f32[32,8,512]{2,1,0:T(8,128)}), f32[32,8,512]{2,1,0:T(8,128)S(1)}, u32[]{:S(2)}, u32[]{:S(2)}) async-start(f32[32,8,512]{2,1,0:T(8,128)} %bitcast), calls=%async_computation.1 | async-start | bytes 1048576 | tf_op jit(solution)/shard_map/all_to_all | solution.py:31
  59.6 3.7 %collective-permute-start.15 = (f32[4,8,1536]{2,1,0:T(8,128)S(1)}, f32[4,8,1536]{2,1,0:T(8,128)S(1)}, u32[]{:S(2)}, u32[]{:S(2)}) collective-permute-start(f32[4,8,1536]{2,1,0:T(8,128)S(1)} %fusion), channel_id=1, source_target_pairs={{0,8},{1,9},{2,10},{3,11},{4,12},{5,13},{6,14},{7,15},{8,16},{9,17... | collective-permute-start | bytes 589832 | tf_op jit(solution)/shard_map/ppermute | solution.py:23
  63.3 6.3 %all-to-all-done.1.refs_0_ = f32[32,8,512]{2,1,0:T(8,128)S(1)} async-done(((f32[32,8,512]{2,1,0:T(8,128)}), f32[32,8,512]{2,1,0:T(8,128)S(1)}, u32[]{:S(2)}, u32[]{:S(2)}) %all-to-all-start.1) | async-done | bytes 524320 | tf_op jit(solution)/shard_map/all_to_all | solution.py:31
  70.3 3.4 %all-to-all-start.2 = ((f32[8,8,512]{2,1,0:T(8,128)}), f32[8,8,512]{2,1,0:T(8,128)S(1)}, u32[]{:S(2)}, u32[]{:S(2)}) async-start(f32[8,8,512]{2,1,0:T(8,128)} %get-tuple-element.66), calls=%async_computation.2 | async-start | bytes 262144 | tf_op jit(solution)/shard_map/all_to_all | solution.py:31
  73.7 5.3 %collective-permute-start.14 = (f32[4,8,512]{2,1,0:T(8,128)S(1)}, f32[4,8,512]{2,1,0:T(8,128)S(1)}, u32[]{:S(2)}, u32[]{:S(2)}) collective-permute-start(f32[4,8,512]{2,1,0:T(8,128)S(1)} %get-tuple-element.110), channel_id=1, source_target_pairs={{0,16},{1,17},{2,18},{3,19},{4,20},{5,21},{6,22},{7,23},{8,24},{9,... | collective-permute-start | bytes 196616 | tf_op jit(solution)/shard_map/ppermute | solution.py:23
  86.3 5.5 %collective-permute-done.11 = f32[64,512]{1,0:T(8,128)S(1)} collective-permute-done((f32[64,512]{1,0:T(8,128)S(1)}, f32[64,512]{1,0:T(8,128)S(1)}, u32[]{:S(2)}, u32[]{:S(2)}) %collective-permute-start.11) | collective-permute-done | bytes 131104 | tf_op jit(solution)/shard_map/ppermute | solution.py:23
  94.4 29.6 %all_to_all.36.parts = f32[128,8,128]{2,1,0:T(8,128)S(1)} all-to-all(f32[128,8,128]{2,1,0:T(8,128)S(1)} %mid_lift.1), channel_id=1, replica_groups={{0,1,2,3,4,5,6,7,8,9,10,11,12,13,14,15,16,17,18,19,20,21,22,23,24,25,26..., dimensions={0} | all-to-all | bytes 1048576 | tf_op jit(solution)/shard_map/all_to_all | solution.py:31
  124.0 18.1 %all_to_all.37.refs_0_ = f32[128,8,128]{2,1,0:T(8,128)S(1)} all-to-all(f32[128,8,128]{2,1,0:T(8,128)S(1)} %mixed.1), channel_id=1, replica_groups={{0,1,2,3,4,5,6,7,8,9,10,11,12,13,14,15,16,17,18,19,20,21,22,23,24,25,26..., dimensions={0} | all-to-all | bytes 1048576 | tf_op jit(solution)/shard_map/all_to_all | solution.py:31
  147.6 2.5 %collective-permute-start.19 = (f32[8,768]{1,0:T(8,128)S(1)}, f32[8,768]{1,0:T(8,128)S(1)}, u32[]{:S(2)}, u32[]{:S(2)}) collective-permute-start(f32[8,768]{1,0:T(8,128)S(1)} %get-tuple-element.75), channel_id=1, source_target_pairs={{0,6},{1,7},{2,4},{3,5},{4,2},{5,3},{6,0},{7,1},{8,14},{9,15},{10,... | collective-permute-start | bytes 73736 | tf_op jit(solution)/shard_map/ppermute | solution.py:23
  153.3 12.8 %all_to_all.38.every.root = f32[16,8,768]{2,1,0:T(8,128)S(1)} all-to-all(f32[16,8,768]{2,1,0:T(8,128)S(1)} %get-tuple-element.77), channel_id=1, replica_groups={{0,8,16,24,32,40,48,56,64,72,80,88,96,104,112,120},{1,9,17,25,33,41,49,..., dimensions={0} | all-to-all | bytes 786432 | tf_op jit(solution)/shard_map/all_to_all | solution.py:31
  167.8 3.1 %collective-permute-start.22 = (f32[16,1536]{1,0:T(8,128)S(1)}, f32[16,1536]{1,0:T(8,128)S(1)}, u32[]{:S(2)}, u32[]{:S(2)}) collective-permute-start(f32[16,1536]{1,0:T(8,128)S(1)} %get-tuple-element.82), channel_id=1, source_target_pairs={{0,4},{1,5},{2,6},{3,7},{4,0},{5,1},{6,2},{7,3},{8,12},{9,13},{10,... | collective-permute-start | bytes 294920 | tf_op jit(solution)/shard_map/ppermute | solution.py:23
  173.4 2.5 %collective-permute-done.22.refs_2_ = f32[16,1536]{1,0:T(8,128)S(1)} collective-permute-done((f32[16,1536]{1,0:T(8,128)S(1)}, f32[16,1536]{1,0:T(8,128)S(1)}, u32[]{:S(2)}, u32[]{:S(2)}) %collective-permute-start.22) | collective-permute-done | bytes 98336 | tf_op jit(solution)/shard_map/ppermute | solution.py:23
  180.3 3.0 %collective-permute-start.26 = (f32[8,512]{1,0:T(8,128)S(1)}, f32[8,512]{1,0:T(8,128)S(1)}, u32[]{:S(2)}, u32[]{:S(2)}) collective-permute-start(f32[8,512]{1,0:T(8,128)S(1)} %get-tuple-element.88), channel_id=1, source_target_pairs={{0,4},{1,5},{2,6},{3,7},{4,0},{5,1},{6,2},{7,3},{8,12},{9,13},{10,... | collective-permute-start | bytes 49160 | tf_op jit(solution)/shard_map/ppermute | solution.py:23
  185.7 2.7 %collective-permute-done.27.refs_3_ = f32[8,512]{1,0:T(8,128)S(1)} collective-permute-done((f32[8,512]{1,0:T(8,128)S(1)}, f32[8,512]{1,0:T(8,128)S(1)}, u32[]{:S(2)}, u32[]{:S(2)}) %collective-permute-start.27) | collective-permute-done | bytes 16416 | tf_op jit(solution)/shard_map/ppermute | solution.py:23
  188.9 9.1 %all_to_all.39.middle = f32[8,8,512]{2,1,0:T(8,128)S(1)} all-to-all(f32[8,8,512]{2,1,0:T(8,128)S(1)} %get-tuple-element.92), channel_id=1, replica_groups={{0,8,16,24,32,40,48,56},{1,9,17,25,33,41,49,57},{2,10,18,26,34,42,50,58..., dimensions={0} | all-to-all | bytes 262144 | tf_op jit(solution)/shard_map/all_to_all | solution.py:31
  199.7 3.1 %collective-permute-start.30 = (f32[16,1280]{1,0:T(8,128)S(1)}, f32[16,1280]{1,0:T(8,128)S(1)}, u32[]{:S(2)}, u32[]{:S(2)}) collective-permute-start(f32[16,1280]{1,0:T(8,128)S(1)} %get-tuple-element.97), channel_id=1, source_target_pairs={{0,4},{1,5},{2,6},{3,7},{4,0},{5,1},{6,2},{7,3},{8,12},{9,13},{10,... | collective-permute-start | bytes 245768 | tf_op jit(solution)/shard_map/ppermute | solution.py:23
  205.1 2.0 collective-permute-done.30.refs_2_
  212.1 3.0 %collective-permute-start.34 = (f32[8,1024]{1,0:T(8,128)S(1)}, f32[8,1024]{1,0:T(8,128)S(1)}, u32[]{:S(2)}, u32[]{:S(2)}) collective-permute-start(f32[8,1024]{1,0:T(8,128)S(1)} %get-tuple-element.107), channel_id=1, source_target_pairs={{0,4},{1,5},{2,6},{3,7},{4,0},{5,1},{6,2},{7,3},{8,12},{9,13},{10,... | collective-permute-start | bytes 98312 | tf_op jit(solution)/shard_map/ppermute | solution.py:23
  217.6 2.7 %collective-permute-done.35 = f32[8,1024]{1,0:T(8,128)S(1)} collective-permute-done((f32[8,1024]{1,0:T(8,128)S(1)}, f32[8,1024]{1,0:T(8,128)S(1)}, u32[]{:S(2)}, u32[]{:S(2)}) %collective-permute-start.35) | collective-permute-done | bytes 32800 | tf_op jit(solution)/shard_map/ppermute | solution.py:23
  (123 shorter events, 63.6 us)
Async XLA Ops:
  25.7 9.6 %collective-permute-start.3 = (f32[64,512]{1,0:T(8,128)S(1)}, f32[64,512]{1,0:T(8,128)S(1)}, u32[]{:S(2)}, u32[]{:S(2)}) collective-permute-start(f32[64,512]{1,0:T(8,128)S(1)} %added.2.refs_0_), channel_id=1, source_target_pairs={{0,24},{1,25},{2,26},{3,27},{4,28},{5,29},{6,30},{7,31},{8,16},{9,... | collective-permute-start | bytes 393224 | tf_op jit(solution)/shard_map/ppermute | solution.py:23
  26.5 8.8 %collective-permute-start.2 = (f32[64,512]{1,0:T(8,128)S(1)}, f32[64,512]{1,0:T(8,128)S(1)}, u32[]{:S(2)}, u32[]{:S(2)}) collective-permute-start(f32[64,512]{1,0:T(8,128)S(1)} %added.2.refs_0_), channel_id=1, source_target_pairs={{0,16},{1,17},{2,18},{3,19},{4,20},{5,21},{6,22},{7,23},{8,24},{9,... | collective-permute-start | bytes 393224 | tf_op jit(solution)/shard_map/ppermute | solution.py:23
  28.0 8.0 %collective-permute-start.1 = (f32[64,512]{1,0:T(8,128)S(1)}, f32[64,512]{1,0:T(8,128)S(1)}, u32[]{:S(2)}, u32[]{:S(2)}) collective-permute-start(f32[64,512]{1,0:T(8,128)S(1)} %added.2.refs_0_), channel_id=1, source_target_pairs={{0,8},{1,9},{2,10},{3,11},{4,12},{5,13},{6,14},{7,15},{8,0},{9,1},... | collective-permute-start | bytes 393224 | tf_op jit(solution)/shard_map/ppermute | solution.py:23
  36.0 5.9 %collective-permute-start.4 = (f32[64,512]{1,0:T(8,128)S(1)}, f32[64,512]{1,0:T(8,128)S(1)}, u32[]{:S(2)}, u32[]{:S(2)}) collective-permute-start(f32[64,512]{1,0:T(8,128)S(1)} %get-tuple-element.59), channel_id=1, source_target_pairs={{0,2},{1,3},{2,0},{3,1},{4,6},{5,7},{6,4},{7,5},{8,10},{9,11},{10,... | collective-permute-start | bytes 393224 | tf_op jit(solution)/shard_map/ppermute | solution.py:23
  36.8 7.7 %collective-permute-start.5 = (f32[64,512]{1,0:T(8,128)S(1)}, f32[64,512]{1,0:T(8,128)S(1)}, u32[]{:S(2)}, u32[]{:S(2)}) collective-permute-start(f32[64,512]{1,0:T(8,128)S(1)} %get-tuple-element.60), channel_id=1, source_target_pairs={{0,4},{1,5},{2,6},{3,7},{4,0},{5,1},{6,2},{7,3},{8,12},{9,13},{10,... | collective-permute-start | bytes 393224 | tf_op jit(solution)/shard_map/ppermute | solution.py:23
  39.1 7.2 %collective-permute-start.6 = (f32[64,512]{1,0:T(8,128)S(1)}, f32[64,512]{1,0:T(8,128)S(1)}, u32[]{:S(2)}, u32[]{:S(2)}) collective-permute-start(f32[64,512]{1,0:T(8,128)S(1)} %get-tuple-element.61), channel_id=1, source_target_pairs={{0,6},{1,7},{2,4},{3,5},{4,2},{5,3},{6,0},{7,1},{8,14},{9,15},{10,... | collective-permute-start | bytes 393224 | tf_op jit(solution)/shard_map/ppermute | solution.py:23
  52.4 17.1 %all-to-all-start.1 = ((f32[32,8,512]{2,1,0:T(8,128)}), f32[32,8,512]{2,1,0:T(8,128)S(1)}, u32[]{:S(2)}, u32[]{:S(2)}) async-start(f32[32,8,512]{2,1,0:T(8,128)} %bitcast), calls=%async_computation.1 | async-start | bytes 1048576 | tf_op jit(solution)/shard_map/all_to_all | solution.py:31
  59.6 14.1 %collective-permute-start.15 = (f32[4,8,1536]{2,1,0:T(8,128)S(1)}, f32[4,8,1536]{2,1,0:T(8,128)S(1)}, u32[]{:S(2)}, u32[]{:S(2)}) collective-permute-start(f32[4,8,1536]{2,1,0:T(8,128)S(1)} %fusion), channel_id=1, source_target_pairs={{0,8},{1,9},{2,10},{3,11},{4,12},{5,13},{6,14},{7,15},{8,16},{9,17... | collective-permute-start | bytes 589832 | tf_op jit(solution)/shard_map/ppermute | solution.py:23
  70.3 9.9 %all-to-all-start.2 = ((f32[8,8,512]{2,1,0:T(8,128)}), f32[8,8,512]{2,1,0:T(8,128)S(1)}, u32[]{:S(2)}, u32[]{:S(2)}) async-start(f32[8,8,512]{2,1,0:T(8,128)} %get-tuple-element.66), calls=%async_computation.2 | async-start | bytes 262144 | tf_op jit(solution)/shard_map/all_to_all | solution.py:31
  73.7 7.2 %collective-permute-start.14 = (f32[4,8,512]{2,1,0:T(8,128)S(1)}, f32[4,8,512]{2,1,0:T(8,128)S(1)}, u32[]{:S(2)}, u32[]{:S(2)}) collective-permute-start(f32[4,8,512]{2,1,0:T(8,128)S(1)} %get-tuple-element.110), channel_id=1, source_target_pairs={{0,16},{1,17},{2,18},{3,19},{4,20},{5,21},{6,22},{7,23},{8,24},{9,... | collective-permute-start | bytes 196616 | tf_op jit(solution)/shard_map/ppermute | solution.py:23
  82.1 9.6 %collective-permute-start.11 = (f32[64,512]{1,0:T(8,128)S(1)}, f32[64,512]{1,0:T(8,128)S(1)}, u32[]{:S(2)}, u32[]{:S(2)}) collective-permute-start(f32[64,512]{1,0:T(8,128)S(1)} %add.42), channel_id=1, source_target_pairs={{0,6},{1,7},{2,4},{3,5},{4,2},{5,3},{6,0},{7,1},{8,14},{9,15},{10,... | collective-permute-start | bytes 393224 | tf_op jit(solution)/shard_map/ppermute | solution.py:23
  83.4 8.3 %collective-permute-start.10 = (f32[64,512]{1,0:T(8,128)S(1)}, f32[64,512]{1,0:T(8,128)S(1)}, u32[]{:S(2)}, u32[]{:S(2)}) collective-permute-start(f32[64,512]{1,0:T(8,128)S(1)} %add.42), channel_id=1, source_target_pairs={{0,4},{1,5},{2,6},{3,7},{4,0},{5,1},{6,2},{7,3},{8,12},{9,13},{10,... | collective-permute-start | bytes 393224 | tf_op jit(solution)/shard_map/ppermute | solution.py:23
  84.8 7.6 %collective-permute-start.9 = (f32[64,512]{1,0:T(8,128)S(1)}, f32[64,512]{1,0:T(8,128)S(1)}, u32[]{:S(2)}, u32[]{:S(2)}) collective-permute-start(f32[64,512]{1,0:T(8,128)S(1)} %add.42), channel_id=1, source_target_pairs={{0,2},{1,3},{2,0},{3,1},{4,6},{5,7},{6,4},{7,5},{8,10},{9,11},{10,... | collective-permute-start | bytes 393224 | tf_op jit(solution)/shard_map/ppermute | solution.py:23
  145.8 5.3 %collective-permute-start.18 = (f32[8,768]{1,0:T(8,128)S(1)}, f32[8,768]{1,0:T(8,128)S(1)}, u32[]{:S(2)}, u32[]{:S(2)}) collective-permute-start(f32[8,768]{1,0:T(8,128)S(1)} %get-tuple-element.74), channel_id=1, source_target_pairs={{0,4},{1,5},{2,6},{3,7},{4,0},{5,1},{6,2},{7,3},{8,12},{9,13},{10,... | collective-permute-start | bytes 73736 | tf_op jit(solution)/shard_map/ppermute | solution.py:23
  147.6 5.0 %collective-permute-start.19 = (f32[8,768]{1,0:T(8,128)S(1)}, f32[8,768]{1,0:T(8,128)S(1)}, u32[]{:S(2)}, u32[]{:S(2)}) collective-permute-start(f32[8,768]{1,0:T(8,128)S(1)} %get-tuple-element.75), channel_id=1, source_target_pairs={{0,6},{1,7},{2,4},{3,5},{4,2},{5,3},{6,0},{7,1},{8,14},{9,15},{10,... | collective-permute-start | bytes 73736 | tf_op jit(solution)/shard_map/ppermute | solution.py:23
  167.7 5.7 %collective-permute-start.21 = (f32[16,1536]{1,0:T(8,128)S(1)}, f32[16,1536]{1,0:T(8,128)S(1)}, u32[]{:S(2)}, u32[]{:S(2)}) collective-permute-start(f32[16,1536]{1,0:T(8,128)S(1)} %get-tuple-element.81), channel_id=1, source_target_pairs={{0,2},{1,3},{2,0},{3,1},{4,6},{5,7},{6,4},{7,5},{8,10},{9,11},{10,... | collective-permute-start | bytes 294920 | tf_op jit(solution)/shard_map/ppermute | solution.py:23
  167.8 8.1 %collective-permute-start.22 = (f32[16,1536]{1,0:T(8,128)S(1)}, f32[16,1536]{1,0:T(8,128)S(1)}, u32[]{:S(2)}, u32[]{:S(2)}) collective-permute-start(f32[16,1536]{1,0:T(8,128)S(1)} %get-tuple-element.82), channel_id=1, source_target_pairs={{0,4},{1,5},{2,6},{3,7},{4,0},{5,1},{6,2},{7,3},{8,12},{9,13},{10,... | collective-permute-start | bytes 294920 | tf_op jit(solution)/shard_map/ppermute | solution.py:23
  170.8 6.9 %collective-permute-start.23 = (f32[16,1536]{1,0:T(8,128)S(1)}, f32[16,1536]{1,0:T(8,128)S(1)}, u32[]{:S(2)}, u32[]{:S(2)}) collective-permute-start(f32[16,1536]{1,0:T(8,128)S(1)} %get-tuple-element.83), channel_id=1, source_target_pairs={{0,6},{1,7},{2,4},{3,5},{4,2},{5,3},{6,0},{7,1},{8,14},{9,15},{10,... | collective-permute-start | bytes 294920 | tf_op jit(solution)/shard_map/ppermute | solution.py:23
  180.3 5.3 %collective-permute-start.26 = (f32[8,512]{1,0:T(8,128)S(1)}, f32[8,512]{1,0:T(8,128)S(1)}, u32[]{:S(2)}, u32[]{:S(2)}) collective-permute-start(f32[8,512]{1,0:T(8,128)S(1)} %get-tuple-element.88), channel_id=1, source_target_pairs={{0,4},{1,5},{2,6},{3,7},{4,0},{5,1},{6,2},{7,3},{8,12},{9,13},{10,... | collective-permute-start | bytes 49160 | tf_op jit(solution)/shard_map/ppermute | solution.py:23
  199.6 5.5 %collective-permute-start.29 = (f32[16,1280]{1,0:T(8,128)S(1)}, f32[16,1280]{1,0:T(8,128)S(1)}, u32[]{:S(2)}, u32[]{:S(2)}) collective-permute-start(f32[16,1280]{1,0:T(8,128)S(1)} %get-tuple-element.96), channel_id=1, source_target_pairs={{0,2},{1,3},{2,0},{3,1},{4,6},{5,7},{6,4},{7,5},{8,10},{9,11},{10,... | collective-permute-start | bytes 245768 | tf_op jit(solution)/shard_map/ppermute | solution.py:23
  199.7 7.4 %collective-permute-start.30 = (f32[16,1280]{1,0:T(8,128)S(1)}, f32[16,1280]{1,0:T(8,128)S(1)}, u32[]{:S(2)}, u32[]{:S(2)}) collective-permute-start(f32[16,1280]{1,0:T(8,128)S(1)} %get-tuple-element.97), channel_id=1, source_target_pairs={{0,4},{1,5},{2,6},{3,7},{4,0},{5,1},{6,2},{7,3},{8,12},{9,13},{10,... | collective-permute-start | bytes 245768 | tf_op jit(solution)/shard_map/ppermute | solution.py:23
  202.8 6.0 %collective-permute-start.31 = (f32[16,1280]{1,0:T(8,128)S(1)}, f32[16,1280]{1,0:T(8,128)S(1)}, u32[]{:S(2)}, u32[]{:S(2)}) collective-permute-start(f32[16,1280]{1,0:T(8,128)S(1)} %get-tuple-element.98), channel_id=1, source_target_pairs={{0,6},{1,7},{2,4},{3,5},{4,2},{5,3},{6,0},{7,1},{8,14},{9,15},{10,... | collective-permute-start | bytes 245768 | tf_op jit(solution)/shard_map/ppermute | solution.py:23
  212.1 5.5 %collective-permute-start.34 = (f32[8,1024]{1,0:T(8,128)S(1)}, f32[8,1024]{1,0:T(8,128)S(1)}, u32[]{:S(2)}, u32[]{:S(2)}) collective-permute-start(f32[8,1024]{1,0:T(8,128)S(1)} %get-tuple-element.107), channel_id=1, source_target_pairs={{0,4},{1,5},{2,6},{3,7},{4,0},{5,1},{6,2},{7,3},{8,12},{9,13},{10,... | collective-permute-start | bytes 98312 | tf_op jit(solution)/shard_map/ppermute | solution.py:23
  215.1 5.1 %collective-permute-start.35 = (f32[8,1024]{1,0:T(8,128)S(1)}, f32[8,1024]{1,0:T(8,128)S(1)}, u32[]{:S(2)}, u32[]{:S(2)}) collective-permute-start(f32[8,1024]{1,0:T(8,128)S(1)} %get-tuple-element.108), channel_id=1, source_target_pairs={{0,6},{1,7},{2,4},{3,5},{4,2},{5,3},{6,0},{7,1},{8,14},{9,15},{10,... | collective-permute-start | bytes 98312 | tf_op jit(solution)/shard_map/ppermute | solution.py:23
  (27 other events, 469.6 us)
